TPU v7x, 32 devices: a whole 2x2x4 slice. The times are simulated.
32 devices in a mesh: bus: 8 (over z, x), case: 4 (over y, core).
Axes of the slice: x: 2, y: 2, z: 4, core: 2. Of those that a mesh axis runs over, the one named last changes fastest.
Arguments:
- z_columns: float32 [8192, 1024], P('bus')
- resident_bus: int32 [1024], replicated, may hold values from 0 to 8191, as said below
- fault_col: int32 [2048], P('case'), may hold values from 0 to 1023
- switch_cols: int32 [2048, 2], P('case'), may hold values from 0 to 1023, as said below
- tie_x: float32 [2048], P('case'), may hold values from 0.5 to 2
- fault_z: float32 [2048], P('case'), may hold values from 0.5 to 2
- boundary_send: int32 [8, 2, 128], replicated, may hold values from 0 to 1023, as said below
- branch_ends: int32 [12288, 2], P('bus'), may hold values from 0 to 1279, as said below
- branch_x: float32 [12288], P('bus'), may hold values from 0.01 to 0.05
- pickup: float32 [12288], P('bus'), may hold values from 0.2 to 1.5
- tds: float32 [12288], P('bus'), may hold values from 0.05 to 0.5
- curve: int32 [12288], P('bus'), may hold values from 0 to 2
Outputs:
- voltage: float32 [8192, 2048], P('bus', 'case')
- relay_rate: float32 [12288, 2048], P('bus', 'case')
- worst_rate: float32 [12288], P('bus')
Inputs may be any that keep to these rules, and one draw needn't show every extreme that they name: `resident_bus`: distinct bus ids. `switch_cols`: the two columns of a case differ. `boundary_send`: rows sent to the lower block lie among the first 256 rows, rows sent to the upper block among the last 256; each block's live slots come first and hold distinct rows, padding repeats the first slot's row; the first block sends nothing down and the last nothing up; some block fills all 128 slots. `branch_ends`: a to slot of 1024 or more points at a live slot of the neighbour's block; the first block never uses the lower slots, the last never the upper ones; a local to row differs from the from row.
All inputs are finite; a program needn't handle non-finite values.
Results may differ from a plain program's by a relative error of at most 0.000049.
Values sent between devices are 32-bit elements; how exact they have to be, the bound alone decides.
No kernel may reach another device: no remote copies, remote signals or barrier semaphores. Data moves between devices by JAX's collectives and lax.ppermute only.
A program may use at most 64 MiB of HBM per device.

v0:
```python
import jax
import jax.numpy as jnp
from jax import lax
from jax.sharding import PartitionSpec as P


def shifted(value, axis, by):
    size = lax.axis_size(axis)
    pairs = [(i, i + by) for i in range(size) if 0 <= i + by < size]
    return lax.ppermute(value, axis, pairs)


def relay_of(currents, pickup, tds, curve):
    factor = jnp.where(curve == 0, 0.14, jnp.where(curve == 1, 13.5, 80.0)).astype(jnp.float32)
    exponent = jnp.where(curve == 0, 0.02, jnp.where(curve == 1, 1.0, 2.0)).astype(jnp.float32)
    scaled = currents / pickup[:, None]
    powered = jnp.exp(0.5 * exponent[:, None] * jnp.log(scaled * scaled + 0.0001))
    return jnp.maximum(powered - 1.0, 0.0) / (factor * tds)[:, None]


def per_device(
    z_columns,
    resident_bus,
    fault_col,
    switch_cols,
    tie_x,
    fault_z,
    boundary_send,
    branch_ends,
    branch_x,
    pickup,
    tds,
    curve,
):
    rows_dev = z_columns.shape[0]
    my_index = lax.axis_index("bus")
    fault_cols = jnp.take(z_columns, fault_col, axis=1)
    branch_diff = jnp.take(z_columns, switch_cols[:, 0], axis=1) - jnp.take(
        z_columns, switch_cols[:, 1], axis=1
    )
    offset = my_index * rows_dev
    row_a = jnp.take(resident_bus, switch_cols[:, 0]) - offset
    row_b = jnp.take(resident_bus, switch_cols[:, 1]) - offset
    row_f = jnp.take(resident_bus, fault_col) - offset
    row_ids = lax.broadcasted_iota(jnp.int32, (rows_dev, 1), 0)

    def pick_rows(column, wanted):
        return jnp.sum(jnp.where(row_ids == wanted[None, :], column, 0.0), axis=0)

    partial_value = jnp.stack(
        [
            pick_rows(branch_diff, row_a) - pick_rows(branch_diff, row_b),
            pick_rows(branch_diff, row_f),
            pick_rows(fault_cols, row_f),
        ]
    )
    own_lists = lax.dynamic_index_in_dim(boundary_send, my_index, 0, keepdims=False)
    entry_sums = lax.psum(partial_value, "bus")
    weight_ratio = entry_sums[1] / (tie_x + entry_sums[0])
    self_z = entry_sums[2] - entry_sums[1] * weight_ratio
    fault_amps = 1.0 / (self_z + fault_z)
    voltage = 1.0 - (fault_cols - branch_diff * weight_ratio[None, :]) * fault_amps[None, :]
    fields = voltage[None]
    going_down = jnp.take(fields, own_lists[0], axis=1)
    going_up = jnp.take(fields, own_lists[1], axis=1)
    from_lower = shifted(going_up, "bus", 1)
    from_upper = shifted(going_down, "bus", -1)
    extended = jnp.concatenate([fields, from_lower, from_upper], axis=1)[0]
    drops = jnp.take(extended, branch_ends[:, 0], axis=0) - jnp.take(
        extended, branch_ends[:, 1], axis=0
    )
    currents = drops / branch_x[:, None]
    relay_rate = relay_of(currents, pickup, tds, curve)
    worst_rate = lax.pmax(jnp.max(relay_rate, axis=1), "case")
    return (voltage, relay_rate, worst_rate)


def solution(mesh):
    in_specs = (
        P("bus", None),
        P(),
        P("case"),
        P("case", None),
        P("case"),
        P("case"),
        P(),
        P("bus", None),
        P("bus"),
        P("bus"),
        P("bus"),
        P("bus"),
    )
    out_specs = (P("bus", "case"), P("bus", "case"), P("bus"))
    return jax.shard_map(
        per_device, mesh=mesh, in_specs=in_specs, out_specs=out_specs, check_vma=False
    )
```

profile of v0, /device:TPU:0, one launch (start us, length us, event | category | flops | bytes accessed | tf_op | source)
XLA Modules:
  0.0 103.6 jit_solution(11522298754595998767)
XLA Ops:
  0.6 0.0 copy-start
  0.6 0.0 copy-start.1
  0.7 0.8 fusion.11
  1.5 3.4 %gather_fusion.4 = s32[512]{0:T(512)S(1)} fusion(s32[1024]{0:T(1024)} %param.21, s32[1024]{0:T(1024)S(1)} %pad_clamp_fusion.4), kind=kCustom, calls=%fused_computation.6.clone | custom fusion | bytes 6144 | tf_op jit(solution)/shard_map/jit(_take)/gather | solution.py:43
  4.8 0.0 copy-done.1
  4.8 2.3 %gather_fusion.3 = s32[512]{0:T(512)S(1)} fusion(s32[1024]{0:T(1024)S(1)} %copy-done.1, s32[1024]{0:T(1024)S(1)} %pad_clamp_fusion.5), kind=kCustom, calls=%fused_computation.1.clone | custom fusion | bytes 6144 | tf_op jit(solution)/shard_map/jit(_take)/gather | solution.py:42
  7.1 5.4 %copy.25 = f32[1024,1024]{0,1:T(8,128)} copy(f32[1024,1024]{1,0:T(8,128)} %param.20) | data formatting | bytes 8388608 | tf_op args[0]
  12.5 5.8 %gather_fusion.1 = f32[512,1024]{1,0:T(8,128)} fusion(f32[1024,1024]{0,1:T(8,128)} %copy.25, s32[1024]{0:T(1024)S(1)} %pad_clamp_fusion.5), kind=kCustom, calls=%fused_computation.4.clone | custom fusion | bytes 4196352 | tf_op jit(solution)/shard_map/jit(_take)/gather | solution.py:38
  18.3 0.0 copy-start.6
  18.3 5.8 %gather_fusion.2 = f32[512,1024]{1,0:T(8,128)} fusion(f32[1024,1024]{0,1:T(8,128)} %copy.25, s32[1024]{0:T(1024)S(1)} %pad_clamp_fusion.4), kind=kCustom, calls=%fused_computation.5.clone | custom fusion | bytes 4196352 | tf_op jit(solution)/shard_map/jit(_take)/gather | solution.py:38
  24.1 0.0 copy-done.6
  24.1 2.3 %gather_fusion.5 = s32[512]{0:T(512)S(1)} fusion(s32[1024]{0:T(1024)S(1)} %copy-done.1, s32[1024]{0:T(1024)S(1)} %pad_clamp_fusion.6), kind=kCustom, calls=%fused_computation.7.clone | custom fusion | bytes 6144 | tf_op jit(solution)/shard_map/jit(_take)/gather | solution.py:44
  26.4 5.0 %gather_fusion = f32[512,1024]{1,0:T(8,128)S(1)} fusion(f32[1024,1024]{0,1:T(8,128)} %copy.25, s32[1024]{0:T(1024)S(1)} %pad_clamp_fusion.6), kind=kCustom, calls=%fused_computation.clone | custom fusion | bytes 4196352 | tf_op jit(solution)/shard_map/jit(_take)/gather | solution.py:37
  31.5 0.0 copy-start.9
  31.5 0.0 copy-start.10
  31.5 4.3 %select_reduce_fusion.1 = (f32[512]{0:T(512)S(1)}, f32[512]{0:T(512)S(1)}, f32[512]{0:T(512)S(1)}, f32[512]{0:T(512)S(1)}, f32[1024,512]{0,1:T(8,128)}) fusion(s32[512]{0:T(512)S(1)} %get-tuple-element.44, s32[512]{0:T(512)S(1)} %get-tuple-element.33, s32[512]{0:T(512)S(1)} %get-tuple-element.31, f32[512,1024]{1,0:T(8,128)S(1)} %gather_fusion, ...), kind=kLoop, calls=%fused_computation.27 | loop fusion | flops 7862272 | bytes 8404480 | tf_op jit(solution)/shard_map/reduce_sum | solution.py:48
  35.8 23.4 %psum.7 = f32[3,512]{1,0:T(4,128)S(1)} all-reduce(f32[3,512]{1,0:T(4,128)S(1)} %pad_maximum_fusion), channel_id=1, replica_groups=mesh['bus'=8,'case'=4] {'bus'}, use_global_device_ids=true, to_apply=%region_4.7 | all-reduce | flops 1536 | bytes 12288 | tf_op jit(solution)/shard_map/psum | solution.py:58
  59.2 0.0 copy-done.9
  59.2 0.0 copy-done.10
  59.2 3.4 %fusion.8 = f32[1024,512]{0,1:T(8,128)} fusion(f32[1024,512]{0,1:T(8,128)} %get-tuple-element.30, f32[512,1024]{1,0:T(8,128)S(1)} %gather_fusion, f32[512]{0:T(512)S(1)} %get-tuple-element.28, f32[512]{0:T(512)S(1)} %get-tuple-element.29, pred[512]{0:T(512)(128)(4,1)S(1)} %get-tuple-element.34), kind=kLoop, calls=%fused_computation.24 | loop fusion | flops 2621440 | bytes 6296064 | tf_op jit(solution)/shard_map/sub | solution.py:62
  62.6 1.9 %copy.34 = f32[1024,512]{1,0:T(8,128)S(1)} copy(f32[1024,512]{0,1:T(8,128)} %fusion.8) | data formatting | bytes 4194304
  64.5 0.0 copy-start.2
  64.6 0.0 copy-done
  64.6 0.8 gather_fusion.6
  65.4 0.1 copy.29
  65.5 0.0 copy-start.3
  65.5 0.0 copy-start.7
  65.5 0.0 copy-start.4
  65.5 0.0 copy-start.5
  65.5 0.0 copy-start.8
  65.6 1.3 %collective-permute-start = (f32[1,128,512]{1,2,0:T(8,128)S(1)}, f32[1,128,512]{1,2,0:T(8,128)S(1)}, u32[]{:S(2)}, u32[]{:S(2)}) collective-permute-start(f32[1,128,512]{1,2,0:T(8,128)S(1)} %bitcast_select_fusion.2), channel_id=1, source_target_pairs={{0,4},{4,8},{8,12},{12,16},{16,20},{20,24},{24,28},{1,5},{5,9},{9,... | collective-permute-start | bytes 786440 | tf_op jit(solution)/shard_map/ppermute | solution.py:10
  66.9 0.8 gather_fusion.7
  67.7 0.0 copy-done.2
  67.7 0.1 copy.31
  67.8 1.3 %collective-permute-start.1 = (f32[1,128,512]{1,2,0:T(8,128)S(1)}, f32[1,128,512]{1,2,0:T(8,128)S(1)}, u32[]{:S(2)}, u32[]{:S(2)}) collective-permute-start(f32[1,128,512]{1,2,0:T(8,128)S(1)} %bitcast_select_fusion.1), channel_id=1, source_target_pairs={{4,0},{8,4},{12,8},{16,12},{20,16},{24,20},{28,24},{5,1},{9,5},{13... | collective-permute-start | bytes 786440 | tf_op jit(solution)/shard_map/ppermute | solution.py:10
  69.1 0.0 copy-done.3
  69.2 0.0 copy-done.7
  69.3 0.0 copy-done.4
  69.3 0.0 copy-done.5
  69.3 0.0 copy-done.8
  69.3 6.5 %collective-permute-done = f32[1,128,512]{1,2,0:T(8,128)S(1)} collective-permute-done((f32[1,128,512]{1,2,0:T(8,128)S(1)}, f32[1,128,512]{1,2,0:T(8,128)S(1)}, u32[]{:S(2)}, u32[]{:S(2)}) %collective-permute-start) | collective-permute-done | bytes 262176 | tf_op jit(solution)/shard_map/ppermute | solution.py:10
  75.8 0.3 collective-permute-done.1
  76.1 3.3 %maximum_bitcast_fusion = f32[1280,512]{0,1:T(8,128)} fusion(f32[1,128,512]{1,2,0:T(8,128)S(1)} %collective-permute-done.1, f32[1,128,512]{1,2,0:T(8,128)S(1)} %collective-permute-done, f32[1,1024,512]{1,2,0:T(8,128)} %bitcast.36), kind=kLoop, calls=%fused_computation.18 | loop fusion | flops 1310720 | bytes 5242880 | tf_op jit(solution)/shard_map/squeeze | solution.py:68
  79.4 2.1 %copy.32 = f32[1280,512]{1,0:T(8,128)S(1)} copy(f32[1280,512]{0,1:T(8,128)} %maximum_bitcast_fusion) | data formatting | bytes 5242880 | tf_op jit(solution)/shard_map/squeeze | solution.py:68
  81.6 5.0 %gather_fusion.8 = f32[1536,512]{1,0:T(8,128)} fusion(f32[1280,512]{1,0:T(8,128)S(1)} %copy.32, s32[2048]{0:T(1024)S(1)} %pad_clamp_fusion.1), kind=kCustom, calls=%fused_computation.3.clone | custom fusion | bytes 6297600 | tf_op jit(solution)/shard_map/jit(_take)/gather | solution.py:69
  86.5 4.9 %gather_fusion.9 = f32[1536,512]{1,0:T(8,128)} fusion(f32[1280,512]{1,0:T(8,128)S(1)} %copy.32, s32[2048]{0:T(1024)S(1)} %pad_clamp_fusion), kind=kCustom, calls=%fused_computation.9.clone | custom fusion | bytes 6297600 | tf_op jit(solution)/shard_map/jit(_take)/gather | solution.py:69
  91.4 5.9 %fusion.9 = (f32[1536]{0:T(1024)S(1)}, f32[1536,512]{1,0:T(8,128)}) fusion(f32[1536]{0:T(1024)S(1)} %select_multiply_fusion, f32[1536]{0:T(1024)S(1)} %multiply.4, f32[1536,512]{1,0:T(8,128)} %gather_fusion.9, pred[1536]{0:T(1024)(128)(4,1)S(1)} %get-tuple-element.48, f32[1536,512]{1,0:T(8,128)} %gather_fusion.8, pred[1536]{0:T(1024)(128)(4,1)S(1)} %get-tuple-element.49, ...), kind=kLoop, calls=%fused_computation.67 | loop fusion | flops 8649216 | bytes 9464832 | tf_op jit(solution)/shard_map/reduce_max | solution.py:74
  97.3 6.3 %pmax.7 = f32[1536]{0:T(1024)} all-reduce(f32[1536]{0:T(1024)S(1)} %get-tuple-element.19), channel_id=1, replica_groups=mesh['bus'=8,'case'=4] {'case'}, use_global_device_ids=true, to_apply=%region_6.11 | all-reduce | flops 1536 | bytes 12288 | tf_op jit(solution)/shard_map/pmax | solution.py:74
  (26 shorter events, 0.3 us)
Async XLA Ops:
  0.6 63.9 %copy-start = (s32[8,2,128]{2,1,0:T(2,128)S(1)}, s32[8,2,128]{2,1,0:T(2,128)}, u32[]{:S(2)}) copy-start(s32[8,2,128]{2,1,0:T(2,128)} %param.26) | copy-start | bytes 24580
  0.6 4.2 %copy-start.1 = (s32[1024]{0:T(1024)S(1)}, s32[1024]{0:T(1024)}, u32[]{:S(2)}) copy-start(s32[1024]{0:T(1024)} %param.21) | copy-start | bytes 12292
  18.3 5.8 %copy-start.6 = (s32[512]{0:T(512)S(1)}, s32[512]{0:T(512)}, u32[]{:S(2)}) copy-start(s32[512]{0:T(512)} %param.22) | copy-start | bytes 6148
  31.5 27.7 %copy-start.9 = (f32[512]{0:T(512)S(1)}, f32[512]{0:T(512)}, u32[]{:S(2)}) copy-start(f32[512]{0:T(512)} %param.25) | copy-start | bytes 6148
  31.5 27.7 %copy-start.10 = (f32[512]{0:T(512)S(1)}, f32[512]{0:T(512)}, u32[]{:S(2)}) copy-start(f32[512]{0:T(512)} %param.24) | copy-start | bytes 6148
  64.5 3.1 %copy-start.2 = (f32[1024,512]{1,0:T(8,128)}, f32[1024,512]{1,0:T(8,128)S(1)}, u32[]{:S(2)}) copy-start(f32[1024,512]{1,0:T(8,128)S(1)} %copy.34) | copy-start | bytes 6291460
  65.5 3.6 %copy-start.3 = (s32[1536,2]{0,1:T(2,128)S(1)}, s32[1536,2]{0,1:T(2,128)}, u32[]{:S(2)}) copy-start(s32[1536,2]{0,1:T(2,128)} %param.27) | copy-start | bytes 36868
  65.5 3.7 %copy-start.7 = (s32[1536]{0:T(1024)S(1)}, s32[1536]{0:T(1024)}, u32[]{:S(2)}) copy-start(s32[1536]{0:T(1024)} %param.31) | copy-start | bytes 18436
  65.5 3.8 %copy-start.4 = (f32[1536]{0:T(1024)S(1)}, f32[1536]{0:T(1024)}, u32[]{:S(2)}) copy-start(f32[1536]{0:T(1024)} %param.28) | copy-start | bytes 18436
  65.5 3.8 %copy-start.5 = (f32[1536]{0:T(1024)S(1)}, f32[1536]{0:T(1024)}, u32[]{:S(2)}) copy-start(f32[1536]{0:T(1024)} %param.29) | copy-start | bytes 18436
  65.5 3.8 %copy-start.8 = (f32[1536]{0:T(1024)S(1)}, f32[1536]{0:T(1024)}, u32[]{:S(2)}) copy-start(f32[1536]{0:T(1024)} %param.30) | copy-start | bytes 18436
  65.6 10.2 %collective-permute-start = (f32[1,128,512]{1,2,0:T(8,128)S(1)}, f32[1,128,512]{1,2,0:T(8,128)S(1)}, u32[]{:S(2)}, u32[]{:S(2)}) collective-permute-start(f32[1,128,512]{1,2,0:T(8,128)S(1)} %bitcast_select_fusion.2), channel_id=1, source_target_pairs={{0,4},{4,8},{8,12},{12,16},{16,20},{20,24},{24,28},{1,5},{5,9},{9,... | collective-permute-start | bytes 786440 | tf_op jit(solution)/shard_map/ppermute | solution.py:10
  67.8 8.3 %collective-permute-start.1 = (f32[1,128,512]{1,2,0:T(8,128)S(1)}, f32[1,128,512]{1,2,0:T(8,128)S(1)}, u32[]{:S(2)}, u32[]{:S(2)}) collective-permute-start(f32[1,128,512]{1,2,0:T(8,128)S(1)} %bitcast_select_fusion.1), channel_id=1, source_target_pairs={{4,0},{8,4},{12,8},{16,12},{20,16},{24,20},{28,24},{5,1},{9,5},{13... | collective-permute-start | bytes 786440 | tf_op jit(solution)/shard_map/ppermute | solution.py:10
where the time goes:
time: 104 us
  local copies, waits for them, and re-layouts  46.5 us (45%)
  blocking collectives  29.7 us (29%)
  other arithmetic  17.1 us (16%)
  waiting for transfers between devices  6.77 us (7%)
  starting transfers between devices  2.6 us (2%)
  between operations  1.04 us (1%)
    psum x1, blocking collectives, per_device(): entry_sums = lax.psum(partial_value, 'bus')  23.4 us
    unnamed x24, local copies, waits for them, and re-layouts  7.35 us
    ppermute x2, waiting for transfers between devices, shifted(): return lax.ppermute(value, axis, pairs)  6.77 us
    pmax x1, blocking collectives, per_device(): worst_rate = lax.pmax(jnp.max(relay_rate, axis=1), 'case')  6.31 us
    reduce_max x1, other arithmetic, per_device(): worst_rate = lax.pmax(jnp.max(relay_rate, axis=1), 'case')  5.89 us
    gather x1, local copies, waits for them, and re-layouts, per_device(): jnp.take(z_columns, switch_cols[:, 1], axis=1)  5.8 us
    gather x1, local copies, waits for them, and re-layouts, per_device(): jnp.take(z_columns, switch_cols[:, 0], axis=1)  5.78 us
    gather x1, local copies, waits for them, and re-layouts, per_device(): fault_cols = jnp.take(z_columns, fault_col, axis=1)  5.01 us
  transfers between devices with their start and end apart: 2, of which 2 were waited for; matrix products, arithmetic and copies ran while one was open for 1% of the time, Pallas kernels for 0%

commit v1 on v0

v1 whole, which is shorter than its diff:
```python
import jax
import jax.numpy as jnp
from jax import lax
from jax.experimental import pallas as pl
from jax.experimental.pallas import tpu as pltpu
from jax.sharding import PartitionSpec as P

RIM = 256
TILE = 256
F32 = jnp.float32
BF16 = jnp.bfloat16


def split_hi_lo(value):
    hi = value.astype(BF16)
    return hi, (value - hi.astype(F32)).astype(BF16)


def two_pass(hi, lo, rhs):
    return jnp.dot(hi, rhs, preferred_element_type=F32) + jnp.dot(
        lo, rhs, preferred_element_type=F32
    )


def send_kernel(meta_ref, z_ref, out_ref):
    for i in range(out_ref.shape[0]):
        out_ref[pl.ds(i, 1), :] = z_ref[pl.ds(meta_ref[1 + i], 1), :]


def gather_send_rows(z_columns, meta, piece):
    cols = z_columns.shape[1]
    return pl.pallas_call(
        send_kernel,
        grid_spec=pltpu.PrefetchScalarGridSpec(
            num_scalar_prefetch=1,
            grid=(1,),
            in_specs=[pl.BlockSpec((RIM, cols), lambda i, meta: (meta[0], 0))],
            out_specs=pl.BlockSpec((piece, cols), lambda i, meta: (0, 0)),
        ),
        out_shape=jax.ShapeDtypeStruct((piece, cols), F32),
        name="gather_send_rows",
    )(meta, z_columns)


def columns_kernel(z_hbm, cases_ref, resident_ref, fd_ref, pick_ref, g_ref, zbuf, sems):
    rows, cols = zbuf.shape
    cases = cases_ref.shape[1]
    tiles = rows // TILE
    copies = [
        pltpu.make_async_copy(
            z_hbm.at[pl.ds(t * TILE, TILE)], zbuf.at[pl.ds(t * TILE, TILE)], sems.at[t]
        )
        for t in range(tiles)
    ]
    for copy in copies:
        copy.start()
    f, a, b = cases_ref[0:1, :], cases_ref[1:2, :], cases_ref[2:3, :]
    for t in range(cols // TILE):
        k = lax.broadcasted_iota(jnp.int32, (TILE, cases), 0) + t * TILE
        span = pl.ds(t * TILE, TILE)
        pick_ref[span, :cases] = jnp.where(k == f, 1.0, 0.0).astype(BF16)
        pick_ref[span, cases:] = jnp.where(
            k == a, 1.0, jnp.where(k == b, -1.0, 0.0)
        ).astype(BF16)
    g1 = jnp.zeros((1, cases), F32)
    g2 = jnp.zeros((1, cases), F32)
    g3 = jnp.zeros((1, cases), F32)
    for t in range(tiles):
        span = pl.ds(t * TILE, TILE)
        row = lax.broadcasted_iota(jnp.int32, (TILE, cols), 0) + t * TILE
        k = lax.broadcasted_iota(jnp.int32, (TILE, cols), 1)
        owner = jnp.max(jnp.where(row == resident_ref[...], k, -1), axis=1, keepdims=True)
        copies[t].wait()
        hi, lo = split_hi_lo(zbuf[span, :])
        fd = two_pass(hi, lo, pick_ref[...])
        fd_ref[span, :] = fd
        fault, diff = fd[:, :cases], fd[:, cases:]
        at_f = owner == f
        g3 += jnp.sum(jnp.where(at_f, fault, 0.0), axis=0, keepdims=True)
        g2 += jnp.sum(jnp.where(at_f, diff, 0.0), axis=0, keepdims=True)
        g1 += jnp.sum(
            jnp.where(owner == a, diff, jnp.where(owner == b, -diff, 0.0)), axis=0, keepdims=True
        )
    g_ref[...] = jnp.broadcast_to(jnp.concatenate([g1, g2, g3])[None], g_ref.shape)


def pick_columns(z_columns, cases, resident, copies):
    rows, cols = z_columns.shape
    count = cases.shape[1]
    vmem = pl.BlockSpec(memory_space=pltpu.VMEM)
    return pl.pallas_call(
        columns_kernel,
        in_specs=[pl.BlockSpec(memory_space=pl.ANY), vmem, vmem],
        out_specs=[vmem, vmem, vmem],
        out_shape=[
            pltpu.VMEM((rows, 2 * count), F32),
            pltpu.VMEM((cols, 2 * count), BF16),
            jax.ShapeDtypeStruct((copies, 3, count), F32),
        ],
        scratch_shapes=[
            pltpu.VMEM((rows, cols), F32),
            pltpu.SemaphoreType.DMA((rows // TILE,)),
        ],
        compiler_params=pltpu.CompilerParams(vmem_limit_bytes=24 * 2**20),
        name="pick_columns",
    )(z_columns, cases, resident)


def branch_kernel(
    offsets,
    where_ref,
    g_ref,
    case_ref,
    fd_ref,
    pick_ref,
    par_ref,
    *refs,
):
    pieces = refs[: len(offsets)]
    volt_hbm, relay_hbm, worst_ref, vbuf, rbuf, zb, uh, ul, vsem, rsem = refs[len(offsets) :]
    rows, cases = vbuf.shape
    branches = rbuf.shape[0]
    ext = uh.shape[0]
    g = jnp.sum(g_ref[...], axis=0)
    g1, g2, g3 = g[0:1], g[1:2], g[2:3]
    ratio = g2 / (case_ref[0:1, :] + g1)
    amps = 1.0 / (g3 - g2 * ratio + case_ref[1:2, :])
    copies = []
    for t in range(rows // TILE):
        span = pl.ds(t * TILE, TILE)
        sag = (fd_ref[span, :cases] - fd_ref[span, cases:] * ratio) * amps
        vbuf[span, :] = 1.0 - sag
        copies.append(pltpu.make_async_copy(vbuf.at[span], volt_hbm.at[span], vsem.at[t]))
        copies[-1].start()
        uh[span, :], ul[span, :] = split_hi_lo(sag)
    for i, piece in enumerate(pieces):
        size = piece.shape[0]
        zb[pl.ds(pl.multiple_of(where_ref[i], size), size), :] = piece[...]
    hi, lo = split_hi_lo(zb[...])
    fd = two_pass(hi, lo, pick_ref[...])
    sag = (fd[:, :cases] - fd[:, cases:] * ratio) * amps
    span = pl.ds(rows, ext - rows)
    uh[span, :], ul[span, :] = split_hi_lo(sag)
    for t in range(branches // TILE):
        span = pl.ds(t * TILE, TILE)
        par = par_ref[span, :]
        bus = lax.broadcasted_iota(jnp.int32, (TILE, ext), 1).astype(F32)
        ends = jnp.where(
            bus == par[:, 1:2], 1.0, jnp.where(bus == par[:, 0:1], -1.0, 0.0)
        ).astype(BF16)
        drop = jnp.dot(ends, uh[...], preferred_element_type=F32) + jnp.dot(
            ends, ul[...], preferred_element_type=F32
        )
        scaled = drop * par[:, 2:3]
        square = scaled * scaled
        powered = jnp.exp2(par[:, 3:4] * jnp.log2(square + 1e-4))
        rbuf[span, :] = jnp.maximum(powered - 1.0, 0.0) * par[:, 4:5]
        copies.append(pltpu.make_async_copy(rbuf.at[span], relay_hbm.at[span], rsem.at[t]))
        copies[-1].start()
        largest = square[:, :128]
        for c in range(128, cases, 128):
            largest = jnp.maximum(largest, square[:, c : c + 128])
        for h in range(TILE // 128):
            worst_ref[pl.ds(t * (TILE // 128) + h, 1), :] = jnp.max(
                largest[h * 128 : (h + 1) * 128, :].T, axis=0, keepdims=True
            )
    for copy in copies:
        copy.wait()


def screen_branches(where, g_all, case_par, fd, pick, par, pieces, rows):
    count = case_par.shape[1]
    branches = par.shape[0]
    ext = rows + sum(piece.shape[0] for piece in pieces)
    vmem = pl.BlockSpec(memory_space=pltpu.VMEM)
    hbm = pl.BlockSpec(memory_space=pl.ANY)

    def kernel(*refs):
        branch_kernel(pieces, *refs)

    return pl.pallas_call(
        kernel,
        in_specs=[pl.BlockSpec(memory_space=pltpu.SMEM)] + [vmem] * (5 + len(pieces)),
        out_specs=[hbm, hbm, vmem],
        out_shape=[
            jax.ShapeDtypeStruct((rows, count), F32),
            jax.ShapeDtypeStruct((branches, count), F32),
            jax.ShapeDtypeStruct((branches // 128, 128), F32),
        ],
        scratch_shapes=[
            pltpu.VMEM((rows, count), F32),
            pltpu.VMEM((branches, count), F32),
            pltpu.VMEM((ext - rows, fd.shape[1]), F32),
            pltpu.VMEM((ext, count), BF16),
            pltpu.VMEM((ext, count), BF16),
            pltpu.SemaphoreType.DMA((rows // TILE,)),
            pltpu.SemaphoreType.DMA((branches // TILE,)),
        ],
        compiler_params=pltpu.CompilerParams(vmem_limit_bytes=40 * 2**20),
        name="screen_branches",
    )(where, g_all, case_par, fd, pick, par, *pieces)


def per_device(
    z_columns,
    resident_bus,
    fault_col,
    switch_cols,
    tie_x,
    fault_z,
    boundary_send,
    branch_ends,
    branch_x,
    pickup,
    tds,
    curve,
):
    rows = z_columns.shape[0]
    n_bus, n_case = lax.axis_size("bus"), lax.axis_size("case")
    my_bus, my_case = lax.axis_index("bus"), lax.axis_index("case")
    slots = boundary_send.shape[2]

    half = n_case // 2
    piece = slots // half
    down = my_case // half
    wanted = lax.dynamic_slice(
        boundary_send, (my_bus, 1 - down, (my_case % half) * piece), (1, 1, piece)
    )[0, 0]
    rim = (1 - down) * (rows // RIM - 1)
    meta = jnp.concatenate([rim[None], wanted - rim * RIM]).astype(jnp.int32)
    send = gather_send_rows(z_columns, meta, piece)
    pairs = []
    for s in range(n_bus):
        for c in range(n_case):
            to = s + 1 if c < half else s - 1
            if 0 <= to < n_bus:
                pairs.append((s * n_case + c, to * n_case + c))
    pieces = [lax.ppermute(send, ("bus", "case"), pairs)]
    masks = [0]

    cases = jnp.concatenate([fault_col[None], switch_cols.T], axis=0)
    resident = (resident_bus - my_bus * rows)[None]
    fd, pick, g_part = pick_columns(z_columns, cases, resident, n_bus)

    bit = n_case // 2
    while bit:
        swap = [(i, i ^ bit) for i in range(n_case)]
        pieces = pieces + [lax.ppermute(x, "case", swap) for x in pieces]
        masks = masks + [m ^ bit for m in masks]
        bit //= 2
    g_all = lax.all_to_all(g_part, "bus", 0, 0)

    where = jnp.stack([(my_case ^ m) * piece for m in masks]).astype(jnp.int32)
    gain = 1.0 / (branch_x * pickup)
    factor = jnp.where(curve == 0, 0.14, jnp.where(curve == 1, 13.5, 80.0)).astype(F32)
    power = jnp.where(curve == 0, 0.01, jnp.where(curve == 1, 0.5, 1.0)).astype(F32)
    rate = 1.0 / (factor * tds)
    zero = jnp.zeros_like(gain)
    par = jnp.stack(
        [
            branch_ends[:, 0].astype(F32),
            branch_ends[:, 1].astype(F32),
            gain,
            power,
            rate,
            zero,
            zero,
            zero,
        ],
        axis=1,
    )
    case_par = jnp.stack([tie_x, fault_z])
    voltage, relay_rate, square = screen_branches(
        where, g_all, case_par, fd, pick, par, pieces, rows
    )
    bit = 1
    while bit < n_case:
        square = jnp.maximum(
            square, lax.ppermute(square, "case", [(i, i ^ bit) for i in range(n_case)])
        )
        bit *= 2
    powered = jnp.exp2(power * jnp.log2(square.reshape(-1) + 1e-4))
    worst_rate = jnp.maximum(powered - 1.0, 0.0) * rate
    return (voltage, relay_rate, worst_rate)


def solution(mesh):
    in_specs = (
        P("bus", None),
        P(),
        P("case"),
        P("case", None),
        P("case"),
        P("case"),
        P(),
        P("bus", None),
        P("bus"),
        P("bus"),
        P("bus"),
        P("bus"),
    )
    out_specs = (P("bus", "case"), P("bus", "case"), P("bus"))
    return jax.shard_map(
        per_device, mesh=mesh, in_specs=in_specs, out_specs=out_specs, check_vma=False
    )
```

time: 104 us -> 52.7 us (0.51)
  local copies, waits for them, and re-layouts: 46.5 us -> 6.72 us
  blocking collectives: 29.7 us -> 0 us
  Pallas kernels: 0 us -> 19.2 us
  other arithmetic: 17.1 us -> 2.11 us
  starting transfers between devices: 2.6 us -> 13.2 us
  waiting for transfers between devices: 6.77 us -> 10.2 us
    gather x12 -> x0, local copies, waits for them, and re-layouts: 36.2 us -> none  [the longest x1 5.8 us: per_device(): jnp.take(z_columns, switch_cols[:, 1], axis=1)]
    psum x1 -> x0, blocking collectives: 23.4 us -> none  [per_device(): entry_sums = lax.psum(partial_value, 'bus')]
    pallas_call x0 -> x3, Pallas kernels: none -> 19.2 us  [the longest x1 9 us: screen_branches(): pl.pallas_call(kernel, in_specs=[pl.BlockSpec(memory_space=pltpu.SMEM)] +...]
    pmax x1 -> x0, blocking collectives: 6.31 us -> none  [per_device(): worst_rate = lax.pmax(jnp.max(relay_rate, axis=1), 'case')]
    reduce_max x1 -> x0, other arithmetic: 5.89 us -> none  [per_device(): worst_rate = lax.pmax(jnp.max(relay_rate, axis=1), 'case')]
    ppermute x2 -> x6, starting transfers between devices: 2.6 us -> 8.32 us  [the longest x1 4.99 us: per_device(): pieces = [lax.ppermute(send, ('bus', 'case'), pairs)]]
    all_to_all x0 -> x1, starting transfers between devices: none -> 4.87 us  [per_device(): g_all = lax.all_to_all(g_part, 'bus', 0, 0)]
    reduce_sum x1 -> x0, other arithmetic: 4.28 us -> none  [pick_rows(): return jnp.sum(jnp.where(row_ids == wanted[None, :], column, 0.0), axis=0)]
  transfers between devices with their start and end apart: 2 -> 7, of which waited for: 2 -> 4; matrix products, arithmetic and copies ran while one was open for 1% -> 1% of each run, Pallas kernels for 0% -> 14%
where the time goes in v1:
time: 52.7 us; the launch traced here: 52.3 us
  Pallas kernels  19.2 us (36%)
  starting transfers between devices  13.2 us (25%)
  waiting for transfers between devices  10.2 us (19%)
  local copies, waits for them, and re-layouts  6.72 us (13%)
  other arithmetic  2.11 us (4%)
  between operations  0.93 us (2%)
    pallas_call x1, Pallas kernels, screen_branches(): pl.pallas_call(kernel, in_specs=[pl.BlockSpec(memory_space=pltpu.SMEM)] +...  9 us
    pallas_call x1, Pallas kernels, pick_columns(): pl.pallas_call(columns_kernel, in_specs=[pl.BlockSpec(memory_space=pl.ANY...  7.33 us
    ppermute x3, waiting for transfers between devices, per_device(): pieces = pieces + [lax.ppermute(x, 'case', swap) for x in pieces]  6.97 us
    unnamed x26, local copies, waits for them, and re-layouts  6.35 us
    ppermute x1, starting transfers between devices, per_device(): pieces = [lax.ppermute(send, ('bus', 'case'), pairs)]  4.99 us
    all_to_all x1, starting transfers between devices, per_device(): g_all = lax.all_to_all(g_part, 'bus', 0, 0)  4.87 us
    ppermute x2, waiting for transfers between devices, per_device(): lax.ppermute(square, 'case', [(i, i ^ bit) for i in range(n_case)])  3.2 us
    pallas_call x1, Pallas kernels, gather_send_rows(): pl.pallas_call(send_kernel, grid_spec=pltpu.PrefetchScalarGridSpec(num_sc...  2.84 us
  transfers between devices with their start and end apart: 7, of which 4 were waited for; matrix products, arithmetic and copies ran while one was open for 1% of the time, Pallas kernels for 14%

profile of v1, /device:TPU:0, one launch (start us, length us, event | category | flops | bytes accessed | tf_op | source)
XLA Modules:
  0.0 52.3 jit_solution(7906991515221490139)
XLA Ops:
  0.6 0.0 copy-start.9
  0.6 0.0 copy-start.8
  0.7 0.0 copy-start.10
  0.7 0.8 %subtract_bitcast_fusion = s32[64]{0:T(128)S(1)} fusion(s32[8,2,128]{2,1,0:T(2,128)} %param.18, s32[]{:T(128)S(6)} %select_n.39, s32[]{:T(128)S(6)} %select_n.40, s32[]{:T(128)S(6)} %select_n.42, s32[]{:T(128)S(6)} %mul.45), kind=kLoop, calls=%fused_computation.18 | loop fusion | flops 64 | bytes 528 | tf_op jit(solution)/shard_map/sub | solution.py:230
  1.5 0.6 %pad_add_fusion.2.meta_ref = s32[65]{0:T(128)} fusion(s32[64]{0:T(128)S(1)} %subtract_bitcast_fusion, s32[1]{0:T(128)} %bitcast.9), kind=kLoop, calls=%fused_computation.17 | loop fusion | flops 65 | bytes 520 | tf_op jit(solution)/shard_map/concatenate | solution.py:230
  2.0 0.0 copy-start.6
  2.0 0.0 copy-start.7
  2.0 0.0 copy-start.12
  2.1 2.8 %gather_send_rows.1 = f32[64,1024]{1,0:T(8,128)} custom-call(s32[65]{0:T(128)} %pad_add_fusion.2.meta_ref, f32[1024,1024]{1,0:T(8,128)} %z_ref.1), custom_call_target="tpu_custom_call" | custom-call | tf_op jit(solution)/shard_map/gather_send_rows/pallas_call | solution.py:32
  4.9 0.0 copy-start.4
  4.9 0.0 copy-start.5
  4.9 0.0 copy-start.3
  4.9 0.0 copy-start.11
  4.9 5.0 %collective-permute-start = (f32[64,1024]{1,0:T(8,128)}, f32[64,1024]{1,0:T(8,128)S(1)}, u32[]{:S(2)}, u32[]{:S(2)}) collective-permute-start(f32[64,1024]{1,0:T(8,128)} %gather_send_rows.1), channel_id=1, source_target_pairs={{0,4},{1,5},{4,8},{5,9},{6,2},{7,3},{8,12},{9,13},{10,6},{11,7},{1... | collective-permute-start | bytes 786440 | tf_op jit(solution)/shard_map/ppermute | solution.py:238
  9.9 0.0 copy-done.9
  9.9 0.0 copy-done.8
  9.9 0.0 copy-done.10
  10.0 0.0 copy-start
  10.0 2.2 %copy-done = f32[1024,1024]{1,0:T(8,128)S(1)} copy-done((f32[1024,1024]{1,0:T(8,128)S(1)}, f32[1024,1024]{1,0:T(8,128)}, u32[]{:S(2)}) %copy-start) | copy-done | bytes 4194328
  12.2 7.3 %pick_columns.1 = (f32[1024,1024]{1,0:T(8,128)S(1)}, bf16[1024,1024]{1,0:T(8,128)(2,1)S(1)}, f32[8,3,512]{2,1,0:T(4,128)}) custom-call(f32[1024,1024]{1,0:T(8,128)S(1)} %copy-done, s32[3,512]{1,0:T(4,128)S(1)} %pad_add_fusion.cases_ref, s32[1,1024]{1,0:T(1,128)S(1)} %bitcast.24), custom_call_target="tpu_custom_call" | custom-call | tf_op jit(solution)/shard_map/pick_columns/pallas_call | solution.py:91
  19.5 0.0 copy-start.1
  19.5 1.9 %copy-done.1 = f32[1024,1024]{1,0:T(8,128)} copy-done((f32[1024,1024]{1,0:T(8,128)}, f32[1024,1024]{1,0:T(8,128)S(1)}, u32[]{:S(2)}) %copy-start.1) | copy-done | bytes 4194328
  21.4 4.9 %all-to-all-start = ((f32[8,3,512]{2,1,0:T(4,128)}), f32[8,3,512]{2,1,0:T(4,128)S(1)}, u32[]{:S(2)}, u32[]{:S(2)}) async-start(f32[8,3,512]{2,1,0:T(4,128)} %get-tuple-element.9), calls=%async_computation | async-start | bytes 131072 | tf_op jit(solution)/shard_map/all_to_all | solution.py:251
  26.3 0.0 copy-done.4
  26.3 0.0 collective-permute-done.refs_6_
  26.3 1.6 %collective-permute-start.1 = (f32[64,1024]{1,0:T(8,128)S(1)}, f32[64,1024]{1,0:T(8,128)S(1)}, u32[]{:S(2)}, u32[]{:S(2)}) collective-permute-start(f32[64,1024]{1,0:T(8,128)S(1)} %collective-permute-done.refs_6_), channel_id=1, source_target_pairs={{0,2},{1,3},{2,0},{3,1},{4,6},{5,7},{6,4},{7,5},{8,10},{9,11},{10,... | collective-permute-start | bytes 786440 | tf_op jit(solution)/shard_map/ppermute | solution.py:248
  27.9 0.0 copy-done.6
  27.9 0.0 copy-done.5
  27.9 0.0 copy-done.7
  27.9 0.0 copy-done.3
  28.0 0.1 collective-permute-start.2
  28.0 5.9 %collective-permute-done.1.refs_7_ = f32[64,1024]{1,0:T(8,128)S(1)} collective-permute-done((f32[64,1024]{1,0:T(8,128)S(1)}, f32[64,1024]{1,0:T(8,128)S(1)}, u32[]{:S(2)}, u32[]{:S(2)}) %collective-permute-start.1) | collective-permute-done | bytes 262176 | tf_op jit(solution)/shard_map/ppermute | solution.py:248
  33.9 0.0 collective-permute-start.3
  34.0 0.1 stack.53
  34.1 0.3 copy.22.refs_5_
  34.3 0.0 copy-done.12
  34.3 0.0 copy-done.11
  34.4 0.1 pad_add_fusion.1.refs_0_
  34.4 0.0 all-to-all-done.refs_1_
  34.5 0.0 collective-permute-done.2.refs_8_
  34.5 1.1 %collective-permute-done.3.refs_9_ = f32[64,1024]{1,0:T(8,128)} collective-permute-done((f32[64,1024]{1,0:T(8,128)S(1)}, f32[64,1024]{1,0:T(8,128)}, u32[]{:S(2)}, u32[]{:S(2)}) %collective-permute-start.3) | collective-permute-done | bytes 262176 | tf_op jit(solution)/shard_map/ppermute | solution.py:248
  35.6 0.0 copy-start.2
  35.6 2.2 %copy-done.2 = f32[1024,1024]{1,0:T(8,128)S(1)} copy-done((f32[1024,1024]{1,0:T(8,128)S(1)}, f32[1024,1024]{1,0:T(8,128)}, u32[]{:S(2)}) %copy-start.2) | copy-done | bytes 4194328
  37.8 9.0 %screen_branches.1 = (f32[1024,512]{1,0:T(8,128)}, f32[1536,512]{1,0:T(8,128)}, f32[12,128]{1,0:T(8,128)S(1)}) custom-call(s32[4]{0:T(128)S(1)} %pad_add_fusion.1.refs_0_, f32[8,3,512]{2,1,0:T(4,128)S(1)} %all-to-all-done.refs_1_, f32[2,512]{1,0:T(2,128)S(1)} %pad_maximum_fusion.refs_2_, f32[1024,1024]{1,0:T(8,128)S(1)} %copy-done.2, ...), custom_call_target="tpu_custom_call" | custom-call | tf_op jit(solution)/shard_map/screen_branches/pallas_call | solution.py:181
  46.8 0.2 collective-permute-start.4
  46.9 1.0 %collective-permute-done.4 = f32[12,128]{1,0:T(8,128)S(1)} collective-permute-done((f32[12,128]{1,0:T(8,128)S(1)}, f32[12,128]{1,0:T(8,128)S(1)}, u32[]{:S(2)}, u32[]{:S(2)}) %collective-permute-start.4) | collective-permute-done | bytes 6176 | tf_op jit(solution)/shard_map/ppermute | solution.py:279
  48.0 1.5 %collective-permute-start.5 = (f32[12,128]{1,0:T(8,128)S(1)}, f32[12,128]{1,0:T(8,128)S(1)}, u32[]{:S(2)}, u32[]{:S(2)}) collective-permute-start(f32[12,128]{1,0:T(8,128)S(1)} %max.12), channel_id=1, source_target_pairs={{0,2},{1,3},{2,0},{3,1},{4,6},{5,7},{6,4},{7,5},{8,10},{9,11},{10,... | collective-permute-start | bytes 18440 | tf_op jit(solution)/shard_map/ppermute | solution.py:279
  49.5 2.1 %collective-permute-done.5 = f32[12,128]{1,0:T(8,128)S(1)} collective-permute-done((f32[12,128]{1,0:T(8,128)S(1)}, f32[12,128]{1,0:T(8,128)S(1)}, u32[]{:S(2)}, u32[]{:S(2)}) %collective-permute-start.5) | collective-permute-done | bytes 6176 | tf_op jit(solution)/shard_map/ppermute | solution.py:279
  51.7 0.6 %fusion.4 = f32[1536]{0:T(1024)} fusion(f32[12,128]{1,0:T(8,128)S(1)} %max.12, f32[12,128]{1,0:T(8,128)S(1)} %collective-permute-done.5, pred[1536]{0:T(1024)(128)(4,1)S(1)} %get-tuple-element.17, pred[1536]{0:T(1024)(128)(4,1)S(1)} %get-tuple-element.16, f32[1536]{0:T(1024)S(1)} %copy-done.3), kind=kLoop, calls=%fused_computation.6 | loop fusion | flops 21504 | bytes 27648 | tf_op jit(solution)/shard_map/mul | solution.py:283
  (13 shorter events, 0.1 us)
Async XLA Ops:
  0.6 9.3 %copy-start.9 = (s32[1024]{0:T(1024)S(1)}, s32[1024]{0:T(1024)}, u32[]{:S(2)}) copy-start(s32[1024]{0:T(1024)} %param.13) | copy-start | bytes 12292
  0.6 9.3 %copy-start.8 = (s32[512,2]{0,1:T(2,128)S(1)}, s32[512,2]{0,1:T(2,128)}, u32[]{:S(2)}) copy-start(s32[512,2]{0,1:T(2,128)} %param.15) | copy-start | bytes 12292
  0.7 9.3 %copy-start.10 = (s32[512]{0:T(512)S(1)}, s32[512]{0:T(512)}, u32[]{:S(2)}) copy-start(s32[512]{0:T(512)} %param.14) | copy-start | bytes 6148
  2.0 25.9 %copy-start.6 = (f32[1536]{0:T(1024)S(1)}, f32[1536]{0:T(1024)}, u32[]{:S(2)}) copy-start(f32[1536]{0:T(1024)} %param.21) | copy-start | bytes 18436
  2.0 25.9 %copy-start.7 = (s32[1536]{0:T(1024)S(1)}, s32[1536]{0:T(1024)}, u32[]{:S(2)}) copy-start(s32[1536]{0:T(1024)} %param.23) | copy-start | bytes 18436
  2.0 32.3 %copy-start.12 = (f32[512]{0:T(512)S(1)}, f32[512]{0:T(512)}, u32[]{:S(2)}) copy-start(f32[512]{0:T(512)} %param.16) | copy-start | bytes 6148
  4.9 21.4 %copy-start.4 = (s32[1536,2]{0,1:T(2,128)S(1)}, s32[1536,2]{0,1:T(2,128)}, u32[]{:S(2)}) copy-start(s32[1536,2]{0,1:T(2,128)} %param.19) | copy-start | bytes 36868
  4.9 23.0 %copy-start.5 = (f32[1536]{0:T(1024)S(1)}, f32[1536]{0:T(1024)}, u32[]{:S(2)}) copy-start(f32[1536]{0:T(1024)} %param.20) | copy-start | bytes 18436
  4.9 23.0 %copy-start.3 = (f32[1536]{0:T(1024)S(1)}, f32[1536]{0:T(1024)}, u32[]{:S(2)}) copy-start(f32[1536]{0:T(1024)} %param.22) | copy-start | bytes 18436
  4.9 29.4 %copy-start.11 = (f32[512]{0:T(512)S(1)}, f32[512]{0:T(512)}, u32[]{:S(2)}) copy-start(f32[512]{0:T(512)} %param.17) | copy-start | bytes 6148
  4.9 21.4 %collective-permute-start = (f32[64,1024]{1,0:T(8,128)}, f32[64,1024]{1,0:T(8,128)S(1)}, u32[]{:S(2)}, u32[]{:S(2)}) collective-permute-start(f32[64,1024]{1,0:T(8,128)} %gather_send_rows.1), channel_id=1, source_target_pairs={{0,4},{1,5},{4,8},{5,9},{6,2},{7,3},{8,12},{9,13},{10,6},{11,7},{1... | collective-permute-start | bytes 786440 | tf_op jit(solution)/shard_map/ppermute | solution.py:238
  10.0 2.2 %copy-start = (f32[1024,1024]{1,0:T(8,128)S(1)}, f32[1024,1024]{1,0:T(8,128)}, u32[]{:S(2)}) copy-start(f32[1024,1024]{1,0:T(8,128)} %z_ref.1) | copy-start | bytes 12582916
  19.5 1.9 %copy-start.1 = (f32[1024,1024]{1,0:T(8,128)}, f32[1024,1024]{1,0:T(8,128)S(1)}, u32[]{:S(2)}) copy-start(f32[1024,1024]{1,0:T(8,128)S(1)} %get-tuple-element.10.refs_3_) | copy-start | bytes 12582916
  21.4 13.0 %all-to-all-start = ((f32[8,3,512]{2,1,0:T(4,128)}), f32[8,3,512]{2,1,0:T(4,128)S(1)}, u32[]{:S(2)}, u32[]{:S(2)}) async-start(f32[8,3,512]{2,1,0:T(4,128)} %get-tuple-element.9), calls=%async_computation | async-start | bytes 131072 | tf_op jit(solution)/shard_map/all_to_all | solution.py:251
  26.3 7.6 %collective-permute-start.1 = (f32[64,1024]{1,0:T(8,128)S(1)}, f32[64,1024]{1,0:T(8,128)S(1)}, u32[]{:S(2)}, u32[]{:S(2)}) collective-permute-start(f32[64,1024]{1,0:T(8,128)S(1)} %collective-permute-done.refs_6_), channel_id=1, source_target_pairs={{0,2},{1,3},{2,0},{3,1},{4,6},{5,7},{6,4},{7,5},{8,10},{9,11},{10,... | collective-permute-start | bytes 786440 | tf_op jit(solution)/shard_map/ppermute | solution.py:248
  28.0 6.5 %collective-permute-start.2 = (f32[64,1024]{1,0:T(8,128)S(1)}, f32[64,1024]{1,0:T(8,128)}, u32[]{:S(2)}, u32[]{:S(2)}) collective-permute-start(f32[64,1024]{1,0:T(8,128)S(1)} %collective-permute-done.refs_6_), channel_id=1, source_target_pairs={{0,1},{1,0},{2,3},{3,2},{4,5},{5,4},{6,7},{7,6},{8,9},{9,8},{10,11... | collective-permute-start | bytes 786440 | tf_op jit(solution)/shard_map/ppermute | solution.py:248
  33.9 1.7 %collective-permute-start.3 = (f32[64,1024]{1,0:T(8,128)S(1)}, f32[64,1024]{1,0:T(8,128)}, u32[]{:S(2)}, u32[]{:S(2)}) collective-permute-start(f32[64,1024]{1,0:T(8,128)S(1)} %collective-permute-done.1.refs_7_), channel_id=1, source_target_pairs={{0,1},{1,0},{2,3},{3,2},{4,5},{5,4},{6,7},{7,6},{8,9},{9,8},{10,11... | collective-permute-start | bytes 786440 | tf_op jit(solution)/shard_map/ppermute | solution.py:248
  35.6 2.2 %copy-start.2 = (f32[1024,1024]{1,0:T(8,128)S(1)}, f32[1024,1024]{1,0:T(8,128)}, u32[]{:S(2)}) copy-start(f32[1024,1024]{1,0:T(8,128)} %copy-done.1) | copy-start | bytes 12582916
  46.8 1.2 %collective-permute-start.4 = (f32[12,128]{1,0:T(8,128)S(1)}, f32[12,128]{1,0:T(8,128)S(1)}, u32[]{:S(2)}, u32[]{:S(2)}) collective-permute-start(f32[12,128]{1,0:T(8,128)S(1)} %get-tuple-element.14), channel_id=1, source_target_pairs={{0,1},{1,0},{2,3},{3,2},{4,5},{5,4},{6,7},{7,6},{8,9},{9,8},{10,11... | collective-permute-start | bytes 18440 | tf_op jit(solution)/shard_map/ppermute | solution.py:279
  48.0 3.7 %collective-permute-start.5 = (f32[12,128]{1,0:T(8,128)S(1)}, f32[12,128]{1,0:T(8,128)S(1)}, u32[]{:S(2)}, u32[]{:S(2)}) collective-permute-start(f32[12,128]{1,0:T(8,128)S(1)} %max.12), channel_id=1, source_target_pairs={{0,2},{1,3},{2,0},{3,1},{4,6},{5,7},{6,4},{7,5},{8,10},{9,11},{10,... | collective-permute-start | bytes 18440 | tf_op jit(solution)/shard_map/ppermute | solution.py:279

commit v2 on v1

v2 whole, which is shorter than its diff:
```python
import functools

import jax
import jax.numpy as jnp
from jax import lax
from jax.experimental import pallas as pl
from jax.experimental.pallas import tpu as pltpu
from jax.sharding import PartitionSpec as P

RIM = 256
TILE = 256
F32 = jnp.float32
BF16 = jnp.bfloat16


def split_hi_lo(value):
    hi = value.astype(BF16)
    return hi, (value - hi.astype(F32)).astype(BF16)


def two_pass(hi, lo, rhs):
    return jnp.dot(hi, rhs, preferred_element_type=F32) + jnp.dot(
        lo, rhs, preferred_element_type=F32
    )


def in_hbm(*arrays):
    return [pltpu.with_memory_space_constraint(x, pltpu.HBM) for x in arrays]


def stage_kernel(
    half, z_hbm, lists_hbm, fault_hbm, switch_hbm, send_ref, z_ref, pick_ref, lists, cases, sems
):
    rows = z_ref.shape[0]
    tiles = rows // RIM
    piece = send_ref.shape[0]
    my_bus, my_case = lax.axis_index("bus"), lax.axis_index("case")
    down = my_case // half
    rim = (1 - down) * (tiles - 1)

    def load(t):
        span = pl.ds(pl.multiple_of(lax.rem(rim + t, tiles) * RIM, RIM), RIM)
        return pltpu.make_async_copy(z_hbm.at[span], z_ref.at[span], sems.at[t])

    loads = [load(t) for t in range(tiles)]
    small = [
        pltpu.make_async_copy(lists_hbm.at[my_bus], lists, sems.at[tiles]),
        pltpu.make_async_copy(fault_hbm, cases.at[pl.ds(0, 1)], sems.at[tiles + 1]),
        pltpu.make_async_copy(switch_hbm, cases.at[pl.ds(8, 2)], sems.at[tiles + 2]),
    ]
    loads[0].start()
    for copy in small + loads[1:]:
        copy.start()
    for copy in small[:1] + loads[:1]:
        copy.wait()
    base = (my_case % half) * piece
    for i in range(piece):
        send_ref[pl.ds(i, 1), :] = z_ref[pl.ds(lists[1 - down, base + i], 1), :]
    for copy in small[1:]:
        copy.wait()
    fill_picks(cases[0:1, :], cases[8:10, :], pick_ref)
    for copy in loads[1:]:
        copy.wait()


def stage(z_columns, boundary_send, fault, switch, n_case):
    rows, cols = z_columns.shape
    half = n_case // 2
    count = fault.shape[1]
    hbm = pl.BlockSpec(memory_space=pltpu.HBM)
    vmem = pl.BlockSpec(memory_space=pltpu.VMEM)
    return pl.pallas_call(
        functools.partial(stage_kernel, half),
        in_specs=[hbm] * 4,
        out_specs=[vmem] * 3,
        out_shape=[
            pltpu.VMEM((boundary_send.shape[2] // half, cols), F32),
            pltpu.VMEM((rows, cols), F32),
            pltpu.VMEM((cols, 2 * count), BF16),
        ],
        scratch_shapes=[
            pltpu.SMEM(boundary_send.shape[1:], jnp.int32),
            pltpu.VMEM((16, count), jnp.int32),
            pltpu.SemaphoreType.DMA((rows // RIM + 3,)),
        ],
        compiler_params=pltpu.CompilerParams(vmem_limit_bytes=4 * 2**20),
        name="stage",
    )(*in_hbm(z_columns, boundary_send, fault, switch))


def fill_picks(f, ab, pick):
    cols, count = pick.shape[0], f.shape[1]
    a, b = ab[0:1, :], ab[1:2, :]
    for t in range(cols // TILE):
        k = lax.broadcasted_iota(jnp.int32, (TILE, count), 0) + t * TILE
        span = pl.ds(t * TILE, TILE)
        pick[span, :count] = jnp.where(k == f, 1.0, 0.0).astype(BF16)
        pick[span, count:] = jnp.where(k == a, 1.0, jnp.where(k == b, -1.0, 0.0)).astype(BF16)


def columns_kernel(z_ref, pick, fault_ref, switch_ref, resident_ref, fd_ref, g_ref):
    rows, cols = z_ref.shape
    cases = fault_ref.shape[1]
    f, a, b = fault_ref[...], switch_ref[0:1, :], switch_ref[1:2, :]
    resident = resident_ref[...] - lax.axis_index("bus") * rows
    g1 = jnp.zeros((1, cases), F32)
    g2 = jnp.zeros((1, cases), F32)
    g3 = jnp.zeros((1, cases), F32)
    for t in range(rows // TILE):
        span = pl.ds(t * TILE, TILE)
        row = lax.broadcasted_iota(jnp.int32, (TILE, cols), 0) + t * TILE
        k = lax.broadcasted_iota(jnp.int32, (TILE, cols), 1)
        owner = jnp.max(jnp.where(row == resident, k, -1), axis=1, keepdims=True)
        hi, lo = split_hi_lo(z_ref[span, :])
        fd = two_pass(hi, lo, pick[...])
        fd_ref[span, :] = fd
        fault, diff = fd[:, :cases], fd[:, cases:]
        at_f = owner == f
        g3 += jnp.sum(jnp.where(at_f, fault, 0.0), axis=0, keepdims=True)
        g2 += jnp.sum(jnp.where(at_f, diff, 0.0), axis=0, keepdims=True)
        g1 += jnp.sum(
            jnp.where(owner == a, diff, jnp.where(owner == b, -diff, 0.0)), axis=0, keepdims=True
        )
    g_ref[...] = jnp.concatenate([g1, g2, g3, jnp.zeros((g_ref.shape[0] - 3, cases), F32)])


def pick_columns(z, pick, fault, switch, resident):
    count = fault.shape[1]
    vmem = pl.BlockSpec(memory_space=pltpu.VMEM)
    return pl.pallas_call(
        columns_kernel,
        in_specs=[vmem] * 5,
        out_specs=[vmem, vmem],
        out_shape=[
            pltpu.VMEM((z.shape[0], 2 * count), F32),
            pltpu.VMEM((4, count), F32),
        ],
        compiler_params=pltpu.CompilerParams(vmem_limit_bytes=16 * 2**20),
        name="pick_columns",
    )(z, pick, fault, switch, resident)


def curve_constants(curve):
    half_power = jnp.where(curve == 0, 0.01, jnp.where(curve == 1, 0.5, 1.0)).astype(F32)
    factor = jnp.where(curve == 0, 0.14, jnp.where(curve == 1, 13.5, 80.0)).astype(F32)
    return half_power, factor


def pack_kernel(ends_ref, x_ref, pickup_ref, tds_ref, curve_ref, own, other, packed_ref, par_ref, sems):
    size = own.shape[0]
    loads = [
        pltpu.make_async_copy(own, packed_ref.at[pl.ds(0, size)], sems.at[0]),
        pltpu.make_async_copy(other, packed_ref.at[pl.ds(size, size)], sems.at[1]),
    ]
    for load in loads:
        load.start()
    ends = ends_ref[...].astype(F32)
    gain = 1.0 / (x_ref[...] * pickup_ref[...])
    half_power, factor = curve_constants(curve_ref[...])
    rate = 1.0 / (factor * tds_ref[...])
    par = jnp.concatenate([ends, gain, half_power, rate, jnp.zeros((3, ends.shape[1]), F32)])
    for c in range(0, ends.shape[1], 128):
        par_ref[pl.ds(c, 128), :] = par[:, c : c + 128].T
    for load in loads:
        load.wait()


def pack(branch_rows, own, other):
    vmem = pl.BlockSpec(memory_space=pltpu.VMEM)
    anywhere = pl.BlockSpec(memory_space=pl.ANY)
    return pl.pallas_call(
        pack_kernel,
        in_specs=[vmem] * len(branch_rows) + [anywhere] * 2,
        out_specs=[vmem, vmem],
        out_shape=[
            pltpu.VMEM((2 * own.shape[0], own.shape[1]), F32),
            pltpu.VMEM((branch_rows[0].shape[1], 8), F32),
        ],
        scratch_shapes=[pltpu.SemaphoreType.DMA((2,))],
        compiler_params=pltpu.CompilerParams(vmem_limit_bytes=4 * 2**20),
        name="pack",
    )(*branch_rows, own, other)


def boundary_kernel(order, fault_ref, switch_ref, *refs):
    n = len(order) // 2
    pairs = refs[:n]
    out_ref, pick, zb, sems = refs[n:]
    size = pairs[0].shape[0] // 2
    my_case = lax.axis_index("case")
    loads = []
    for i, mask in enumerate(order):
        first = pl.multiple_of((my_case ^ mask) * size, size)
        piece = pairs[i // 2].at[pl.ds(i % 2 * size, size)]
        loads.append(pltpu.make_async_copy(piece, zb.at[pl.ds(first, size)], sems.at[i]))
        loads[-1].start()
    fill_picks(fault_ref[...], switch_ref[...], pick)
    for load in loads:
        load.wait()
    hi, lo = split_hi_lo(zb[...])
    out_ref[...] = two_pass(hi, lo, pick[...])


def boundary_columns(order, fault, switch, pairs):
    cols = pairs[0].shape[1]
    total = sum(pair.shape[0] for pair in pairs)
    count = fault.shape[1]
    vmem = pl.BlockSpec(memory_space=pltpu.VMEM)
    anywhere = pl.BlockSpec(memory_space=pl.ANY)
    return pl.pallas_call(
        functools.partial(boundary_kernel, order),
        in_specs=[vmem] * 2 + [anywhere] * len(pairs),
        out_specs=vmem,
        out_shape=pltpu.VMEM((total, 2 * count), F32),
        scratch_shapes=[
            pltpu.VMEM((cols, 2 * count), BF16),
            pltpu.VMEM((total, cols), F32),
            pltpu.SemaphoreType.DMA((len(order),)),
        ],
        compiler_params=pltpu.CompilerParams(vmem_limit_bytes=16 * 2**20),
        cost_estimate=pl.CostEstimate(
            flops=8 * total * cols * count, bytes_accessed=8 * total * cols, transcendentals=0
        ),
        name="boundary_columns",
    )(fault, switch, *pairs)


def relay_of_square(square, power, rate):
    return jnp.maximum(jnp.exp2(power * jnp.log2(square + 1e-4)) - 1.0, 0.0) * rate


def branch_kernel(
    early,
    g_ref,
    tie_ref,
    fault_ref,
    par_ref,
    fd_ref,
    edge_ref,
    volt_hbm,
    relay_hbm,
    square_ref,
    worst_ref,
    vbuf,
    rbuf,
    uh,
    ul,
    vsem,
    rsem,
):
    rows, cases = vbuf.shape
    branches = par_ref.shape[0]
    ext = uh.shape[0]
    g1, g2, g3 = g_ref[0:1, :], g_ref[1:2, :], g_ref[2:3, :]
    ratio = g2 / (tie_ref[...] + g1)
    amps = 1.0 / (g3 - g2 * ratio + fault_ref[...])

    def sag_of(fd, span):
        sag = (fd[:, :cases] - fd[:, cases:] * ratio) * amps
        uh[span, :], ul[span, :] = split_hi_lo(sag)
        return sag

    sag_of(edge_ref[...], pl.ds(rows, ext - rows))
    copies = []
    for t in range(rows // TILE):
        span = pl.ds(t * TILE, TILE)
        vbuf[span, :] = 1.0 - sag_of(fd_ref[span, :], span)
        copies.append(pltpu.make_async_copy(vbuf.at[span], volt_hbm.at[span], vsem.at[t]))
        copies[-1].start()
    for t in range(branches // TILE):
        span = pl.ds(t * TILE, TILE)
        par = par_ref[span, :]
        bus = lax.broadcasted_iota(jnp.int32, (TILE, ext), 1).astype(F32)
        ends = jnp.where(
            bus == par[:, 1:2], 1.0, jnp.where(bus == par[:, 0:1], -1.0, 0.0)
        ).astype(BF16)
        drop = jnp.dot(ends, uh[...], preferred_element_type=F32) + jnp.dot(
            ends, ul[...], preferred_element_type=F32
        )
        scaled = drop * par[:, 2:3]
        square = scaled * scaled
        if t * TILE < early:
            rbuf[span, :] = relay_of_square(square, par[:, 3:4], par[:, 4:5])
            copies.append(pltpu.make_async_copy(rbuf.at[span], relay_hbm.at[span], rsem.at[t]))
            copies[-1].start()
        else:
            square_ref[pl.ds(t * TILE - early, TILE), :] = square
        largest = square[:, :128]
        for c in range(128, cases, 128):
            largest = jnp.maximum(largest, square[:, c : c + 128])
        for h in range(TILE // 128):
            worst_ref[pl.ds(t * (TILE // 128) + h, 1), :] = jnp.max(
                largest[h * 128 : (h + 1) * 128, :].T, axis=0, keepdims=True
            )
    for copy in copies:
        copy.wait()


def screen_branches(g, tie_x, fault_z, par, fd, edge, early):
    count = tie_x.shape[1]
    rows = fd.shape[0]
    branches = par.shape[0]
    ext = rows + edge.shape[0]
    vmem = pl.BlockSpec(memory_space=pltpu.VMEM)
    hbm = pl.BlockSpec(memory_space=pltpu.HBM)
    return pl.pallas_call(
        functools.partial(branch_kernel, early),
        in_specs=[vmem] * 6,
        out_specs=[hbm, hbm, vmem, vmem],
        out_shape=[
            jax.ShapeDtypeStruct((rows, count), F32),
            jax.ShapeDtypeStruct((branches, count), F32),
            pltpu.VMEM((branches - early, count), F32),
            pltpu.VMEM((branches // 128, 128), F32),
        ],
        scratch_shapes=[
            pltpu.VMEM((rows, count), F32),
            pltpu.VMEM((early, count), F32),
            pltpu.VMEM((ext, count), BF16),
            pltpu.VMEM((ext, count), BF16),
            pltpu.SemaphoreType.DMA((rows // TILE,)),
            pltpu.SemaphoreType.DMA((branches // TILE,)),
        ],
        compiler_params=pltpu.CompilerParams(vmem_limit_bytes=32 * 2**20),
        name="screen_branches",
    )(g, tie_x, fault_z, par, fd, edge)


def late_kernel(early, square_ref, par_ref, relay_in, relay_hbm, rbuf, sems):
    copies = []
    for t in range(square_ref.shape[0] // TILE):
        span = pl.ds(t * TILE, TILE)
        par = par_ref[pl.ds(early + t * TILE, TILE), :]
        rbuf[span, :] = relay_of_square(square_ref[span, :], par[:, 3:4], par[:, 4:5])
        copies.append(
            pltpu.make_async_copy(
                rbuf.at[span], relay_hbm.at[pl.ds(early + t * TILE, TILE)], sems.at[t]
            )
        )
        copies[-1].start()
    for copy in copies:
        copy.wait()


def late_relays(square, par, relay_rate, early):
    vmem = pl.BlockSpec(memory_space=pltpu.VMEM)
    hbm = pl.BlockSpec(memory_space=pltpu.HBM)
    return pl.pallas_call(
        functools.partial(late_kernel, early),
        in_specs=[vmem, vmem, hbm],
        out_specs=hbm,
        out_shape=jax.ShapeDtypeStruct(relay_rate.shape, F32),
        input_output_aliases={2: 0},
        scratch_shapes=[
            pltpu.VMEM(square.shape, F32),
            pltpu.SemaphoreType.DMA((square.shape[0] // TILE,)),
        ],
        compiler_params=pltpu.CompilerParams(vmem_limit_bytes=8 * 2**20),
        cost_estimate=pl.CostEstimate(
            flops=8 * square.size, bytes_accessed=8 * square.size, transcendentals=2 * square.size
        ),
        name="late_relays",
    )(square, par, relay_rate)


def per_device(
    z_columns,
    resident_bus,
    fault_col,
    switch_cols,
    tie_x,
    fault_z,
    boundary_send,
    branch_ends,
    branch_x,
    pickup,
    tds,
    curve,
):
    n_bus, n_case = lax.axis_size("bus"), lax.axis_size("case")
    half = n_case // 2
    fault, switch = fault_col[None], switch_cols.T
    send, z, pick = stage(z_columns, boundary_send, fault, switch, n_case)
    pairs = []
    for s in range(n_bus):
        for c in range(n_case):
            to = s + 1 if c < half else s - 1
            if 0 <= to < n_bus:
                pairs.append((s * n_case + c, to * n_case + c))
    own = lax.ppermute(send, ("bus", "case"), pairs)

    fd, g = pick_columns(z, pick, fault, switch, resident_bus[None])
    g, own = lax.optimization_barrier((g, own))

    def add_over_bus(g, bit):
        return g + lax.ppermute(g, "bus", [(i, i ^ bit) for i in range(n_bus)])

    other = lax.ppermute(own, "case", [(i, i ^ half) for i in range(n_case)])
    bit = 1
    while bit < n_bus // 2:
        g = add_over_bus(g, bit)
        bit *= 2
    g, other = lax.optimization_barrier((g, other))
    branch_rows = [branch_ends.T, branch_x[None], pickup[None], tds[None], curve[None]]
    packed, par = pack(branch_rows, own, other)
    packs = [packed]
    order = [0, half]
    bit = half // 2
    while bit:
        swap = [(i, i ^ bit) for i in range(n_case)]
        packs = packs + [lax.ppermute(x, "case", swap) for x in packs]
        order = order + [m ^ bit for m in order]
        bit //= 2
    g = add_over_bus(g, n_bus // 2)
    edge = boundary_columns(order, fault, switch, packs)
    early = par.shape[0] * 2 // 3 // TILE * TILE
    voltage, relay_rate, square, worst = screen_branches(
        g, tie_x[None], fault_z[None], par, fd, edge, early
    )
    bit = 1
    while bit < n_case:
        other = lax.ppermute(worst, "case", [(i, i ^ bit) for i in range(n_case)])
        worst = jnp.maximum(worst, other)
        bit *= 2
    relay_rate = late_relays(square, par, relay_rate, early)
    half_power, factor = curve_constants(curve)
    worst_rate = relay_of_square(worst.reshape(-1), half_power, 1.0 / (factor * tds))
    return (voltage, relay_rate, worst_rate)


def solution(mesh):
    in_specs = (
        P("bus", None),
        P(),
        P("case"),
        P("case", None),
        P("case"),
        P("case"),
        P(),
        P("bus", None),
        P("bus"),
        P("bus"),
        P("bus"),
        P("bus"),
    )
    out_specs = (P("bus", "case"), P("bus", "case"), P("bus"))
    return jax.shard_map(
        per_device, mesh=mesh, in_specs=in_specs, out_specs=out_specs, check_vma=False
    )
```

time: 52.7 us -> 42.8 us (0.81)
  local copies, waits for them, and re-layouts: 6.72 us -> 0.08 us
  Pallas kernels: 19.2 us -> 17.5 us
  starting transfers between devices: 13.2 us -> 14.8 us
  waiting for transfers between devices: 10.2 us -> 8.7 us
  other arithmetic: 2.11 us -> 0.64 us
    ppermute x6 -> x8, starting transfers between devices: 8.32 us -> 14.8 us  [the longest x3 6.62 us: add_over_bus(): return g + lax.ppermute(g, 'bus', [(i, i ^ bit) for i in range(n_bus)])]
    unnamed x26 -> x20, local copies, waits for them, and re-layouts: 6.35 us -> 0.06 us
    all_to_all x1 -> x0, starting transfers between devices: 4.87 us -> none  [per_device(): g_all = lax.all_to_all(g_part, 'bus', 0, 0)]
    pallas_call x3 -> x6, Pallas kernels: 19.2 us -> 17.5 us  [the longest x1 6.62 us: screen_branches(): pl.pallas_call(functools.partial(branch_kernel, early), in_specs=[vmem] *...]
    ppermute x6 -> x8, waiting for transfers between devices: 10.2 us -> 8.7 us  [the longest x3 5.58 us: add_over_bus(): return g + lax.ppermute(g, 'bus', [(i, i ^ bit) for i in range(n_bus)])]
    sub x2 -> x0, other arithmetic: 0.76 us -> none  [the longest x1 0.76 us: per_device(): meta = jnp.concatenate([rim[None], wanted - rim * RIM]).astype(jnp.int32)]
    concatenate x2 -> x0, other arithmetic: 0.6 us -> none  [the longest x1 0.59 us: per_device(): meta = jnp.concatenate([rim[None], wanted - rim * RIM]).astype(jnp.int32)]
  transfers between devices with their start and end apart: 7 -> 8, of which waited for: 4 -> 6; matrix products, arithmetic and copies ran while one was open for 1% -> 0% of each run, Pallas kernels for 14% -> 15%
where the time goes in v2:
time: 42.8 us; the launch traced here: 42.7 us
  Pallas kernels  17.5 us (41%)
  starting transfers between devices  14.8 us (35%)
  waiting for transfers between devices  8.7 us (20%)
  between operations  0.89 us (2%)
  other arithmetic  0.64 us (1%)
    ppermute x3, starting transfers between devices, add_over_bus(): return g + lax.ppermute(g, 'bus', [(i, i ^ bit) for i in range(n_bus)])  6.62 us
    pallas_call x1, Pallas kernels, screen_branches(): pl.pallas_call(functools.partial(branch_kernel, early), in_specs=[vmem] *...  6.62 us
    ppermute x3, waiting for transfers between devices, add_over_bus(): return g + lax.ppermute(g, 'bus', [(i, i ^ bit) for i in range(n_bus)])  5.58 us
    pallas_call x1, Pallas kernels, pick_columns(): pl.pallas_call(columns_kernel, in_specs=[vmem] * 5, out_specs=[vmem, vmem...  5.19 us
    ppermute x1, starting transfers between devices, per_device(): own = lax.ppermute(send, ('bus', 'case'), pairs)  4.86 us
    ppermute x2, waiting for transfers between devices, per_device(): other = lax.ppermute(worst, 'case', [(i, i ^ bit) for i in range(n_case)])  2.9 us
    ppermute x1, starting transfers between devices, per_device(): other = lax.ppermute(own, 'case', [(i, i ^ half) for i in range(n_case)])  2.51 us
    pallas_call x1, Pallas kernels, stage(): pl.pallas_call(functools.partial(stage_kernel, half), in_specs=[hbm] * 4,...  2.29 us
  transfers between devices with their start and end apart: 8, of which 6 were waited for; matrix products, arithmetic and copies ran while one was open for 0% of the time, Pallas kernels for 15%

profile of v2, /device:TPU:0, one launch (start us, length us, event | category | flops | bytes accessed | tf_op | source)
XLA Modules:
  0.0 42.7 jit_solution(17760620605160753055)
XLA Ops:
  0.6 0.0 copy-start
  0.6 0.0 copy-start.2
  0.7 0.0 copy-start.3
  0.7 2.3 %stage.1 = (f32[64,1024]{1,0:T(8,128)S(1)}, f32[1024,1024]{1,0:T(8,128)S(1)}, bf16[1024,1024]{1,0:T(8,128)(2,1)S(1)}) custom-call(f32[1024,1024]{1,0:T(8,128)} %z_hbm.1, s32[8,2,128]{2,1,0:T(2,128)} %lists_hbm.1, s32[1,512]{1,0:T(1,128)} %bitcast.22, s32[2,512]{1,0:T(2,128)} %bitcast.18), custom_call_target="tpu_custom_call" | custom-call | tf_op jit(solution)/shard_map/stage/pallas_call | solution.py:72
  3.0 4.9 %collective-permute-start = (f32[64,1024]{1,0:T(8,128)S(1)}, f32[64,1024]{1,0:T(8,128)S(1)}, u32[]{:S(2)}, u32[]{:S(2)}) collective-permute-start(f32[64,1024]{1,0:T(8,128)S(1)} %get-tuple-element.21), channel_id=1, source_target_pairs={{0,4},{1,5},{4,8},{5,9},{6,2},{7,3},{8,12},{9,13},{10,6},{11,7},{1... | collective-permute-start | bytes 786440 | tf_op jit(solution)/shard_map/ppermute | solution.py:390
  7.8 0.0 copy-done
  7.8 0.0 copy-done.2
  7.8 0.0 copy-done.3
  7.9 0.0 copy-start.8
  7.9 0.0 copy-start.9
  7.9 0.0 copy-start.6
  7.9 0.0 copy-start.7
  7.9 0.0 copy-start.1
  7.9 5.2 %pick_columns.1 = (f32[1024,1024]{1,0:T(8,128)S(1)}, f32[4,512]{1,0:T(4,128)S(1)}) custom-call(f32[1024,1024]{1,0:T(8,128)S(1)} %get-tuple-element.18.z_ref, bf16[1024,1024]{1,0:T(8,128)(2,1)S(1)} %get-tuple-element.19.pick, s32[1,512]{1,0:T(1,128)S(1)} %bitcast.23, s32[2,512]{1,0:T(2,128)S(1)} %bitcast.19, s32[1,1024]{1,0:T(1,128)S(1)} %bitcast.25), custom_call_target="tpu_custom_call" | custom-call | tf_op jit(solution)/shard_map/pick_columns/pallas_call | solution.py:130
  13.1 0.0 copy-start.4
  13.1 0.0 copy-start.5
  13.1 0.2 collective-permute-done.own
  13.4 2.5 %collective-permute-start.3 = (f32[64,1024]{1,0:T(8,128)S(1)}, f32[64,1024]{1,0:T(8,128)S(1)}, u32[]{:S(2)}, u32[]{:S(2)}) collective-permute-start(f32[64,1024]{1,0:T(8,128)S(1)} %collective-permute-done.own), channel_id=1, source_target_pairs={{0,2},{1,3},{2,0},{3,1},{4,6},{5,7},{6,4},{7,5},{8,10},{9,11},{10,... | collective-permute-start | bytes 786440 | tf_op jit(solution)/shard_map/ppermute | solution.py:398
  15.9 2.4 %collective-permute-start.1 = (f32[4,512]{1,0:T(4,128)S(1)}, f32[4,512]{1,0:T(4,128)S(1)}, u32[]{:S(2)}, u32[]{:S(2)}) collective-permute-start(f32[4,512]{1,0:T(4,128)S(1)} %get-tuple-element.22), channel_id=1, source_target_pairs={{0,4},{4,0},{8,12},{12,8},{16,20},{20,16},{24,28},{28,24},{1,5},{5... | collective-permute-start | bytes 24584 | tf_op jit(solution)/shard_map/ppermute | solution.py:396
  18.3 1.6 %collective-permute-done.1 = f32[4,512]{1,0:T(4,128)S(1)} collective-permute-done((f32[4,512]{1,0:T(4,128)S(1)}, f32[4,512]{1,0:T(4,128)S(1)}, u32[]{:S(2)}, u32[]{:S(2)}) %collective-permute-start.1) | collective-permute-done | bytes 8224 | tf_op jit(solution)/shard_map/ppermute | solution.py:396
  19.9 1.6 %collective-permute-start.2 = (f32[4,512]{1,0:T(4,128)S(1)}, f32[4,512]{1,0:T(4,128)S(1)}, u32[]{:S(2)}, u32[]{:S(2)}) collective-permute-start(f32[4,512]{1,0:T(4,128)S(1)} %add.17), channel_id=1, source_target_pairs={{0,8},{4,12},{8,0},{12,4},{16,24},{20,28},{24,16},{28,20},{1,9},{5... | collective-permute-start | bytes 24584 | tf_op jit(solution)/shard_map/ppermute | solution.py:396
  21.5 0.0 copy-done.8
  21.5 0.0 copy-done.9
  21.5 0.0 copy-done.6
  21.5 0.0 copy-done.7
  21.5 2.0 %collective-permute-done.2 = f32[4,512]{1,0:T(4,128)S(1)} collective-permute-done((f32[4,512]{1,0:T(4,128)S(1)}, f32[4,512]{1,0:T(4,128)S(1)}, u32[]{:S(2)}, u32[]{:S(2)}) %collective-permute-start.2) | collective-permute-done | bytes 8224 | tf_op jit(solution)/shard_map/ppermute | solution.py:396
  23.5 0.0 collective-permute-done.3.other
  23.6 0.0 copy-done.1
  23.6 0.3 pack.1
  23.9 0.1 collective-permute-start.5
  24.0 2.7 %collective-permute-start.4 = (f32[4,512]{1,0:T(4,128)S(1)}, f32[4,512]{1,0:T(4,128)S(1)}, u32[]{:S(2)}, u32[]{:S(2)}) collective-permute-start(f32[4,512]{1,0:T(4,128)S(1)} %add.18), channel_id=1, source_target_pairs={{0,16},{4,20},{8,24},{12,28},{16,0},{20,4},{24,8},{28,12},{1,17},{... | collective-permute-start | bytes 24584 | tf_op jit(solution)/shard_map/ppermute | solution.py:396
  26.6 2.0 %collective-permute-done.4 = f32[4,512]{1,0:T(4,128)S(1)} collective-permute-done((f32[4,512]{1,0:T(4,128)S(1)}, f32[4,512]{1,0:T(4,128)S(1)}, u32[]{:S(2)}, u32[]{:S(2)}) %collective-permute-start.4) | collective-permute-done | bytes 8224 | tf_op jit(solution)/shard_map/ppermute | solution.py:396
  28.6 0.0 collective-permute-done.5.refs_1_
  28.6 1.9 %boundary_columns.1.edge_ref = f32[256,1024]{1,0:T(8,128)S(1)} custom-call(s32[1,512]{1,0:T(1,128)S(1)} %bitcast.24, s32[2,512]{1,0:T(2,128)S(1)} %bitcast.20, f32[128,1024]{1,0:T(8,128)S(1)} %get-tuple-element.28.refs_0_, f32[128,1024]{1,0:T(8,128)S(1)} %collective-permute-done.5.refs_1_), custom_call_target="tpu_custom_call" | custom-call | flops 1073741824 | bytes 2097152 | tf_op jit(solution)/shard_map/boundary_columns/pallas_call | solution.py:210
  30.5 0.0 copy-done.4
  30.5 0.0 copy-done.5
  30.5 6.6 %screen_branches.1 = (f32[1024,512]{1,0:T(8,128)}, f32[1536,512]{1,0:T(8,128)}, f32[512,512]{1,0:T(8,128)S(1)}, f32[12,128]{1,0:T(8,128)S(1)}) custom-call(f32[4,512]{1,0:T(4,128)S(1)} %add.19.g_ref, f32[1,512]{1,0:T(1,128)S(1)} %bitcast.26, f32[1,512]{1,0:T(1,128)S(1)} %bitcast.27, f32[1536,8]{1,0:T(8,128)S(1)} %get-tuple-element.26.par_ref, ...), custom_call_target="tpu_custom_call" | custom-call | tf_op jit(solution)/shard_map/screen_branches/pallas_call | solution.py:306
  37.2 0.1 collective-permute-start.6
  37.2 1.2 %collective-permute-done.6 = f32[12,128]{1,0:T(8,128)S(1)} collective-permute-done((f32[12,128]{1,0:T(8,128)S(1)}, f32[12,128]{1,0:T(8,128)S(1)}, u32[]{:S(2)}, u32[]{:S(2)}) %collective-permute-start.6) | collective-permute-done | bytes 6176 | tf_op jit(solution)/shard_map/ppermute | solution.py:422
  38.4 0.7 %collective-permute-start.7 = (f32[12,128]{1,0:T(8,128)S(1)}, f32[12,128]{1,0:T(8,128)S(1)}, u32[]{:S(2)}, u32[]{:S(2)}) collective-permute-start(f32[12,128]{1,0:T(8,128)S(1)} %max.12), channel_id=1, source_target_pairs={{0,2},{1,3},{2,0},{3,1},{4,6},{5,7},{6,4},{7,5},{8,10},{9,11},{10,... | collective-permute-start | bytes 18440 | tf_op jit(solution)/shard_map/ppermute | solution.py:422
  39.1 1.2 %late_relays.1 = f32[1536,512]{1,0:T(8,128)} custom-call(f32[512,512]{1,0:T(8,128)S(1)} %get-tuple-element.30.square_ref, f32[1536,8]{1,0:T(8,128)S(1)} %get-tuple-element.26.par_ref, f32[1536,512]{1,0:T(8,128)} %get-tuple-element.31.relay_in), custom_call_target="tpu_custom_call", output_to_operand_aliasing={{}: (2, {})} | custom-call | flops 2097152 | bytes 2097152 | tf_op jit(solution)/shard_map/late_relays/pallas_call | solution.py:348
  40.3 1.7 %collective-permute-done.7 = f32[12,128]{1,0:T(8,128)S(1)} collective-permute-done((f32[12,128]{1,0:T(8,128)S(1)}, f32[12,128]{1,0:T(8,128)S(1)}, u32[]{:S(2)}, u32[]{:S(2)}) %collective-permute-start.7) | collective-permute-done | bytes 6176 | tf_op jit(solution)/shard_map/ppermute | solution.py:422
  42.1 0.6 %fusion.4 = f32[1536]{0:T(1024)} fusion(f32[1536]{0:T(1024)S(1)} %copy-done.6, f32[12,128]{1,0:T(8,128)S(1)} %max.12, f32[12,128]{1,0:T(8,128)S(1)} %collective-permute-done.7, s32[1536]{0:T(1024)S(1)} %copy-done.7), kind=kLoop, calls=%fused_computation.5 | loop fusion | flops 24576 | bytes 30720 | tf_op jit(solution)/shard_map/mul | solution.py:229
  (8 shorter events, 0.0 us)
Async XLA Ops:
  0.6 7.2 %copy-start = (s32[512,2]{0,1:T(2,128)S(1)}, s32[512,2]{0,1:T(2,128)}, u32[]{:S(2)}) copy-start(s32[512,2]{0,1:T(2,128)} %param.15) | copy-start | bytes 12292
  0.6 7.2 %copy-start.2 = (s32[512]{0:T(512)S(1)}, s32[512]{0:T(512)}, u32[]{:S(2)}) copy-start(s32[512]{0:T(512)} %param.14) | copy-start | bytes 6148
  0.7 7.2 %copy-start.3 = (s32[1024]{0:T(1024)S(1)}, s32[1024]{0:T(1024)}, u32[]{:S(2)}) copy-start(s32[1024]{0:T(1024)} %param.13) | copy-start | bytes 12292
  3.0 10.4 %collective-permute-start = (f32[64,1024]{1,0:T(8,128)S(1)}, f32[64,1024]{1,0:T(8,128)S(1)}, u32[]{:S(2)}, u32[]{:S(2)}) collective-permute-start(f32[64,1024]{1,0:T(8,128)S(1)} %get-tuple-element.21), channel_id=1, source_target_pairs={{0,4},{1,5},{4,8},{5,9},{6,2},{7,3},{8,12},{9,13},{10,6},{11,7},{1... | collective-permute-start | bytes 786440 | tf_op jit(solution)/shard_map/ppermute | solution.py:390
  7.9 13.6 %copy-start.8 = (f32[1536]{0:T(1024)S(1)}, f32[1536]{0:T(1024)}, u32[]{:S(2)}) copy-start(f32[1536]{0:T(1024)} %param.20) | copy-start | bytes 18436
  7.9 13.6 %copy-start.9 = (f32[1536]{0:T(1024)S(1)}, f32[1536]{0:T(1024)}, u32[]{:S(2)}) copy-start(f32[1536]{0:T(1024)} %param.21) | copy-start | bytes 18436
  7.9 13.6 %copy-start.6 = (f32[1536]{0:T(1024)S(1)}, f32[1536]{0:T(1024)}, u32[]{:S(2)}) copy-start(f32[1536]{0:T(1024)} %param.22) | copy-start | bytes 18436
  7.9 13.6 %copy-start.7 = (s32[1536]{0:T(1024)S(1)}, s32[1536]{0:T(1024)}, u32[]{:S(2)}) copy-start(s32[1536]{0:T(1024)} %param.23) | copy-start | bytes 18436
  7.9 15.7 %copy-start.1 = (s32[1536,2]{0,1:T(2,128)S(1)}, s32[1536,2]{0,1:T(2,128)}, u32[]{:S(2)}) copy-start(s32[1536,2]{0,1:T(2,128)} %param.19) | copy-start | bytes 36868
  13.1 17.4 %copy-start.4 = (f32[512]{0:T(512)S(1)}, f32[512]{0:T(512)}, u32[]{:S(2)}) copy-start(f32[512]{0:T(512)} %param.16) | copy-start | bytes 6148
  13.1 17.4 %copy-start.5 = (f32[512]{0:T(512)S(1)}, f32[512]{0:T(512)}, u32[]{:S(2)}) copy-start(f32[512]{0:T(512)} %param.17) | copy-start | bytes 6148
  13.4 10.2 %collective-permute-start.3 = (f32[64,1024]{1,0:T(8,128)S(1)}, f32[64,1024]{1,0:T(8,128)S(1)}, u32[]{:S(2)}, u32[]{:S(2)}) collective-permute-start(f32[64,1024]{1,0:T(8,128)S(1)} %collective-permute-done.own), channel_id=1, source_target_pairs={{0,2},{1,3},{2,0},{3,1},{4,6},{5,7},{6,4},{7,5},{8,10},{9,11},{10,... | collective-permute-start | bytes 786440 | tf_op jit(solution)/shard_map/ppermute | solution.py:398
  15.9 4.0 %collective-permute-start.1 = (f32[4,512]{1,0:T(4,128)S(1)}, f32[4,512]{1,0:T(4,128)S(1)}, u32[]{:S(2)}, u32[]{:S(2)}) collective-permute-start(f32[4,512]{1,0:T(4,128)S(1)} %get-tuple-element.22), channel_id=1, source_target_pairs={{0,4},{4,0},{8,12},{12,8},{16,20},{20,16},{24,28},{28,24},{1,5},{5... | collective-permute-start | bytes 24584 | tf_op jit(solution)/shard_map/ppermute | solution.py:396
  19.9 3.7 %collective-permute-start.2 = (f32[4,512]{1,0:T(4,128)S(1)}, f32[4,512]{1,0:T(4,128)S(1)}, u32[]{:S(2)}, u32[]{:S(2)}) collective-permute-start(f32[4,512]{1,0:T(4,128)S(1)} %add.17), channel_id=1, source_target_pairs={{0,8},{4,12},{8,0},{12,4},{16,24},{20,28},{24,16},{28,20},{1,9},{5... | collective-permute-start | bytes 24584 | tf_op jit(solution)/shard_map/ppermute | solution.py:396
  23.9 4.7 %collective-permute-start.5 = (f32[128,1024]{1,0:T(8,128)S(1)}, f32[128,1024]{1,0:T(8,128)S(1)}, u32[]{:S(2)}, u32[]{:S(2)}) collective-permute-start(f32[128,1024]{1,0:T(8,128)S(1)} %get-tuple-element.28.refs_0_), channel_id=1, source_target_pairs={{0,1},{1,0},{2,3},{3,2},{4,5},{5,4},{6,7},{7,6},{8,9},{9,8},{10,11... | collective-permute-start | bytes 1572872 | tf_op jit(solution)/shard_map/ppermute | solution.py:411
  24.0 4.6 %collective-permute-start.4 = (f32[4,512]{1,0:T(4,128)S(1)}, f32[4,512]{1,0:T(4,128)S(1)}, u32[]{:S(2)}, u32[]{:S(2)}) collective-permute-start(f32[4,512]{1,0:T(4,128)S(1)} %add.18), channel_id=1, source_target_pairs={{0,16},{4,20},{8,24},{12,28},{16,0},{20,4},{24,8},{28,12},{1,17},{... | collective-permute-start | bytes 24584 | tf_op jit(solution)/shard_map/ppermute | solution.py:396
  37.2 1.2 %collective-permute-start.6 = (f32[12,128]{1,0:T(8,128)S(1)}, f32[12,128]{1,0:T(8,128)S(1)}, u32[]{:S(2)}, u32[]{:S(2)}) collective-permute-start(f32[12,128]{1,0:T(8,128)S(1)} %get-tuple-element.32), channel_id=1, source_target_pairs={{0,1},{1,0},{2,3},{3,2},{4,5},{5,4},{6,7},{7,6},{8,9},{9,8},{10,11... | collective-permute-start | bytes 18440 | tf_op jit(solution)/shard_map/ppermute | solution.py:422
  38.4 3.7 %collective-permute-start.7 = (f32[12,128]{1,0:T(8,128)S(1)}, f32[12,128]{1,0:T(8,128)S(1)}, u32[]{:S(2)}, u32[]{:S(2)}) collective-permute-start(f32[12,128]{1,0:T(8,128)S(1)} %max.12), channel_id=1, source_target_pairs={{0,2},{1,3},{2,0},{3,1},{4,6},{5,7},{6,4},{7,5},{8,10},{9,11},{10,... | collective-permute-start | bytes 18440 | tf_op jit(solution)/shard_map/ppermute | solution.py:422

commit v3 on v0

v3 whole, which is shorter than its diff:
```python
import functools

import jax
import jax.numpy as jnp
from jax import lax
from jax.experimental import pallas as pl
from jax.experimental.pallas import tpu as pltpu
from jax.sharding import PartitionSpec as P

TILE = 256
STAGED = 2
F32 = jnp.float32
BF16 = jnp.bfloat16


def split_hi_lo(value):
    hi = value.astype(BF16)
    return hi, (value - hi.astype(F32)).astype(BF16)


def two_pass(hi, lo, rhs):
    return jnp.dot(hi, rhs, preferred_element_type=F32) + jnp.dot(
        lo, rhs, preferred_element_type=F32
    )


def in_hbm(*arrays):
    return [pltpu.with_memory_space_constraint(x, pltpu.HBM) for x in arrays]


def rim_tile(half, tiles):
    return (1 - lax.axis_index("case") // half) * (tiles - 1)


def tile_span(t, tiles):
    return pl.ds(pl.multiple_of(lax.rem(t, tiles) * TILE, TILE), TILE)


def stage_kernel(
    half, z_hbm, lists_hbm, fault_hbm, switch_hbm, send_ref, z_ref, pick_ref, lists, cases, sems
):
    tiles = z_hbm.shape[0] // TILE
    piece = send_ref.shape[0]
    my_bus, my_case = lax.axis_index("bus"), lax.axis_index("case")
    rim = rim_tile(half, tiles)
    loads = [
        pltpu.make_async_copy(fault_hbm, cases.at[pl.ds(0, 1)], sems.at[0]),
        pltpu.make_async_copy(switch_hbm, cases.at[pl.ds(8, 2)], sems.at[1]),
        pltpu.make_async_copy(lists_hbm.at[my_bus], lists, sems.at[2]),
    ]
    for t in range(z_ref.shape[0] // TILE):
        target = z_ref.at[pl.ds(t * TILE, TILE)]
        source = z_hbm.at[tile_span(rim + t, tiles)]
        loads.append(pltpu.make_async_copy(source, target, sems.at[3 + t]))
    for load in loads:
        load.start()
    for load in loads[:2]:
        load.wait()
    fill_picks(cases[0:1, :], cases[8:10, :], pick_ref)
    for load in loads[2:4]:
        load.wait()
    down = my_case // half
    base = (my_case % half) * piece
    first = rim * TILE
    for i in range(piece):
        send_ref[pl.ds(i, 1), :] = z_ref[pl.ds(lists[1 - down, base + i] - first, 1), :]
    for load in loads[4:]:
        load.wait()


def stage(z_columns, boundary_send, fault, switch, n_case):
    cols = z_columns.shape[1]
    half = n_case // 2
    count = fault.shape[1]
    return pl.pallas_call(
        functools.partial(stage_kernel, half),
        in_specs=[pl.BlockSpec(memory_space=pltpu.HBM)] * 4,
        out_specs=[pl.BlockSpec(memory_space=pltpu.VMEM)] * 3,
        out_shape=[
            pltpu.VMEM((boundary_send.shape[2] // half, cols), F32),
            pltpu.VMEM((STAGED * TILE, cols), F32),
            pltpu.VMEM((cols, 2 * count), BF16),
        ],
        scratch_shapes=[
            pltpu.SMEM(boundary_send.shape[1:], jnp.int32),
            pltpu.VMEM((16, count), jnp.int32),
            pltpu.SemaphoreType.DMA((STAGED + 3,)),
        ],
        compiler_params=pltpu.CompilerParams(vmem_limit_bytes=4 * 2**20),
        name="stage",
    )(*in_hbm(z_columns, boundary_send, fault, switch))


def fill_picks(f, ab, pick):
    cols, count = pick.shape[0], f.shape[1]
    a, b = ab[0:1, :], ab[1:2, :]
    for t in range(cols // TILE):
        k = lax.broadcasted_iota(jnp.int32, (TILE, count), 0) + t * TILE
        span = pl.ds(t * TILE, TILE)
        pick[span, :count] = jnp.where(k == f, 1.0, 0.0).astype(BF16)
        pick[span, count:] = jnp.where(k == a, 1.0, jnp.where(k == b, -1.0, 0.0)).astype(BF16)


def columns_kernel(
    half,
    z_ref,
    pick,
    fault_ref,
    switch_ref,
    resident_ref,
    z_hbm,
    ends_hbm,
    x_hbm,
    pickup_hbm,
    tds_hbm,
    curve_hbm,
    fd_ref,
    g_ref,
    par_ref,
    fd_hi,
    fd_lo,
    later,
    ends,
    floats,
    curves,
    sems,
):
    rows, cols = z_hbm.shape
    cases = fault_ref.shape[1]
    tiles = rows // TILE
    rim = rim_tile(half, tiles)
    loads = []
    for t in range(STAGED, tiles):
        target = later.at[pl.ds((t - STAGED) * TILE, TILE)]
        source = z_hbm.at[tile_span(rim + t, tiles)]
        loads.append(pltpu.make_async_copy(source, target, sems.at[t]))
    small = [
        pltpu.make_async_copy(source, target, sems.at[tiles + i])
        for i, (source, target) in enumerate(
            [
                (ends_hbm, ends),
                (x_hbm, floats.at[0]),
                (pickup_hbm, floats.at[1]),
                (tds_hbm, floats.at[2]),
                (curve_hbm, curves),
            ]
        )
    ]
    for load in loads + small:
        load.start()
    f, a, b = fault_ref[...], switch_ref[0:1, :], switch_ref[1:2, :]
    resident = resident_ref[...] - lax.axis_index("bus") * rows
    g1 = jnp.zeros((1, cases), F32)
    g2 = jnp.zeros((1, cases), F32)
    g3 = jnp.zeros((1, cases), F32)
    k = lax.broadcasted_iota(jnp.int32, (TILE, cols), 1)
    for t in range(tiles + 1):
        if t == STAGED:
            for load in loads + small:
                load.wait()
        if t < tiles:
            if t < STAGED:
                z = z_ref[pl.ds(t * TILE, TILE), :]
            else:
                z = later[pl.ds((t - STAGED) * TILE, TILE), :]
            hi, lo = split_hi_lo(z)
            fd_ref[pl.ds(t * TILE, TILE), :] = two_pass(hi, lo, pick[...])
        if t == STAGED:
            gain = 1.0 / (floats[0] * floats[1])
            half_power, factor = curve_constants(curves[...])
            rate = 1.0 / (factor * floats[2])
            for c in range(gain.shape[0]):
                line = pl.ds(c * 128, 128)
                lines = [ends[:, line].astype(F32)]
                lines += [x[c : c + 1] for x in (gain, half_power, rate)]
                par_ref[line, :] = jnp.concatenate(lines + [jnp.zeros((3, 128), F32)]).T
        if t > 0:
            span = pl.ds((t - 1) * TILE, TILE)
            first = tile_span(rim + t - 1, tiles).start
            row = lax.broadcasted_iota(jnp.int32, (TILE, cols), 0) + first
            owner = jnp.max(jnp.where(row == resident, k, -1), axis=1, keepdims=True)
            fd_hi[span, :], fd_lo[span, :] = split_hi_lo(fd_ref[span, :])
            fault, diff = fd_ref[span, :cases], fd_ref[span, cases:]
            at_f = owner == f
            g3 += jnp.sum(jnp.where(at_f, fault, 0.0), axis=0, keepdims=True)
            g2 += jnp.sum(jnp.where(at_f, diff, 0.0), axis=0, keepdims=True)
            g1 += jnp.sum(
                jnp.where(owner == a, diff, jnp.where(owner == b, -diff, 0.0)),
                axis=0,
                keepdims=True,
            )
    g_ref[...] = jnp.concatenate([g1, g2, g3, jnp.zeros((g_ref.shape[0] - 3, cases), F32)])


def pick_columns(z, pick, fault, switch, resident, z_columns, ends, values, curve, n_case):
    rows, cols = z_columns.shape
    count = fault.shape[1]
    lines = curve.shape[0]
    vmem = pl.BlockSpec(memory_space=pltpu.VMEM)
    return pl.pallas_call(
        functools.partial(columns_kernel, n_case // 2),
        in_specs=[vmem] * 5 + [pl.BlockSpec(memory_space=pltpu.HBM)] * 6,
        out_specs=[vmem] * 5,
        out_shape=[
            pltpu.VMEM((rows, 2 * count), F32),
            pltpu.VMEM((4, count), F32),
            pltpu.VMEM((lines * 128, 8), F32),
            pltpu.VMEM((rows, 2 * count), BF16),
            pltpu.VMEM((rows, 2 * count), BF16),
        ],
        scratch_shapes=[
            pltpu.VMEM((rows - STAGED * TILE, cols), F32),
            pltpu.VMEM(ends.shape, jnp.int32),
            pltpu.VMEM((3, lines, 128), F32),
            pltpu.VMEM((lines, 128), jnp.int32),
            pltpu.SemaphoreType.DMA((rows // TILE + 5,)),
        ],
        compiler_params=pltpu.CompilerParams(vmem_limit_bytes=20 * 2**20),
        name="pick_columns",
    )(z, pick, fault, switch, resident, *in_hbm(z_columns, ends, *values, curve))


def curve_constants(curve):
    half_power = jnp.where(curve == 0, 0.01, jnp.where(curve == 1, 0.5, 1.0)).astype(F32)
    factor = jnp.where(curve == 0, 0.14, jnp.where(curve == 1, 13.5, 80.0)).astype(F32)
    return half_power, factor


def incidence(bus, par):
    return jnp.where(bus == par[:, 1:2], 1.0, jnp.where(bus == par[:, 0:1], -1.0, 0.0)).astype(BF16)


def advance_kernel(half, start, fd_hi, fd_lo, par_ref, out_ref):
    rows = fd_hi.shape[0]
    count = out_ref.shape[0]
    bus = lax.broadcasted_iota(jnp.int32, (count, rows), 1)
    bus = bus + rim_tile(half, rows // TILE) * TILE
    bus = jnp.where(bus >= rows, bus - rows, bus).astype(F32)
    ends = incidence(bus, par_ref[pl.ds(start, count), :])
    out_ref[...] = jnp.dot(ends, fd_hi[...], preferred_element_type=F32) + jnp.dot(
        ends, fd_lo[...], preferred_element_type=F32
    )


def advance(fd_parts, par, start, count, n_case):
    rows, width = fd_parts[0].shape
    vmem = pl.BlockSpec(memory_space=pltpu.VMEM)
    return pl.pallas_call(
        functools.partial(advance_kernel, n_case // 2, start),
        in_specs=[vmem] * 3,
        out_specs=vmem,
        out_shape=pltpu.VMEM((count, width), F32),
        compiler_params=pltpu.CompilerParams(vmem_limit_bytes=8 * 2**20),
        cost_estimate=pl.CostEstimate(
            flops=4 * count * rows * width, bytes_accessed=8 * count * width, transcendentals=0
        ),
        name="advance",
    )(*fd_parts, par)


def boundary_kernel(order, pick, *refs):
    pieces = refs[: len(order)]
    out_ref, hi, lo = refs[len(order) :]
    my_case = lax.axis_index("case")
    for mask, piece in zip(order, pieces):
        size = piece.shape[0]
        span = pl.ds(pl.multiple_of((my_case ^ mask) * size, size), size)
        hi[span, :], lo[span, :] = split_hi_lo(piece[...])
    out_ref[...] = two_pass(hi[...], lo[...], pick[...])


def boundary_columns(order, pick, pieces):
    cols, width = pick.shape
    total = sum(piece.shape[0] for piece in pieces)
    vmem = pl.BlockSpec(memory_space=pltpu.VMEM)
    return pl.pallas_call(
        functools.partial(boundary_kernel, order),
        in_specs=[vmem] * (1 + len(pieces)),
        out_specs=vmem,
        out_shape=pltpu.VMEM((total, width), F32),
        scratch_shapes=[pltpu.VMEM((total, cols), BF16)] * 2,
        compiler_params=pltpu.CompilerParams(vmem_limit_bytes=8 * 2**20),
        cost_estimate=pl.CostEstimate(
            flops=4 * total * cols * width, bytes_accessed=8 * total * cols, transcendentals=0
        ),
        name="boundary_columns",
    )(pick, *pieces)


def relay_of_square(square, power, rate):
    return jnp.maximum(jnp.exp2(power * jnp.log2(square + 1e-4)) - 1.0, 0.0) * rate


def branch_kernel(half, n_ahead, g_ref, far_ref, tie_ref, fault_ref, par_ref, fd_ref, edge_ref, *refs):
    ahead = refs[:n_ahead]
    volt_hbm, relay_hbm, square_ref, worst_ref, vbuf, rbuf, uh, ul, vsem, rsem = refs[n_ahead:]
    rows, cases = vbuf.shape
    branches = par_ref.shape[0]
    early = square_ref.shape[0]
    ext = uh.shape[0]
    g = g_ref[...] + far_ref[...]
    g1, g2, g3 = g[0:1], g[1:2], g[2:3]
    ratio = g2 / (tie_ref[...] + g1)
    amps = 1.0 / (g3 - g2 * ratio + fault_ref[...])

    def sag_of(fd):
        return (fd[:, :cases] - fd[:, cases:] * ratio) * amps

    edge = pl.ds(rows, ext - rows)
    uh[edge, :], ul[edge, :] = split_hi_lo(sag_of(edge_ref[...]))
    tiles = rows // TILE
    rim = rim_tile(half, tiles)
    for t in range(tiles):
        span = tile_span(rim + t, tiles)
        sag = sag_of(fd_ref[pl.ds(t * TILE, TILE), :])
        vbuf[span, :] = 1.0 - sag
        uh[span, :], ul[span, :] = split_hi_lo(sag)
    copies = [pltpu.make_async_copy(vbuf, volt_hbm, vsem)]
    copies[0].start()

    def drops(par, first):
        count = par.shape[0]
        bus = lax.broadcasted_iota(jnp.int32, (count, ext - first), 1) + first
        ends = incidence(bus.astype(F32), par)
        span = pl.ds(first, ext - first)
        return jnp.dot(ends, uh[span, :], preferred_element_type=F32) + jnp.dot(
            ends, ul[span, :], preferred_element_type=F32
        )

    def square_of(drop, par, start):
        scaled = drop * par[:, 2:3]
        square = scaled * scaled
        largest = square[:, :128]
        for c in range(128, cases, 128):
            largest = jnp.maximum(largest, square[:, c : c + 128])
        for h in range(par.shape[0] // 128):
            worst_ref[pl.ds(start // 128 + h, 1), :] = jnp.max(
                largest[h * 128 : (h + 1) * 128, :].T, axis=0, keepdims=True
            )
        return square

    start = 0
    ready = []
    for part in ahead:
        ready.append((part, start))
        start += part.shape[0]
    for t in range((branches - early) // TILE):
        start = early + t * TILE
        par = par_ref[pl.ds(start, TILE), :]
        square = square_of(drops(par, 0), par, start)
        span = pl.ds(t * TILE, TILE)
        rbuf[span, :] = relay_of_square(square, par[:, 3:4], par[:, 4:5])
        if t < len(ready):
            part, start = ready[t]
            count = part.shape[0]
            par = par_ref[pl.ds(start, count), :]
            drop = sag_of(part[...]) + drops(par, rows)
            square_ref[pl.ds(start, count), :] = square_of(drop, par, start)
        target = relay_hbm.at[pl.ds(early + t * TILE, TILE)]
        copies.append(pltpu.make_async_copy(rbuf.at[span], target, rsem.at[t]))
        copies[-1].start()
    for copy in copies:
        copy.wait()


def screen_branches(g, g_far, tie_x, fault_z, par, fd, edge, ahead, n_case):
    count = tie_x.shape[1]
    rows = fd.shape[0]
    branches = par.shape[0]
    early = sum(part.shape[0] for part in ahead)
    ext = rows + edge.shape[0]
    vmem = pl.BlockSpec(memory_space=pltpu.VMEM)
    hbm = pl.BlockSpec(memory_space=pltpu.HBM)
    return pl.pallas_call(
        functools.partial(branch_kernel, n_case // 2, len(ahead)),
        in_specs=[vmem] * (7 + len(ahead)),
        out_specs=[hbm, hbm, vmem, vmem],
        out_shape=[
            jax.ShapeDtypeStruct((rows, count), F32),
            jax.ShapeDtypeStruct((branches, count), F32),
            pltpu.VMEM((early, count), F32),
            pltpu.VMEM((branches // 128, 128), F32),
        ],
        scratch_shapes=[
            pltpu.VMEM((rows, count), F32),
            pltpu.VMEM((branches - early, count), F32),
            pltpu.VMEM((ext, count), BF16),
            pltpu.VMEM((ext, count), BF16),
            pltpu.SemaphoreType.DMA,
            pltpu.SemaphoreType.DMA((branches // TILE,)),
        ],
        compiler_params=pltpu.CompilerParams(vmem_limit_bytes=24 * 2**20),
        name="screen_branches",
    )(g, g_far, tie_x, fault_z, par, fd, edge, *ahead)


def late_kernel(square_ref, par_ref, relay_in, relay_hbm, rbuf, sems):
    copies = []
    for t in range(square_ref.shape[0] // TILE):
        span = pl.ds(t * TILE, TILE)
        par = par_ref[span, :]
        rbuf[span, :] = relay_of_square(square_ref[span, :], par[:, 3:4], par[:, 4:5])
        copies.append(pltpu.make_async_copy(rbuf.at[span], relay_hbm.at[span], sems.at[t]))
        copies[-1].start()
    for copy in copies:
        copy.wait()


def late_relays(square, par, relay_rate):
    vmem = pl.BlockSpec(memory_space=pltpu.VMEM)
    hbm = pl.BlockSpec(memory_space=pltpu.HBM)
    return pl.pallas_call(
        late_kernel,
        in_specs=[vmem, vmem, hbm],
        out_specs=hbm,
        out_shape=jax.ShapeDtypeStruct(relay_rate.shape, F32),
        input_output_aliases={2: 0},
        scratch_shapes=[
            pltpu.VMEM(square.shape, F32),
            pltpu.SemaphoreType.DMA((square.shape[0] // TILE,)),
        ],
        compiler_params=pltpu.CompilerParams(vmem_limit_bytes=8 * 2**20),
        cost_estimate=pl.CostEstimate(
            flops=8 * square.size, bytes_accessed=8 * square.size, transcendentals=2 * square.size
        ),
        name="late_relays",
    )(square, par, relay_rate)


def per_device(
    z_columns,
    resident_bus,
    fault_col,
    switch_cols,
    tie_x,
    fault_z,
    boundary_send,
    branch_ends,
    branch_x,
    pickup,
    tds,
    curve,
):
    n_bus, n_case = lax.axis_size("bus"), lax.axis_size("case")
    half = n_case // 2
    fault, switch = fault_col[None], switch_cols.T
    send, z, pick = stage(z_columns, boundary_send, fault, switch, n_case)
    pairs = []
    for s in range(n_bus):
        for c in range(n_case):
            to = s + 1 if c < half else s - 1
            if 0 <= to < n_bus:
                pairs.append((s * n_case + c, to * n_case + c))
    own = lax.ppermute(send, ("bus", "case"), pairs)

    by_lines = [x.reshape(-1, 128) for x in (branch_x, pickup, tds, curve)]
    fd, g, par, *fd_parts = pick_columns(
        z,
        pick,
        fault,
        switch,
        resident_bus[None],
        z_columns,
        branch_ends.T,
        by_lines[:3],
        by_lines[3],
        n_case,
    )

    def swap_over_bus(g, bit):
        return lax.ppermute(g, "bus", [(i, i ^ bit) for i in range(n_bus)])

    def after(first, *values):
        return lax.optimization_barrier((first, *values))[1:]

    (own,) = after(g, own)
    other = lax.ppermute(own, "case", [(i, i ^ half) for i in range(n_case)])
    ahead = []
    part = par.shape[0] // 4
    bit = 1
    while bit < n_bus // 2:
        far = swap_over_bus(g, bit)
        if len(ahead) < 2:
            ahead.append(advance(fd_parts, par, len(ahead) * part, part, n_case))
            (far,) = after(ahead[-1], far)
        g = g + far
        bit *= 2
    g_far = swap_over_bus(g, n_bus // 2)
    pieces, order = list(after(g, own, other)), [0, half]
    bit = half // 2
    while bit:
        swap = [(i, i ^ bit) for i in range(n_case)]
        pieces = pieces + [lax.ppermute(x, "case", swap) for x in pieces]
        order = order + [m ^ bit for m in order]
        bit //= 2
    edge = boundary_columns(order, pick, pieces)
    voltage, relay_rate, square, worst = screen_branches(
        g, g_far, tie_x[None], fault_z[None], par, fd, edge, ahead, n_case
    )
    others = [
        lax.ppermute(worst, "case", [(i, i ^ m) for i in range(n_case)])
        for m in range(n_case - 1, 0, -1)
    ]
    relay_rate = late_relays(square, par, relay_rate)
    half_power, factor = curve_constants(curve)
    worst = functools.reduce(jnp.maximum, others, worst).reshape(-1)
    worst_rate = relay_of_square(worst, half_power, 1.0 / (factor * tds))
    return (voltage, relay_rate, worst_rate)


def solution(mesh):
    in_specs = (
        P("bus", None),
        P(),
        P("case"),
        P("case", None),
        P("case"),
        P("case"),
        P(),
        P("bus", None),
        P("bus"),
        P("bus"),
        P("bus"),
        P("bus"),
    )
    out_specs = (P("bus", "case"), P("bus", "case"), P("bus"))
    return jax.shard_map(
        per_device, mesh=mesh, in_specs=in_specs, out_specs=out_specs, check_vma=False
    )
```

time: 104 us -> 37.4 us (0.36)
  local copies, waits for them, and re-layouts: 46.5 us -> 0.03 us
  blocking collectives: 29.7 us -> 0 us
  Pallas kernels: 0 us -> 19.7 us
  other arithmetic: 17.1 us -> 0.64 us
  starting transfers between devices: 2.6 us -> 13.6 us
  waiting for transfers between devices: 6.77 us -> 2.36 us
    gather x12 -> x0, local copies, waits for them, and re-layouts: 36.2 us -> none  [the longest x1 5.8 us: per_device(): jnp.take(z_columns, switch_cols[:, 1], axis=1)]
    psum x1 -> x0, blocking collectives: 23.4 us -> none  [per_device(): entry_sums = lax.psum(partial_value, 'bus')]
    pallas_call x0 -> x7, Pallas kernels: none -> 19.7 us  [the longest x1 6.56 us: pick_columns(): pl.pallas_call(functools.partial(columns_kernel, n_case // 2), in_specs=[...]
    ppermute x2 -> x10, starting transfers between devices: 2.6 us -> 13.6 us  [the longest x3 5.84 us: swap_over_bus(): return lax.ppermute(g, 'bus', [(i, i ^ bit) for i in range(n_bus)])]
    unnamed x24 -> x14, local copies, waits for them, and re-layouts: 7.35 us -> 0.03 us
    pmax x1 -> x0, blocking collectives: 6.31 us -> none  [per_device(): worst_rate = lax.pmax(jnp.max(relay_rate, axis=1), 'case')]
    reduce_max x1 -> x0, other arithmetic: 5.89 us -> none  [per_device(): worst_rate = lax.pmax(jnp.max(relay_rate, axis=1), 'case')]
    ppermute x2 -> x10, waiting for transfers between devices: 6.77 us -> 2.36 us  [the longest x1 1.32 us: per_device(): other = lax.ppermute(own, 'case', [(i, i ^ half) for i in range(n_case)])]
  transfers between devices with their start and end apart: 2 -> 10, of which waited for: 2 -> 4; matrix products, arithmetic and copies ran while one was open for 1% -> 0% of each run, Pallas kernels for 0% -> 36%
where the time goes in v3:
time: 37.4 us; the launch traced here: 37.2 us
  Pallas kernels  19.7 us (53%)
  starting transfers between devices  13.6 us (36%)
  waiting for transfers between devices  2.36 us (6%)
  between operations  0.79 us (2%)
  other arithmetic  0.64 us (2%)
    pallas_call x1, Pallas kernels, pick_columns(): pl.pallas_call(functools.partial(columns_kernel, n_case // 2), in_specs=[...  6.56 us
    ppermute x3, starting transfers between devices, swap_over_bus(): return lax.ppermute(g, 'bus', [(i, i ^ bit) for i in range(n_bus)])  5.84 us
    ppermute x1, starting transfers between devices, per_device(): own = lax.ppermute(send, ('bus', 'case'), pairs)  4.86 us
    pallas_call x1, Pallas kernels, screen_branches(): pl.pallas_call(functools.partial(branch_kernel, n_case // 2, len(ahead)),...  4.8 us
    pallas_call x2, Pallas kernels, advance(): pl.pallas_call(functools.partial(advance_kernel, n_case // 2, start), in_...  3.79 us
    ppermute x3, starting transfers between devices, per_device(): lax.ppermute(worst, 'case', [(i, i ^ m) for i in range(n_case)])  1.93 us
    pallas_call x1, Pallas kernels, stage(): pl.pallas_call(functools.partial(stage_kernel, half), in_specs=[pl.BlockS...  1.63 us
    pallas_call x1, Pallas kernels, late_relays(): pl.pallas_call(late_kernel, in_specs=[vmem, vmem, hbm], out_specs=hbm, ou...  1.51 us
  transfers between devices with their start and end apart: 10, of which 4 were waited for; matrix products, arithmetic and copies ran while one was open for 0% of the time, Pallas kernels for 36%

profile of v3, /device:TPU:0, one launch (start us, length us, event | category | flops | bytes accessed | tf_op | source)
XLA Modules:
  0.0 37.2 jit_solution(10215682760503807060)
XLA Ops:
  0.6 0.0 copy-start
  0.6 0.0 copy-start.1
  0.7 0.0 copy-start.2
  0.7 1.6 %stage.1 = (f32[64,1024]{1,0:T(8,128)S(1)}, f32[512,1024]{1,0:T(8,128)S(1)}, bf16[1024,1024]{1,0:T(8,128)(2,1)S(1)}) custom-call(f32[1024,1024]{1,0:T(8,128)} %z_hbm.3, s32[8,2,128]{2,1,0:T(2,128)} %lists_hbm.1, s32[1,512]{1,0:T(1,128)} %bitcast.24, s32[2,512]{1,0:T(2,128)} %bitcast.22), custom_call_target="tpu_custom_call" | custom-call | tf_op jit(solution)/shard_map/stage/pallas_call | solution.py:75
  2.3 4.9 %collective-permute-start.3 = (f32[64,1024]{1,0:T(8,128)S(1)}, f32[64,1024]{1,0:T(8,128)S(1)}, u32[]{:S(2)}, u32[]{:S(2)}) collective-permute-start(f32[64,1024]{1,0:T(8,128)S(1)} %get-tuple-element.29), channel_id=1, source_target_pairs={{0,4},{1,5},{4,8},{5,9},{6,2},{7,3},{8,12},{9,13},{10,6},{11,7},{1... | collective-permute-start | bytes 786440 | tf_op jit(solution)/shard_map/ppermute | solution.py:454
  7.2 0.0 copy-done
  7.2 0.0 copy-done.1
  7.2 0.0 copy-done.2
  7.2 6.6 %pick_columns.1 = (f32[1024,1024]{1,0:T(8,128)S(1)}, f32[4,512]{1,0:T(4,128)S(1)}, f32[1536,8]{1,0:T(8,128)S(1)}, bf16[1024,1024]{1,0:T(8,128)(2,1)S(1)}, bf16[1024,1024]{1,0:T(8,128)(2,1)S(1)}) custom-call(f32[512,1024]{1,0:T(8,128)S(1)} %get-tuple-element.20.z_ref, bf16[1024,1024]{1,0:T(8,128)(2,1)S(1)} %get-tuple-element.21.pick, s32[1,512]{1,0:T(1,128)S(1)} %bitcast.25, ...), custom_call_target="tpu_custom_call" | custom-call | tf_op jit(solution)/shard_map/pick_columns/pallas_call | solution.py:200
  13.8 1.6 %collective-permute-start = (f32[4,512]{1,0:T(4,128)S(1)}, f32[4,512]{1,0:T(4,128)S(1)}, u32[]{:S(2)}, u32[]{:S(2)}) collective-permute-start(f32[4,512]{1,0:T(4,128)S(1)} %get-tuple-element.22), channel_id=1, source_target_pairs={{0,4},{4,0},{8,12},{12,8},{16,20},{20,16},{24,28},{28,24},{1,5},{5... | collective-permute-start | bytes 24584 | tf_op jit(solution)/shard_map/ppermute | solution.py:471
  15.4 0.0 collective-permute-done.3.refs_0_
  15.4 0.5 %collective-permute-start.4 = (f32[64,1024]{1,0:T(8,128)S(1)}, f32[64,1024]{1,0:T(8,128)S(1)}, u32[]{:S(2)}, u32[]{:S(2)}) collective-permute-start(f32[64,1024]{1,0:T(8,128)S(1)} %collective-permute-done.3.refs_0_), channel_id=1, source_target_pairs={{0,2},{1,3},{2,0},{3,1},{4,6},{5,7},{6,4},{7,5},{8,10},{9,11},{10,... | collective-permute-start | bytes 786440 | tf_op jit(solution)/shard_map/ppermute | solution.py:477
  15.9 1.9 %advance.2.refs_0_ = f32[384,1024]{1,0:T(8,128)S(1)} custom-call(bf16[1024,1024]{1,0:T(8,128)(2,1)S(1)} %get-tuple-element.23.fd_hi, bf16[1024,1024]{1,0:T(8,128)(2,1)S(1)} %get-tuple-element.24.fd_lo, f32[1536,8]{1,0:T(8,128)S(1)} %get-tuple-element.25.par_ref), custom_call_target="tpu_custom_call" | custom-call | flops 1610612736 | bytes 3145728 | tf_op jit(solution)/shard_map/advance/pallas_call | solution.py:248
  17.8 0.0 collective-permute-done
  17.8 1.6 %collective-permute-start.1 = (f32[4,512]{1,0:T(4,128)S(1)}, f32[4,512]{1,0:T(4,128)S(1)}, u32[]{:S(2)}, u32[]{:S(2)}) collective-permute-start(f32[4,512]{1,0:T(4,128)S(1)} %add.14), channel_id=1, source_target_pairs={{0,8},{4,12},{8,0},{12,4},{16,24},{20,28},{24,16},{28,20},{1,9},{5... | collective-permute-start | bytes 24584 | tf_op jit(solution)/shard_map/ppermute | solution.py:471
  19.5 1.9 %advance.3.refs_1_ = f32[384,1024]{1,0:T(8,128)S(1)} custom-call(bf16[1024,1024]{1,0:T(8,128)(2,1)S(1)} %get-tuple-element.23.fd_hi, bf16[1024,1024]{1,0:T(8,128)(2,1)S(1)} %get-tuple-element.24.fd_lo, f32[1536,8]{1,0:T(8,128)S(1)} %get-tuple-element.25.par_ref), custom_call_target="tpu_custom_call" | custom-call | flops 1610612736 | bytes 3145728 | tf_op jit(solution)/shard_map/advance/pallas_call | solution.py:248
  21.4 0.2 collective-permute-done.1
  21.5 0.0 copy-start.3
  21.5 0.0 copy-start.4
  21.5 1.3 %collective-permute-done.4.refs_1_ = f32[64,1024]{1,0:T(8,128)S(1)} collective-permute-done((f32[64,1024]{1,0:T(8,128)S(1)}, f32[64,1024]{1,0:T(8,128)S(1)}, u32[]{:S(2)}, u32[]{:S(2)}) %collective-permute-start.4) | collective-permute-done | bytes 262176 | tf_op jit(solution)/shard_map/ppermute | solution.py:477
  22.9 0.0 collective-permute-start.5
  22.9 0.5 %collective-permute-start.6 = (f32[64,1024]{1,0:T(8,128)S(1)}, f32[64,1024]{1,0:T(8,128)S(1)}, u32[]{:S(2)}, u32[]{:S(2)}) collective-permute-start(f32[64,1024]{1,0:T(8,128)S(1)} %collective-permute-done.4.refs_1_), channel_id=1, source_target_pairs={{0,1},{1,0},{2,3},{3,2},{4,5},{5,4},{6,7},{7,6},{8,9},{9,8},{10,11... | collective-permute-start | bytes 786440 | tf_op jit(solution)/shard_map/ppermute | solution.py:493
  23.4 2.6 %collective-permute-start.2 = (f32[4,512]{1,0:T(4,128)S(1)}, f32[4,512]{1,0:T(4,128)S(1)}, u32[]{:S(2)}, u32[]{:S(2)}) collective-permute-start(f32[4,512]{1,0:T(4,128)S(1)} %add.15.g_ref), channel_id=1, source_target_pairs={{0,16},{4,20},{8,24},{12,28},{16,0},{20,4},{24,8},{28,12},{1,17},{... | collective-permute-start | bytes 24584 | tf_op jit(solution)/shard_map/ppermute | solution.py:471
  26.0 0.0 collective-permute-done.5.refs_2_
  26.0 0.0 collective-permute-done.6.refs_3_
  26.0 1.4 %boundary_columns.1.edge_ref = f32[256,1024]{1,0:T(8,128)S(1)} custom-call(bf16[1024,1024]{1,0:T(8,128)(2,1)S(1)} %get-tuple-element.21.pick, f32[64,1024]{1,0:T(8,128)S(1)} %collective-permute-done.3.refs_0_, f32[64,1024]{1,0:T(8,128)S(1)} %collective-permute-done.4.refs_1_, f32[64,1024]{1,0:T(8,128)S(1)} %collective-permute-done.5.refs_2_, ...), custom_call_target="tpu_custom_call" | custom-call | flops 1073741824 | bytes 2097152 | tf_op jit(solution)/shard_map/boundary_columns/pallas_call | solution.py:276
  27.4 0.5 %collective-permute-done.2.far_ref = f32[4,512]{1,0:T(4,128)S(1)} collective-permute-done((f32[4,512]{1,0:T(4,128)S(1)}, f32[4,512]{1,0:T(4,128)S(1)}, u32[]{:S(2)}, u32[]{:S(2)}) %collective-permute-start.2) | collective-permute-done | bytes 8224 | tf_op jit(solution)/shard_map/ppermute | solution.py:471
  27.9 0.0 copy-done.3
  27.9 0.0 copy-done.4
  27.9 4.8 %screen_branches.1 = (f32[1024,512]{1,0:T(8,128)}, f32[1536,512]{1,0:T(8,128)}, f32[768,512]{1,0:T(8,128)S(1)}, f32[12,128]{1,0:T(8,128)S(1)}) custom-call(f32[4,512]{1,0:T(4,128)S(1)} %add.15.g_ref, f32[4,512]{1,0:T(4,128)S(1)} %collective-permute-done.2.far_ref, f32[1,512]{1,0:T(1,128)S(1)} %bitcast.27, f32[1,512]{1,0:T(1,128)S(1)} %bitcast.28, ...), custom_call_target="tpu_custom_call" | custom-call | tf_op jit(solution)/shard_map/screen_branches/pallas_call | solution.py:374
  32.8 0.1 collective-permute-start.9
  32.8 0.6 %collective-permute-start.8 = (f32[12,128]{1,0:T(8,128)S(1)}, f32[12,128]{1,0:T(8,128)S(1)}, u32[]{:S(2)}, u32[]{:S(2)}) collective-permute-start(f32[12,128]{1,0:T(8,128)S(1)} %get-tuple-element.36), channel_id=1, source_target_pairs={{0,2},{1,3},{2,0},{3,1},{4,6},{5,7},{6,4},{7,5},{8,10},{9,11},{10,... | collective-permute-start | bytes 18440 | tf_op jit(solution)/shard_map/ppermute | solution.py:501
  33.4 1.3 %collective-permute-start.7 = (f32[12,128]{1,0:T(8,128)S(1)}, f32[12,128]{1,0:T(8,128)S(1)}, u32[]{:S(2)}, u32[]{:S(2)}) collective-permute-start(f32[12,128]{1,0:T(8,128)S(1)} %get-tuple-element.36), channel_id=1, source_target_pairs={{0,3},{1,2},{2,1},{3,0},{4,7},{5,6},{6,5},{7,4},{8,11},{9,10},{10,... | collective-permute-start | bytes 18440 | tf_op jit(solution)/shard_map/ppermute | solution.py:501
  34.7 0.0 copy-start.5
  34.7 0.0 copy-start.6
  34.7 1.5 %late_relays.1 = f32[1536,512]{1,0:T(8,128)} custom-call(f32[768,512]{1,0:T(8,128)S(1)} %get-tuple-element.34.square_ref, f32[1536,8]{1,0:T(8,128)S(1)} %get-tuple-element.25.par_ref, f32[1536,512]{1,0:T(8,128)} %get-tuple-element.35.relay_in), custom_call_target="tpu_custom_call", output_to_operand_aliasing={{}: (2, {})} | custom-call | flops 3145728 | bytes 3145728 | tf_op jit(solution)/shard_map/late_relays/pallas_call | solution.py:412
  36.2 0.0 collective-permute-done.9
  36.2 0.3 collective-permute-done.8
  36.6 0.0 collective-permute-done.7
  36.6 0.0 copy-done.5
  36.6 0.0 copy-done.6
  36.6 0.6 %fusion.4 = f32[1536]{0:T(1024)} fusion(f32[1536]{0:T(1024)S(1)} %copy-done.5, f32[12,128]{1,0:T(8,128)S(1)} %collective-permute-done.9, f32[12,128]{1,0:T(8,128)S(1)} %collective-permute-done.8, f32[12,128]{1,0:T(8,128)S(1)} %get-tuple-element.36, f32[12,128]{1,0:T(8,128)S(1)} %collective-permute-done.7, s32[1536]{0:T(1024)S(1)} %copy-done.6), kind=kLoop, calls=%fused_computation.5 | loop fusion | flops 27648 | bytes 43008 | tf_op jit(solution)/shard_map/mul | solution.py:291
  (2 shorter events, 0.0 us)
Async XLA Ops:
  0.6 6.5 %copy-start = (s32[512,2]{0,1:T(2,128)S(1)}, s32[512,2]{0,1:T(2,128)}, u32[]{:S(2)}) copy-start(s32[512,2]{0,1:T(2,128)} %param.15) | copy-start | bytes 12292
  0.6 6.5 %copy-start.1 = (s32[512]{0:T(512)S(1)}, s32[512]{0:T(512)}, u32[]{:S(2)}) copy-start(s32[512]{0:T(512)} %param.14) | copy-start | bytes 6148
  0.7 6.5 %copy-start.2 = (s32[1024]{0:T(1024)S(1)}, s32[1024]{0:T(1024)}, u32[]{:S(2)}) copy-start(s32[1024]{0:T(1024)} %param.13) | copy-start | bytes 12292
  2.3 13.1 %collective-permute-start.3 = (f32[64,1024]{1,0:T(8,128)S(1)}, f32[64,1024]{1,0:T(8,128)S(1)}, u32[]{:S(2)}, u32[]{:S(2)}) collective-permute-start(f32[64,1024]{1,0:T(8,128)S(1)} %get-tuple-element.29), channel_id=1, source_target_pairs={{0,4},{1,5},{4,8},{5,9},{6,2},{7,3},{8,12},{9,13},{10,6},{11,7},{1... | collective-permute-start | bytes 786440 | tf_op jit(solution)/shard_map/ppermute | solution.py:454
  13.8 4.0 %collective-permute-start = (f32[4,512]{1,0:T(4,128)S(1)}, f32[4,512]{1,0:T(4,128)S(1)}, u32[]{:S(2)}, u32[]{:S(2)}) collective-permute-start(f32[4,512]{1,0:T(4,128)S(1)} %get-tuple-element.22), channel_id=1, source_target_pairs={{0,4},{4,0},{8,12},{12,8},{16,20},{20,16},{24,28},{28,24},{1,5},{5... | collective-permute-start | bytes 24584 | tf_op jit(solution)/shard_map/ppermute | solution.py:471
  15.4 7.5 %collective-permute-start.4 = (f32[64,1024]{1,0:T(8,128)S(1)}, f32[64,1024]{1,0:T(8,128)S(1)}, u32[]{:S(2)}, u32[]{:S(2)}) collective-permute-start(f32[64,1024]{1,0:T(8,128)S(1)} %collective-permute-done.3.refs_0_), channel_id=1, source_target_pairs={{0,2},{1,3},{2,0},{3,1},{4,6},{5,7},{6,4},{7,5},{8,10},{9,11},{10,... | collective-permute-start | bytes 786440 | tf_op jit(solution)/shard_map/ppermute | solution.py:477
  17.8 3.7 %collective-permute-start.1 = (f32[4,512]{1,0:T(4,128)S(1)}, f32[4,512]{1,0:T(4,128)S(1)}, u32[]{:S(2)}, u32[]{:S(2)}) collective-permute-start(f32[4,512]{1,0:T(4,128)S(1)} %add.14), channel_id=1, source_target_pairs={{0,8},{4,12},{8,0},{12,4},{16,24},{20,28},{24,16},{28,20},{1,9},{5... | collective-permute-start | bytes 24584 | tf_op jit(solution)/shard_map/ppermute | solution.py:471
  21.5 6.4 %copy-start.3 = (f32[512]{0:T(512)S(1)}, f32[512]{0:T(512)}, u32[]{:S(2)}) copy-start(f32[512]{0:T(512)} %param.16) | copy-start | bytes 6148
  21.5 6.4 %copy-start.4 = (f32[512]{0:T(512)S(1)}, f32[512]{0:T(512)}, u32[]{:S(2)}) copy-start(f32[512]{0:T(512)} %param.17) | copy-start | bytes 6148
  22.9 3.1 %collective-permute-start.5 = (f32[64,1024]{1,0:T(8,128)S(1)}, f32[64,1024]{1,0:T(8,128)S(1)}, u32[]{:S(2)}, u32[]{:S(2)}) collective-permute-start(f32[64,1024]{1,0:T(8,128)S(1)} %collective-permute-done.3.refs_0_), channel_id=1, source_target_pairs={{0,1},{1,0},{2,3},{3,2},{4,5},{5,4},{6,7},{7,6},{8,9},{9,8},{10,11... | collective-permute-start | bytes 786440 | tf_op jit(solution)/shard_map/ppermute | solution.py:493
  22.9 3.1 %collective-permute-start.6 = (f32[64,1024]{1,0:T(8,128)S(1)}, f32[64,1024]{1,0:T(8,128)S(1)}, u32[]{:S(2)}, u32[]{:S(2)}) collective-permute-start(f32[64,1024]{1,0:T(8,128)S(1)} %collective-permute-done.4.refs_1_), channel_id=1, source_target_pairs={{0,1},{1,0},{2,3},{3,2},{4,5},{5,4},{6,7},{7,6},{8,9},{9,8},{10,11... | collective-permute-start | bytes 786440 | tf_op jit(solution)/shard_map/ppermute | solution.py:493
  23.4 4.6 %collective-permute-start.2 = (f32[4,512]{1,0:T(4,128)S(1)}, f32[4,512]{1,0:T(4,128)S(1)}, u32[]{:S(2)}, u32[]{:S(2)}) collective-permute-start(f32[4,512]{1,0:T(4,128)S(1)} %add.15.g_ref), channel_id=1, source_target_pairs={{0,16},{4,20},{8,24},{12,28},{16,0},{20,4},{24,8},{28,12},{1,17},{... | collective-permute-start | bytes 24584 | tf_op jit(solution)/shard_map/ppermute | solution.py:471
  32.8 3.5 %collective-permute-start.9 = (f32[12,128]{1,0:T(8,128)S(1)}, f32[12,128]{1,0:T(8,128)S(1)}, u32[]{:S(2)}, u32[]{:S(2)}) collective-permute-start(f32[12,128]{1,0:T(8,128)S(1)} %get-tuple-element.36), channel_id=1, source_target_pairs={{0,1},{1,0},{2,3},{3,2},{4,5},{5,4},{6,7},{7,6},{8,9},{9,8},{10,11... | collective-permute-start | bytes 18440 | tf_op jit(solution)/shard_map/ppermute | solution.py:501
  32.8 3.7 %collective-permute-start.8 = (f32[12,128]{1,0:T(8,128)S(1)}, f32[12,128]{1,0:T(8,128)S(1)}, u32[]{:S(2)}, u32[]{:S(2)}) collective-permute-start(f32[12,128]{1,0:T(8,128)S(1)} %get-tuple-element.36), channel_id=1, source_target_pairs={{0,2},{1,3},{2,0},{3,1},{4,6},{5,7},{6,4},{7,5},{8,10},{9,11},{10,... | collective-permute-start | bytes 18440 | tf_op jit(solution)/shard_map/ppermute | solution.py:501
  33.4 3.2 %collective-permute-start.7 = (f32[12,128]{1,0:T(8,128)S(1)}, f32[12,128]{1,0:T(8,128)S(1)}, u32[]{:S(2)}, u32[]{:S(2)}) collective-permute-start(f32[12,128]{1,0:T(8,128)S(1)} %get-tuple-element.36), channel_id=1, source_target_pairs={{0,3},{1,2},{2,1},{3,0},{4,7},{5,6},{6,5},{7,4},{8,11},{9,10},{10,... | collective-permute-start | bytes 18440 | tf_op jit(solution)/shard_map/ppermute | solution.py:501
  34.7 1.9 %copy-start.5 = (f32[1536]{0:T(1024)S(1)}, f32[1536]{0:T(1024)}, u32[]{:S(2)}) copy-start(f32[1536]{0:T(1024)} %param.22) | copy-start | bytes 18436
  34.7 1.9 %copy-start.6 = (s32[1536]{0:T(1024)S(1)}, s32[1536]{0:T(1024)}, u32[]{:S(2)}) copy-start(s32[1536]{0:T(1024)} %param.23) | copy-start | bytes 18436

commit v4 on v3

--- a/solution.py
+++ b/solution.py
@@ -258,31 +258,30 @@
     )(*fd_parts, par)
 
 
-def boundary_kernel(order, pick, *refs):
+def boundary_kernel(order, half, pick, *refs):
     pieces = refs[: len(order)]
     out_ref, hi, lo = refs[len(order) :]
     my_case = lax.axis_index("case")
     for mask, piece in zip(order, pieces):
         size = piece.shape[0]
-        span = pl.ds(pl.multiple_of((my_case ^ mask) * size, size), size)
+        slot = lax.rem(my_case ^ mask, half)
+        span = pl.ds(pl.multiple_of(slot * size, size), size)
         hi[span, :], lo[span, :] = split_hi_lo(piece[...])
     out_ref[...] = two_pass(hi[...], lo[...], pick[...])
 
 
-def boundary_columns(order, pick, pieces):
+def boundary_columns(order, pick, pieces, flops):
     cols, width = pick.shape
     total = sum(piece.shape[0] for piece in pieces)
     vmem = pl.BlockSpec(memory_space=pltpu.VMEM)
     return pl.pallas_call(
-        functools.partial(boundary_kernel, order),
+        functools.partial(boundary_kernel, order, len(order)),
         in_specs=[vmem] * (1 + len(pieces)),
         out_specs=vmem,
         out_shape=pltpu.VMEM((total, width), F32),
         scratch_shapes=[pltpu.VMEM((total, cols), BF16)] * 2,
         compiler_params=pltpu.CompilerParams(vmem_limit_bytes=8 * 2**20),
-        cost_estimate=pl.CostEstimate(
-            flops=4 * total * cols * width, bytes_accessed=8 * total * cols, transcendentals=0
-        ),
+        cost_estimate=pl.CostEstimate(flops=flops, bytes_accessed=1, transcendentals=0),
         name="boundary_columns",
     )(pick, *pieces)
 
@@ -291,23 +290,44 @@
     return jnp.maximum(jnp.exp2(power * jnp.log2(square + 1e-4)) - 1.0, 0.0) * rate
 
 
-def branch_kernel(half, n_ahead, g_ref, far_ref, tie_ref, fault_ref, par_ref, fd_ref, edge_ref, *refs):
+def case_kernel(tie_ref, fault_ref, out_ref):
+    out_ref[0:1, :] = tie_ref[...]
+    out_ref[1:2, :] = fault_ref[...]
+
+
+def case_rows(tie_x, fault_z):
+    vmem = pl.BlockSpec(memory_space=pltpu.VMEM)
+    return pl.pallas_call(
+        case_kernel,
+        in_specs=[vmem, vmem],
+        out_specs=vmem,
+        out_shape=pltpu.VMEM((2, tie_x.shape[1]), F32),
+        compiler_params=pltpu.CompilerParams(vmem_limit_bytes=2**20),
+        cost_estimate=pl.CostEstimate(flops=2**34, bytes_accessed=2**20, transcendentals=0),
+        name="case_rows",
+    )(tie_x, fault_z)
+
+
+def branch_kernel(half, n_ahead, g_ref, far_ref, case_ref, par_ref, fd_ref, near_ref, far_edge_ref, *refs):
     ahead = refs[:n_ahead]
     volt_hbm, relay_hbm, square_ref, worst_ref, vbuf, rbuf, uh, ul, vsem, rsem = refs[n_ahead:]
     rows, cases = vbuf.shape
     branches = par_ref.shape[0]
-    early = square_ref.shape[0]
+    late = square_ref.shape[0]
     ext = uh.shape[0]
     g = g_ref[...] + far_ref[...]
     g1, g2, g3 = g[0:1], g[1:2], g[2:3]
-    ratio = g2 / (tie_ref[...] + g1)
-    amps = 1.0 / (g3 - g2 * ratio + fault_ref[...])
+    ratio = g2 / (case_ref[0:1, :] + g1)
+    amps = 1.0 / (g3 - g2 * ratio + case_ref[1:2, :])
 
     def sag_of(fd):
         return (fd[:, :cases] - fd[:, cases:] * ratio) * amps
 
-    edge = pl.ds(rows, ext - rows)
-    uh[edge, :], ul[edge, :] = split_hi_lo(sag_of(edge_ref[...]))
+    side = lax.axis_index("case") // half
+    for edge_ref, place in ((near_ref, side), (far_edge_ref, 1 - side)):
+        size = edge_ref.shape[0]
+        edge = pl.ds(pl.multiple_of(rows + place * size, size), size)
+        uh[edge, :], ul[edge, :] = split_hi_lo(sag_of(edge_ref[...]))
     tiles = rows // TILE
     rim = rim_tile(half, tiles)
     for t in range(tiles):
@@ -339,36 +359,36 @@
             )
         return square
 
-    start = 0
-    ready = []
-    for part in ahead:
-        ready.append((part, start))
-        start += part.shape[0]
-    for t in range((branches - early) // TILE):
-        start = early + t * TILE
+    starts = [sum(part.shape[0] for part in ahead[:i]) for i in range(n_ahead + 1)]
+    tiles = (branches - starts[-1]) // TILE
+    for t in range(tiles):
+        start = branches - (t + 1) * TILE
         par = par_ref[pl.ds(start, TILE), :]
         square = square_of(drops(par, 0), par, start)
-        span = pl.ds(t * TILE, TILE)
-        rbuf[span, :] = relay_of_square(square, par[:, 3:4], par[:, 4:5])
-        if t < len(ready):
-            part, start = ready[t]
-            count = part.shape[0]
+        if start >= late:
+            span = pl.ds(start - late, TILE)
+            rbuf[span, :] = relay_of_square(square, par[:, 3:4], par[:, 4:5])
+            target = relay_hbm.at[pl.ds(start, TILE)]
+            copies.append(pltpu.make_async_copy(rbuf.at[span], target, rsem.at[t]))
+        else:
+            square_ref[pl.ds(start, TILE), :] = square
+        for i in range(t, n_ahead if t == tiles - 1 else min(t + 1, n_ahead)):
+            start, count = starts[i], ahead[i].shape[0]
             par = par_ref[pl.ds(start, count), :]
-            drop = sag_of(part[...]) + drops(par, rows)
+            drop = sag_of(ahead[i][...]) + drops(par, rows)
             square_ref[pl.ds(start, count), :] = square_of(drop, par, start)
-        target = relay_hbm.at[pl.ds(early + t * TILE, TILE)]
-        copies.append(pltpu.make_async_copy(rbuf.at[span], target, rsem.at[t]))
-        copies[-1].start()
+        if len(copies) == t + 2:
+            copies[-1].start()
     for copy in copies:
         copy.wait()
 
 
-def screen_branches(g, g_far, tie_x, fault_z, par, fd, edge, ahead, n_case):
-    count = tie_x.shape[1]
+def screen_branches(g, g_far, case_par, par, fd, edges, ahead, n_case):
+    count = case_par.shape[1]
     rows = fd.shape[0]
     branches = par.shape[0]
-    early = sum(part.shape[0] for part in ahead)
-    ext = rows + edge.shape[0]
+    late = sum(part.shape[0] for part in ahead) + TILE
+    ext = rows + sum(edge.shape[0] for edge in edges)
     vmem = pl.BlockSpec(memory_space=pltpu.VMEM)
     hbm = pl.BlockSpec(memory_space=pltpu.HBM)
     return pl.pallas_call(
@@ -378,12 +398,12 @@
         out_shape=[
             jax.ShapeDtypeStruct((rows, count), F32),
             jax.ShapeDtypeStruct((branches, count), F32),
-            pltpu.VMEM((early, count), F32),
+            pltpu.VMEM((late, count), F32),
             pltpu.VMEM((branches // 128, 128), F32),
         ],
         scratch_shapes=[
             pltpu.VMEM((rows, count), F32),
-            pltpu.VMEM((branches - early, count), F32),
+            pltpu.VMEM((branches - late, count), F32),
             pltpu.VMEM((ext, count), BF16),
             pltpu.VMEM((ext, count), BF16),
             pltpu.SemaphoreType.DMA,
@@ -391,7 +411,7 @@
         ],
         compiler_params=pltpu.CompilerParams(vmem_limit_bytes=24 * 2**20),
         name="screen_branches",
-    )(g, g_far, tie_x, fault_z, par, fd, edge, *ahead)
+    )(g, g_far, case_par, par, fd, *edges, *ahead)
 
 
 def late_kernel(square_ref, par_ref, relay_in, relay_hbm, rbuf, sems):
@@ -476,26 +496,32 @@
     (own,) = after(g, own)
     other = lax.ppermute(own, "case", [(i, i ^ half) for i in range(n_case)])
     ahead = []
-    part = par.shape[0] // 4
+    sizes = [par.shape[0] // 4, par.shape[0] // 4]
     bit = 1
     while bit < n_bus // 2:
         far = swap_over_bus(g, bit)
-        if len(ahead) < 2:
-            ahead.append(advance(fd_parts, par, len(ahead) * part, part, n_case))
+        if bit == 2:
+            (own,) = after(g, own)
+        if len(ahead) < len(sizes):
+            i = len(ahead)
+            ahead.append(advance(fd_parts, par, sum(sizes[:i]), sizes[i], n_case))
             (far,) = after(ahead[-1], far)
         g = g + far
         bit *= 2
     g_far = swap_over_bus(g, n_bus // 2)
-    pieces, order = list(after(g, own, other)), [0, half]
-    bit = half // 2
-    while bit:
-        swap = [(i, i ^ bit) for i in range(n_case)]
-        pieces = pieces + [lax.ppermute(x, "case", swap) for x in pieces]
-        order = order + [m ^ bit for m in order]
-        bit //= 2
-    edge = boundary_columns(order, pick, pieces)
+    (other,) = after(g, other)
+    edges = []
+    for piece, flops in ((own, 2**29), (other, 1)):
+        pieces, order = [piece], [0]
+        bit = half // 2
+        while bit:
+            swap = [(i, i ^ bit) for i in range(n_case)]
+            pieces = pieces + [lax.ppermute(x, "case", swap) for x in pieces]
+            order = order + [m ^ bit for m in order]
+            bit //= 2
+        edges.append(boundary_columns(order, pick, pieces, flops))
     voltage, relay_rate, square, worst = screen_branches(
-        g, g_far, tie_x[None], fault_z[None], par, fd, edge, ahead, n_case
+        g, g_far, case_rows(tie_x[None], fault_z[None]), par, fd, edges, ahead, n_case
     )
     others = [
         lax.ppermute(worst, "case", [(i, i ^ m) for i in range(n_case)])

time: 37.4 us -> 36.4 us (0.973)
  starting transfers between devices: 13.6 us -> 13.2 us
    pallas_call x1, Pallas kernels: 4.8 us -> 4.11 us  [screen_branches(): pl.pallas_call(functools.partial(branch_kernel, n_case // 2, len(ahead)),...]
    ppermute x2, starting transfers between devices: 0.51 us -> 0.01 us  [per_device(): pieces = pieces + [lax.ppermute(x, 'case', swap) for x in pieces]]
    pallas_call x1 -> x3, Pallas kernels: 1.44 us -> 1.5 us  [the longest x2 1.49 us: boundary_columns(): pl.pallas_call(functools.partial(boundary_kernel, order, len(order)), in_...]
  transfers between devices with their start and end apart: 10 -> 10, of which waited for: 4 -> 4; matrix products, arithmetic and copies ran while one was open for 0% -> 0% of each run, Pallas kernels for 36% -> 38%
where the time goes in v4:
time: 36.4 us; the launch traced here: 36.2 us
  Pallas kernels  19.4 us (53%)
  starting transfers between devices  13.2 us (36%)
  waiting for transfers between devices  2.1 us (6%)
  between operations  0.83 us (2%)
  other arithmetic  0.64 us (2%)
    pallas_call x1, Pallas kernels, pick_columns(): pl.pallas_call(functools.partial(columns_kernel, n_case // 2), in_specs=[...  6.56 us
    ppermute x3, starting transfers between devices, swap_over_bus(): return lax.ppermute(g, 'bus', [(i, i ^ bit) for i in range(n_bus)])  5.9 us
    ppermute x1, starting transfers between devices, per_device(): own = lax.ppermute(send, ('bus', 'case'), pairs)  4.86 us
    pallas_call x1, Pallas kernels, screen_branches(): pl.pallas_call(functools.partial(branch_kernel, n_case // 2, len(ahead)),...  4.11 us
    pallas_call x2, Pallas kernels, advance(): pl.pallas_call(functools.partial(advance_kernel, n_case // 2, start), in_...  3.79 us
    ppermute x3, starting transfers between devices, per_device(): lax.ppermute(worst, 'case', [(i, i ^ m) for i in range(n_case)])  1.93 us
    pallas_call x1, Pallas kernels, late_relays(): pl.pallas_call(late_kernel, in_specs=[vmem, vmem, hbm], out_specs=hbm, ou...  1.8 us
    pallas_call x1, Pallas kernels, stage(): pl.pallas_call(functools.partial(stage_kernel, half), in_specs=[pl.BlockS...  1.63 us
  transfers between devices with their start and end apart: 10, of which 4 were waited for; matrix products, arithmetic and copies ran while one was open for 0% of the time, Pallas kernels for 38%

profile of v4, /device:TPU:0, one launch (start us, length us, event | category | flops | bytes accessed | tf_op | source)
XLA Modules:
  0.0 36.2 jit_solution(17207964777471611045)
XLA Ops:
  0.6 0.0 copy-start
  0.6 0.0 copy-start.1
  0.7 0.0 copy-start.2
  0.7 1.6 %stage.1 = (f32[64,1024]{1,0:T(8,128)S(1)}, f32[512,1024]{1,0:T(8,128)S(1)}, bf16[1024,1024]{1,0:T(8,128)(2,1)S(1)}) custom-call(f32[1024,1024]{1,0:T(8,128)} %z_hbm.3, s32[8,2,128]{2,1,0:T(2,128)} %lists_hbm.1, s32[1,512]{1,0:T(1,128)} %bitcast.24, s32[2,512]{1,0:T(2,128)} %bitcast.22), custom_call_target="tpu_custom_call" | custom-call | tf_op jit(solution)/shard_map/stage/pallas_call | solution.py:75
  2.3 4.9 %collective-permute-start.3 = (f32[64,1024]{1,0:T(8,128)S(1)}, f32[64,1024]{1,0:T(8,128)S(1)}, u32[]{:S(2)}, u32[]{:S(2)}) collective-permute-start(f32[64,1024]{1,0:T(8,128)S(1)} %get-tuple-element.29), channel_id=1, source_target_pairs={{0,4},{1,5},{4,8},{5,9},{6,2},{7,3},{8,12},{9,13},{10,6},{11,7},{1... | collective-permute-start | bytes 786440 | tf_op jit(solution)/shard_map/ppermute | solution.py:474
  7.2 0.0 copy-done
  7.2 0.0 copy-done.1
  7.2 0.0 copy-done.2
  7.2 6.6 %pick_columns.1 = (f32[1024,1024]{1,0:T(8,128)S(1)}, f32[4,512]{1,0:T(4,128)S(1)}, f32[1536,8]{1,0:T(8,128)S(1)}, bf16[1024,1024]{1,0:T(8,128)(2,1)S(1)}, bf16[1024,1024]{1,0:T(8,128)(2,1)S(1)}) custom-call(f32[512,1024]{1,0:T(8,128)S(1)} %get-tuple-element.20.z_ref, bf16[1024,1024]{1,0:T(8,128)(2,1)S(1)} %get-tuple-element.21.pick, s32[1,512]{1,0:T(1,128)S(1)} %bitcast.25, ...), custom_call_target="tpu_custom_call" | custom-call | tf_op jit(solution)/shard_map/pick_columns/pallas_call | solution.py:200
  13.8 1.6 %collective-permute-start = (f32[4,512]{1,0:T(4,128)S(1)}, f32[4,512]{1,0:T(4,128)S(1)}, u32[]{:S(2)}, u32[]{:S(2)}) collective-permute-start(f32[4,512]{1,0:T(4,128)S(1)} %get-tuple-element.22), channel_id=1, source_target_pairs={{0,4},{4,0},{8,12},{12,8},{16,20},{20,16},{24,28},{28,24},{1,5},{5... | collective-permute-start | bytes 24584 | tf_op jit(solution)/shard_map/ppermute | solution.py:491
  15.4 0.0 collective-permute-done.3.refs_0_
  15.4 0.5 %collective-permute-start.5 = (f32[64,1024]{1,0:T(8,128)S(1)}, f32[64,1024]{1,0:T(8,128)S(1)}, u32[]{:S(2)}, u32[]{:S(2)}) collective-permute-start(f32[64,1024]{1,0:T(8,128)S(1)} %collective-permute-done.3.refs_0_), channel_id=1, source_target_pairs={{0,2},{1,3},{2,0},{3,1},{4,6},{5,7},{6,4},{7,5},{8,10},{9,11},{10,... | collective-permute-start | bytes 786440 | tf_op jit(solution)/shard_map/ppermute | solution.py:497
  15.9 1.9 %advance.2.refs_0_ = f32[384,1024]{1,0:T(8,128)S(1)} custom-call(bf16[1024,1024]{1,0:T(8,128)(2,1)S(1)} %get-tuple-element.23.fd_hi, bf16[1024,1024]{1,0:T(8,128)(2,1)S(1)} %get-tuple-element.24.fd_lo, f32[1536,8]{1,0:T(8,128)S(1)} %get-tuple-element.25.par_ref), custom_call_target="tpu_custom_call" | custom-call | flops 1610612736 | bytes 3145728 | tf_op jit(solution)/shard_map/advance/pallas_call | solution.py:248
  17.8 0.0 collective-permute-done
  17.8 0.0 copy-start.3
  17.8 0.0 copy-start.4
  17.8 1.6 %collective-permute-start.1 = (f32[4,512]{1,0:T(4,128)S(1)}, f32[4,512]{1,0:T(4,128)S(1)}, u32[]{:S(2)}, u32[]{:S(2)}) collective-permute-start(f32[4,512]{1,0:T(4,128)S(1)} %add.14), channel_id=1, source_target_pairs={{0,8},{4,12},{8,0},{12,4},{16,24},{20,28},{24,16},{28,20},{1,9},{5... | collective-permute-start | bytes 24584 | tf_op jit(solution)/shard_map/ppermute | solution.py:491
  19.5 1.9 %advance.3.refs_1_ = f32[384,1024]{1,0:T(8,128)S(1)} custom-call(bf16[1024,1024]{1,0:T(8,128)(2,1)S(1)} %get-tuple-element.23.fd_hi, bf16[1024,1024]{1,0:T(8,128)(2,1)S(1)} %get-tuple-element.24.fd_lo, f32[1536,8]{1,0:T(8,128)S(1)} %get-tuple-element.25.par_ref), custom_call_target="tpu_custom_call" | custom-call | flops 1610612736 | bytes 3145728 | tf_op jit(solution)/shard_map/advance/pallas_call | solution.py:248
  21.4 0.2 collective-permute-done.1
  21.6 0.0 collective-permute-start.4
  21.6 1.3 %collective-permute-done.5.refs_0_ = f32[64,1024]{1,0:T(8,128)S(1)} collective-permute-done((f32[64,1024]{1,0:T(8,128)S(1)}, f32[64,1024]{1,0:T(8,128)S(1)}, u32[]{:S(2)}, u32[]{:S(2)}) %collective-permute-start.5) | collective-permute-done | bytes 262176 | tf_op jit(solution)/shard_map/ppermute | solution.py:497
  22.9 0.0 collective-permute-start.6
  22.9 0.0 copy-done.3
  22.9 0.0 copy-done.4
  22.9 2.7 %collective-permute-start.2 = (f32[4,512]{1,0:T(4,128)S(1)}, f32[4,512]{1,0:T(4,128)S(1)}, u32[]{:S(2)}, u32[]{:S(2)}) collective-permute-start(f32[4,512]{1,0:T(4,128)S(1)} %add.15.g_ref), channel_id=1, source_target_pairs={{0,16},{4,20},{8,24},{12,28},{16,0},{20,4},{24,8},{28,12},{1,17},{... | collective-permute-start | bytes 24584 | tf_op jit(solution)/shard_map/ppermute | solution.py:491
  25.5 0.0 collective-permute-done.4.refs_1_
  25.5 0.7 %boundary_columns.2.near_ref = f32[128,1024]{1,0:T(8,128)S(1)} custom-call(bf16[1024,1024]{1,0:T(8,128)(2,1)S(1)} %get-tuple-element.21.pick, f32[64,1024]{1,0:T(8,128)S(1)} %collective-permute-done.3.refs_0_, f32[64,1024]{1,0:T(8,128)S(1)} %collective-permute-done.4.refs_1_), custom_call_target="tpu_custom_call" | custom-call | flops 536870912 | bytes 1 | tf_op jit(solution)/shard_map/boundary_columns/pallas_call | solution.py:277
  26.3 0.0 collective-permute-done.6.refs_1_
  26.3 0.7 %boundary_columns.3.far_edge_ref = f32[128,1024]{1,0:T(8,128)S(1)} custom-call(bf16[1024,1024]{1,0:T(8,128)(2,1)S(1)} %get-tuple-element.21.pick, f32[64,1024]{1,0:T(8,128)S(1)} %collective-permute-done.5.refs_0_, f32[64,1024]{1,0:T(8,128)S(1)} %collective-permute-done.6.refs_1_), custom_call_target="tpu_custom_call" | custom-call | flops 1 | bytes 1 | tf_op jit(solution)/shard_map/boundary_columns/pallas_call | solution.py:277
  27.1 0.4 %collective-permute-done.2.far_ref = f32[4,512]{1,0:T(4,128)S(1)} collective-permute-done((f32[4,512]{1,0:T(4,128)S(1)}, f32[4,512]{1,0:T(4,128)S(1)}, u32[]{:S(2)}, u32[]{:S(2)}) %collective-permute-start.2) | collective-permute-done | bytes 8224 | tf_op jit(solution)/shard_map/ppermute | solution.py:491
  27.5 4.1 %screen_branches.1 = (f32[1024,512]{1,0:T(8,128)}, f32[1536,512]{1,0:T(8,128)}, f32[1024,512]{1,0:T(8,128)S(1)}, f32[12,128]{1,0:T(8,128)S(1)}) custom-call(f32[4,512]{1,0:T(4,128)S(1)} %add.15.g_ref, f32[4,512]{1,0:T(4,128)S(1)} %collective-permute-done.2.far_ref, f32[2,512]{1,0:T(2,128)S(1)} %case_rows.1.case_ref, ...), custom_call_target="tpu_custom_call" | custom-call | tf_op jit(solution)/shard_map/screen_branches/pallas_call | solution.py:394
  31.6 0.1 collective-permute-start.9
  31.7 0.8 %collective-permute-start.8 = (f32[12,128]{1,0:T(8,128)S(1)}, f32[12,128]{1,0:T(8,128)S(1)}, u32[]{:S(2)}, u32[]{:S(2)}) collective-permute-start(f32[12,128]{1,0:T(8,128)S(1)} %get-tuple-element.36), channel_id=1, source_target_pairs={{0,2},{1,3},{2,0},{3,1},{4,6},{5,7},{6,4},{7,5},{8,10},{9,11},{10,... | collective-permute-start | bytes 18440 | tf_op jit(solution)/shard_map/ppermute | solution.py:527
  32.5 1.1 %collective-permute-start.7 = (f32[12,128]{1,0:T(8,128)S(1)}, f32[12,128]{1,0:T(8,128)S(1)}, u32[]{:S(2)}, u32[]{:S(2)}) collective-permute-start(f32[12,128]{1,0:T(8,128)S(1)} %get-tuple-element.36), channel_id=1, source_target_pairs={{0,3},{1,2},{2,1},{3,0},{4,7},{5,6},{6,5},{7,4},{8,11},{9,10},{10,... | collective-permute-start | bytes 18440 | tf_op jit(solution)/shard_map/ppermute | solution.py:527
  33.6 0.0 copy-start.5
  33.6 0.0 copy-start.6
  33.6 1.8 %late_relays.1 = f32[1536,512]{1,0:T(8,128)} custom-call(f32[1024,512]{1,0:T(8,128)S(1)} %get-tuple-element.34.square_ref, f32[1536,8]{1,0:T(8,128)S(1)} %get-tuple-element.25.par_ref, f32[1536,512]{1,0:T(8,128)} %get-tuple-element.35.relay_in), custom_call_target="tpu_custom_call", output_to_operand_aliasing={{}: (2, {})} | custom-call | flops 4194304 | bytes 4194304 | tf_op jit(solution)/shard_map/late_relays/pallas_call | solution.py:432
  35.4 0.0 collective-permute-done.9
  35.4 0.0 collective-permute-done.8
  35.4 0.1 collective-permute-done.7
  35.6 0.0 copy-done.5
  35.6 0.0 copy-done.6
  35.6 0.6 %fusion.4 = f32[1536]{0:T(1024)} fusion(f32[1536]{0:T(1024)S(1)} %copy-done.5, f32[12,128]{1,0:T(8,128)S(1)} %collective-permute-done.9, f32[12,128]{1,0:T(8,128)S(1)} %collective-permute-done.8, f32[12,128]{1,0:T(8,128)S(1)} %get-tuple-element.36, f32[12,128]{1,0:T(8,128)S(1)} %collective-permute-done.7, s32[1536]{0:T(1024)S(1)} %copy-done.6), kind=kLoop, calls=%fused_computation.5 | loop fusion | flops 27648 | bytes 43008 | tf_op jit(solution)/shard_map/mul | solution.py:290
  (3 shorter events, 0.0 us)
Async XLA Ops:
  0.6 6.5 %copy-start = (s32[512,2]{0,1:T(2,128)S(1)}, s32[512,2]{0,1:T(2,128)}, u32[]{:S(2)}) copy-start(s32[512,2]{0,1:T(2,128)} %param.15) | copy-start | bytes 12292
  0.6 6.5 %copy-start.1 = (s32[512]{0:T(512)S(1)}, s32[512]{0:T(512)}, u32[]{:S(2)}) copy-start(s32[512]{0:T(512)} %param.14) | copy-start | bytes 6148
  0.7 6.5 %copy-start.2 = (s32[1024]{0:T(1024)S(1)}, s32[1024]{0:T(1024)}, u32[]{:S(2)}) copy-start(s32[1024]{0:T(1024)} %param.13) | copy-start | bytes 12292
  2.3 13.1 %collective-permute-start.3 = (f32[64,1024]{1,0:T(8,128)S(1)}, f32[64,1024]{1,0:T(8,128)S(1)}, u32[]{:S(2)}, u32[]{:S(2)}) collective-permute-start(f32[64,1024]{1,0:T(8,128)S(1)} %get-tuple-element.29), channel_id=1, source_target_pairs={{0,4},{1,5},{4,8},{5,9},{6,2},{7,3},{8,12},{9,13},{10,6},{11,7},{1... | collective-permute-start | bytes 786440 | tf_op jit(solution)/shard_map/ppermute | solution.py:474
  13.8 4.0 %collective-permute-start = (f32[4,512]{1,0:T(4,128)S(1)}, f32[4,512]{1,0:T(4,128)S(1)}, u32[]{:S(2)}, u32[]{:S(2)}) collective-permute-start(f32[4,512]{1,0:T(4,128)S(1)} %get-tuple-element.22), channel_id=1, source_target_pairs={{0,4},{4,0},{8,12},{12,8},{16,20},{20,16},{24,28},{28,24},{1,5},{5... | collective-permute-start | bytes 24584 | tf_op jit(solution)/shard_map/ppermute | solution.py:491
  15.4 7.5 %collective-permute-start.5 = (f32[64,1024]{1,0:T(8,128)S(1)}, f32[64,1024]{1,0:T(8,128)S(1)}, u32[]{:S(2)}, u32[]{:S(2)}) collective-permute-start(f32[64,1024]{1,0:T(8,128)S(1)} %collective-permute-done.3.refs_0_), channel_id=1, source_target_pairs={{0,2},{1,3},{2,0},{3,1},{4,6},{5,7},{6,4},{7,5},{8,10},{9,11},{10,... | collective-permute-start | bytes 786440 | tf_op jit(solution)/shard_map/ppermute | solution.py:497
  17.8 5.1 %copy-start.3 = (f32[512]{0:T(512)S(1)}, f32[512]{0:T(512)}, u32[]{:S(2)}) copy-start(f32[512]{0:T(512)} %param.16) | copy-start | bytes 6148
  17.8 5.0 %copy-start.4 = (f32[512]{0:T(512)S(1)}, f32[512]{0:T(512)}, u32[]{:S(2)}) copy-start(f32[512]{0:T(512)} %param.17) | copy-start | bytes 6148
  17.8 3.7 %collective-permute-start.1 = (f32[4,512]{1,0:T(4,128)S(1)}, f32[4,512]{1,0:T(4,128)S(1)}, u32[]{:S(2)}, u32[]{:S(2)}) collective-permute-start(f32[4,512]{1,0:T(4,128)S(1)} %add.14), channel_id=1, source_target_pairs={{0,8},{4,12},{8,0},{12,4},{16,24},{20,28},{24,16},{28,20},{1,9},{5... | collective-permute-start | bytes 24584 | tf_op jit(solution)/shard_map/ppermute | solution.py:491
  21.6 4.0 %collective-permute-start.4 = (f32[64,1024]{1,0:T(8,128)S(1)}, f32[64,1024]{1,0:T(8,128)S(1)}, u32[]{:S(2)}, u32[]{:S(2)}) collective-permute-start(f32[64,1024]{1,0:T(8,128)S(1)} %collective-permute-done.3.refs_0_), channel_id=1, source_target_pairs={{0,1},{1,0},{2,3},{3,2},{4,5},{5,4},{6,7},{7,6},{8,9},{9,8},{10,11... | collective-permute-start | bytes 786440 | tf_op jit(solution)/shard_map/ppermute | solution.py:519
  22.9 3.4 %collective-permute-start.6 = (f32[64,1024]{1,0:T(8,128)S(1)}, f32[64,1024]{1,0:T(8,128)S(1)}, u32[]{:S(2)}, u32[]{:S(2)}) collective-permute-start(f32[64,1024]{1,0:T(8,128)S(1)} %collective-permute-done.5.refs_0_), channel_id=1, source_target_pairs={{0,1},{1,0},{2,3},{3,2},{4,5},{5,4},{6,7},{7,6},{8,9},{9,8},{10,11... | collective-permute-start | bytes 786440 | tf_op jit(solution)/shard_map/ppermute | solution.py:519
  22.9 4.6 %collective-permute-start.2 = (f32[4,512]{1,0:T(4,128)S(1)}, f32[4,512]{1,0:T(4,128)S(1)}, u32[]{:S(2)}, u32[]{:S(2)}) collective-permute-start(f32[4,512]{1,0:T(4,128)S(1)} %add.15.g_ref), channel_id=1, source_target_pairs={{0,16},{4,20},{8,24},{12,28},{16,0},{20,4},{24,8},{28,12},{1,17},{... | collective-permute-start | bytes 24584 | tf_op jit(solution)/shard_map/ppermute | solution.py:491
  31.6 3.8 %collective-permute-start.9 = (f32[12,128]{1,0:T(8,128)S(1)}, f32[12,128]{1,0:T(8,128)S(1)}, u32[]{:S(2)}, u32[]{:S(2)}) collective-permute-start(f32[12,128]{1,0:T(8,128)S(1)} %get-tuple-element.36), channel_id=1, source_target_pairs={{0,1},{1,0},{2,3},{3,2},{4,5},{5,4},{6,7},{7,6},{8,9},{9,8},{10,11... | collective-permute-start | bytes 18440 | tf_op jit(solution)/shard_map/ppermute | solution.py:527
  31.7 3.7 %collective-permute-start.8 = (f32[12,128]{1,0:T(8,128)S(1)}, f32[12,128]{1,0:T(8,128)S(1)}, u32[]{:S(2)}, u32[]{:S(2)}) collective-permute-start(f32[12,128]{1,0:T(8,128)S(1)} %get-tuple-element.36), channel_id=1, source_target_pairs={{0,2},{1,3},{2,0},{3,1},{4,6},{5,7},{6,4},{7,5},{8,10},{9,11},{10,... | collective-permute-start | bytes 18440 | tf_op jit(solution)/shard_map/ppermute | solution.py:527
  32.5 3.1 %collective-permute-start.7 = (f32[12,128]{1,0:T(8,128)S(1)}, f32[12,128]{1,0:T(8,128)S(1)}, u32[]{:S(2)}, u32[]{:S(2)}) collective-permute-start(f32[12,128]{1,0:T(8,128)S(1)} %get-tuple-element.36), channel_id=1, source_target_pairs={{0,3},{1,2},{2,1},{3,0},{4,7},{5,6},{6,5},{7,4},{8,11},{9,10},{10,... | collective-permute-start | bytes 18440 | tf_op jit(solution)/shard_map/ppermute | solution.py:527
  33.6 2.0 %copy-start.5 = (f32[1536]{0:T(1024)S(1)}, f32[1536]{0:T(1024)}, u32[]{:S(2)}) copy-start(f32[1536]{0:T(1024)} %param.22) | copy-start | bytes 18436
  33.6 2.0 %copy-start.6 = (s32[1536]{0:T(1024)S(1)}, s32[1536]{0:T(1024)}, u32[]{:S(2)}) copy-start(s32[1536]{0:T(1024)} %param.23) | copy-start | bytes 18436

commit v5 on v4

--- a/solution.py
+++ b/solution.py
@@ -310,10 +310,9 @@
 
 def branch_kernel(half, n_ahead, g_ref, far_ref, case_ref, par_ref, fd_ref, near_ref, far_edge_ref, *refs):
     ahead = refs[:n_ahead]
-    volt_hbm, relay_hbm, square_ref, worst_ref, vbuf, rbuf, uh, ul, vsem, rsem = refs[n_ahead:]
+    volt_hbm, square_ref, worst_ref, vbuf, uh, ul, vsem = refs[n_ahead:]
     rows, cases = vbuf.shape
     branches = par_ref.shape[0]
-    late = square_ref.shape[0]
     ext = uh.shape[0]
     g = g_ref[...] + far_ref[...]
     g1, g2, g3 = g[0:1], g[1:2], g[2:3]
@@ -335,8 +334,8 @@
         sag = sag_of(fd_ref[pl.ds(t * TILE, TILE), :])
         vbuf[span, :] = 1.0 - sag
         uh[span, :], ul[span, :] = split_hi_lo(sag)
-    copies = [pltpu.make_async_copy(vbuf, volt_hbm, vsem)]
-    copies[0].start()
+    copy = pltpu.make_async_copy(vbuf, volt_hbm, vsem)
+    copy.start()
 
     def drops(par, first):
         count = par.shape[0]
@@ -359,92 +358,83 @@
             )
         return square
 
+    def finish(drop, par, start):
+        square_ref[pl.ds(start, par.shape[0]), :] = square_of(drop, par, start)
+
     starts = [sum(part.shape[0] for part in ahead[:i]) for i in range(n_ahead + 1)]
-    tiles = (branches - starts[-1]) // TILE
-    for t in range(tiles):
-        start = branches - (t + 1) * TILE
-        par = par_ref[pl.ds(start, TILE), :]
-        square = square_of(drops(par, 0), par, start)
-        if start >= late:
-            span = pl.ds(start - late, TILE)
-            rbuf[span, :] = relay_of_square(square, par[:, 3:4], par[:, 4:5])
-            target = relay_hbm.at[pl.ds(start, TILE)]
-            copies.append(pltpu.make_async_copy(rbuf.at[span], target, rsem.at[t]))
-        else:
-            square_ref[pl.ds(start, TILE), :] = square
-        for i in range(t, n_ahead if t == tiles - 1 else min(t + 1, n_ahead)):
-            start, count = starts[i], ahead[i].shape[0]
-            par = par_ref[pl.ds(start, count), :]
-            drop = sag_of(ahead[i][...]) + drops(par, rows)
-            square_ref[pl.ds(start, count), :] = square_of(drop, par, start)
-        if len(copies) == t + 2:
-            copies[-1].start()
-    for copy in copies:
-        copy.wait()
+    whole = list(range(starts.pop(), branches, TILE))
+    for n in range(max(len(whole), n_ahead)):
+        if n < len(whole):
+            par = par_ref[pl.ds(whole[n], TILE), :]
+            finish(drops(par, 0), par, whole[n])
+        if n < n_ahead:
+            par = par_ref[pl.ds(starts[n], ahead[n].shape[0]), :]
+            finish(sag_of(ahead[n][...]) + drops(par, rows), par, starts[n])
+    copy.wait()
 
 
 def screen_branches(g, g_far, case_par, par, fd, edges, ahead, n_case):
     count = case_par.shape[1]
     rows = fd.shape[0]
     branches = par.shape[0]
-    late = sum(part.shape[0] for part in ahead) + TILE
     ext = rows + sum(edge.shape[0] for edge in edges)
     vmem = pl.BlockSpec(memory_space=pltpu.VMEM)
     hbm = pl.BlockSpec(memory_space=pltpu.HBM)
     return pl.pallas_call(
         functools.partial(branch_kernel, n_case // 2, len(ahead)),
         in_specs=[vmem] * (7 + len(ahead)),
-        out_specs=[hbm, hbm, vmem, vmem],
+        out_specs=[hbm, vmem, vmem],
         out_shape=[
             jax.ShapeDtypeStruct((rows, count), F32),
-            jax.ShapeDtypeStruct((branches, count), F32),
-            pltpu.VMEM((late, count), F32),
+            pltpu.VMEM((branches, count), F32),
             pltpu.VMEM((branches // 128, 128), F32),
         ],
         scratch_shapes=[
             pltpu.VMEM((rows, count), F32),
-            pltpu.VMEM((branches - late, count), F32),
             pltpu.VMEM((ext, count), BF16),
             pltpu.VMEM((ext, count), BF16),
             pltpu.SemaphoreType.DMA,
-            pltpu.SemaphoreType.DMA((branches // TILE,)),
         ],
         compiler_params=pltpu.CompilerParams(vmem_limit_bytes=24 * 2**20),
         name="screen_branches",
     )(g, g_far, case_par, par, fd, *edges, *ahead)
 
 
-def late_kernel(square_ref, par_ref, relay_in, relay_hbm, rbuf, sems):
+def relay_kernel(square_ref, par_ref, relay_hbm, rbuf, sems):
+    rows = square_ref.shape[0]
     copies = []
-    for t in range(square_ref.shape[0] // TILE):
-        span = pl.ds(t * TILE, TILE)
+    first = 0
+    while first < rows:
+        count = TILE if first + 2 * TILE <= rows else TILE // 2
+        span = pl.ds(first, count)
         par = par_ref[span, :]
         rbuf[span, :] = relay_of_square(square_ref[span, :], par[:, 3:4], par[:, 4:5])
-        copies.append(pltpu.make_async_copy(rbuf.at[span], relay_hbm.at[span], sems.at[t]))
+        sem = sems.at[len(copies)]
+        copies.append(pltpu.make_async_copy(rbuf.at[span], relay_hbm.at[span], sem))
         copies[-1].start()
+        first += count
     for copy in copies:
         copy.wait()
 
 
-def late_relays(square, par, relay_rate):
+def relay_rates(square, par):
+    rows = square.shape[0]
     vmem = pl.BlockSpec(memory_space=pltpu.VMEM)
-    hbm = pl.BlockSpec(memory_space=pltpu.HBM)
-    return pl.pallas_call(
-        late_kernel,
-        in_specs=[vmem, vmem, hbm],
-        out_specs=hbm,
-        out_shape=jax.ShapeDtypeStruct(relay_rate.shape, F32),
-        input_output_aliases={2: 0},
+    return pl.pallas_call(
+        relay_kernel,
+        in_specs=[vmem, vmem],
+        out_specs=pl.BlockSpec(memory_space=pltpu.HBM),
+        out_shape=jax.ShapeDtypeStruct(square.shape, F32),
         scratch_shapes=[
             pltpu.VMEM(square.shape, F32),
-            pltpu.SemaphoreType.DMA((square.shape[0] // TILE,)),
+            pltpu.SemaphoreType.DMA((rows // TILE + 1,)),
         ],
         compiler_params=pltpu.CompilerParams(vmem_limit_bytes=8 * 2**20),
         cost_estimate=pl.CostEstimate(
             flops=8 * square.size, bytes_accessed=8 * square.size, transcendentals=2 * square.size
         ),
-        name="late_relays",
-    )(square, par, relay_rate)
+        name="relay_rates",
+    )(square, par)
 
 
 def per_device(
@@ -496,19 +486,18 @@
     (own,) = after(g, own)
     other = lax.ppermute(own, "case", [(i, i ^ half) for i in range(n_case)])
     ahead = []
-    sizes = [par.shape[0] // 4, par.shape[0] // 4]
-    bit = 1
-    while bit < n_bus // 2:
+    sizes = [par.shape[0] // 12 * i for i in (3, 5)]
+    bits = [2**i for i in range(1, (n_bus - 1).bit_length())]
+    bits.insert(len(bits) - 1, 1)
+    for n, bit in enumerate(bits[:-1]):
         far = swap_over_bus(g, bit)
-        if bit == 2:
+        if n == 1:
             (own,) = after(g, own)
-        if len(ahead) < len(sizes):
-            i = len(ahead)
-            ahead.append(advance(fd_parts, par, sum(sizes[:i]), sizes[i], n_case))
-            (far,) = after(ahead[-1], far)
+        if n < len(sizes):
+            ahead.append(advance(fd_parts, par, sum(sizes[:n]), sizes[n], n_case))
+            (far,) = after(ahead[n], far)
         g = g + far
-        bit *= 2
-    g_far = swap_over_bus(g, n_bus // 2)
+    g_far = swap_over_bus(g, bits[-1])
     (other,) = after(g, other)
     edges = []
     for piece, flops in ((own, 2**29), (other, 1)):
@@ -520,14 +509,14 @@
             order = order + [m ^ bit for m in order]
             bit //= 2
         edges.append(boundary_columns(order, pick, pieces, flops))
-    voltage, relay_rate, square, worst = screen_branches(
+    voltage, square, worst = screen_branches(
         g, g_far, case_rows(tie_x[None], fault_z[None]), par, fd, edges, ahead, n_case
     )
     others = [
         lax.ppermute(worst, "case", [(i, i ^ m) for i in range(n_case)])
         for m in range(n_case - 1, 0, -1)
     ]
-    relay_rate = late_relays(square, par, relay_rate)
+    relay_rate = relay_rates(square, par)
     half_power, factor = curve_constants(curve)
     worst = functools.reduce(jnp.maximum, others, worst).reshape(-1)
     worst_rate = relay_of_square(worst, half_power, 1.0 / (factor * tds))

time: 36.4 us -> 36.7 us (level)
  waiting for transfers between devices: 2.1 us -> 0.83 us
  Pallas kernels: 19.4 us -> 20.3 us
  starting transfers between devices: 13.2 us -> 13.8 us
    ppermute x1, waiting for transfers between devices: 1.3 us -> 0.12 us  [per_device(): other = lax.ppermute(own, 'case', [(i, i ^ half) for i in range(n_case)])]
    pallas_call x2, Pallas kernels: 3.79 us -> 4.93 us  [advance(): pl.pallas_call(functools.partial(advance_kernel, n_case // 2, start), in_...]
    ppermute x1, starting transfers between devices: 0.51 us -> 1.39 us  [per_device(): other = lax.ppermute(own, 'case', [(i, i ^ half) for i in range(n_case)])]
    pallas_call x1, Pallas kernels: 4.11 us -> 3.3 us  [screen_branches(): pl.pallas_call(functools.partial(branch_kernel, n_case // 2, len(ahead)),...]
    ppermute x3, starting transfers between devices: 5.9 us -> 5.16 us  [swap_over_bus(): return lax.ppermute(g, 'bus', [(i, i ^ bit) for i in range(n_bus)])]
    pallas_call x1, Pallas kernels: 1.8 us -> 2.38 us  [relay_rates(): pl.pallas_call(relay_kernel, in_specs=[vmem, vmem], out_specs=pl.BlockSpe...]
    ppermute x2, starting transfers between devices: 0.01 us -> 0.45 us  [per_device(): pieces = pieces + [lax.ppermute(x, 'case', swap) for x in pieces]]
  transfers between devices with their start and end apart: 10 -> 10, of which waited for: 4 -> 3; matrix products, arithmetic and copies ran while one was open for 0% -> 0% of each run, Pallas kernels for 38% -> 42%
where the time goes in v5:
time: 36.7 us; the launch traced here: 36.5 us
  Pallas kernels  20.3 us (55%)
  starting transfers between devices  13.8 us (38%)
  between operations  0.85 us (2%)
  waiting for transfers between devices  0.83 us (2%)
  other arithmetic  0.64 us (2%)
    pallas_call x1, Pallas kernels, pick_columns(): pl.pallas_call(functools.partial(columns_kernel, n_case // 2), in_specs=[...  6.57 us
    ppermute x3, starting transfers between devices, swap_over_bus(): return lax.ppermute(g, 'bus', [(i, i ^ bit) for i in range(n_bus)])  5.16 us
    pallas_call x2, Pallas kernels, advance(): pl.pallas_call(functools.partial(advance_kernel, n_case // 2, start), in_...  4.93 us
    ppermute x1, starting transfers between devices, per_device(): own = lax.ppermute(send, ('bus', 'case'), pairs)  4.86 us
    pallas_call x1, Pallas kernels, screen_branches(): pl.pallas_call(functools.partial(branch_kernel, n_case // 2, len(ahead)),...  3.3 us
    pallas_call x1, Pallas kernels, relay_rates(): pl.pallas_call(relay_kernel, in_specs=[vmem, vmem], out_specs=pl.BlockSpe...  2.38 us
    ppermute x3, starting transfers between devices, per_device(): lax.ppermute(worst, 'case', [(i, i ^ m) for i in range(n_case)])  1.93 us
    pallas_call x1, Pallas kernels, stage(): pl.pallas_call(functools.partial(stage_kernel, half), in_specs=[pl.BlockS...  1.63 us
  transfers between devices with their start and end apart: 10, of which 3 were waited for; matrix products, arithmetic and copies ran while one was open for 0% of the time, Pallas kernels for 42%

profile of v5, /device:TPU:0, one launch (start us, length us, event | category | flops | bytes accessed | tf_op | source)
XLA Modules:
  0.0 36.5 jit_solution(5513157224042996935)
XLA Ops:
  0.6 0.0 copy-start
  0.6 0.0 copy-start.1
  0.7 0.0 copy-start.2
  0.7 1.6 %stage.1 = (f32[64,1024]{1,0:T(8,128)S(1)}, f32[512,1024]{1,0:T(8,128)S(1)}, bf16[1024,1024]{1,0:T(8,128)(2,1)S(1)}) custom-call(f32[1024,1024]{1,0:T(8,128)} %z_hbm.3, s32[8,2,128]{2,1,0:T(2,128)} %lists_hbm.1, s32[1,512]{1,0:T(1,128)} %bitcast.24, s32[2,512]{1,0:T(2,128)} %bitcast.22), custom_call_target="tpu_custom_call" | custom-call | tf_op jit(solution)/shard_map/stage/pallas_call | solution.py:75
  2.3 4.9 %collective-permute-start.3 = (f32[64,1024]{1,0:T(8,128)S(1)}, f32[64,1024]{1,0:T(8,128)S(1)}, u32[]{:S(2)}, u32[]{:S(2)}) collective-permute-start(f32[64,1024]{1,0:T(8,128)S(1)} %get-tuple-element.28), channel_id=1, source_target_pairs={{0,4},{1,5},{4,8},{5,9},{6,2},{7,3},{8,12},{9,13},{10,6},{11,7},{1... | collective-permute-start | bytes 786440 | tf_op jit(solution)/shard_map/ppermute | solution.py:464
  7.2 0.0 copy-done
  7.2 0.0 copy-done.1
  7.2 0.0 copy-done.2
  7.2 6.6 %pick_columns.1 = (f32[1024,1024]{1,0:T(8,128)S(1)}, f32[4,512]{1,0:T(4,128)S(1)}, f32[1536,8]{1,0:T(8,128)S(1)}, bf16[1024,1024]{1,0:T(8,128)(2,1)S(1)}, bf16[1024,1024]{1,0:T(8,128)(2,1)S(1)}) custom-call(f32[512,1024]{1,0:T(8,128)S(1)} %get-tuple-element.19.z_ref, bf16[1024,1024]{1,0:T(8,128)(2,1)S(1)} %get-tuple-element.20.pick, s32[1,512]{1,0:T(1,128)S(1)} %bitcast.25, ...), custom_call_target="tpu_custom_call" | custom-call | tf_op jit(solution)/shard_map/pick_columns/pallas_call | solution.py:200
  13.8 1.6 %collective-permute-start = (f32[4,512]{1,0:T(4,128)S(1)}, f32[4,512]{1,0:T(4,128)S(1)}, u32[]{:S(2)}, u32[]{:S(2)}) collective-permute-start(f32[4,512]{1,0:T(4,128)S(1)} %get-tuple-element.21), channel_id=1, source_target_pairs={{0,8},{4,12},{8,0},{12,4},{16,24},{20,28},{24,16},{28,20},{1,9},{5... | collective-permute-start | bytes 24584 | tf_op jit(solution)/shard_map/ppermute | solution.py:481
  15.4 0.0 collective-permute-done.3.refs_0_
  15.4 1.4 %collective-permute-start.5 = (f32[64,1024]{1,0:T(8,128)S(1)}, f32[64,1024]{1,0:T(8,128)S(1)}, u32[]{:S(2)}, u32[]{:S(2)}) collective-permute-start(f32[64,1024]{1,0:T(8,128)S(1)} %collective-permute-done.3.refs_0_), channel_id=1, source_target_pairs={{0,2},{1,3},{2,0},{3,1},{4,6},{5,7},{6,4},{7,5},{8,10},{9,11},{10,... | collective-permute-start | bytes 786440 | tf_op jit(solution)/shard_map/ppermute | solution.py:487
  16.8 1.9 %advance.2.refs_0_ = f32[384,1024]{1,0:T(8,128)S(1)} custom-call(bf16[1024,1024]{1,0:T(8,128)(2,1)S(1)} %get-tuple-element.22.fd_hi, bf16[1024,1024]{1,0:T(8,128)(2,1)S(1)} %get-tuple-element.23.fd_lo, f32[1536,8]{1,0:T(8,128)S(1)} %get-tuple-element.24.par_ref), custom_call_target="tpu_custom_call" | custom-call | flops 1610612736 | bytes 3145728 | tf_op jit(solution)/shard_map/advance/pallas_call | solution.py:248
  18.7 0.0 collective-permute-done
  18.7 0.0 copy-start.3
  18.7 0.0 copy-start.4
  18.8 0.9 %collective-permute-start.1 = (f32[4,512]{1,0:T(4,128)S(1)}, f32[4,512]{1,0:T(4,128)S(1)}, u32[]{:S(2)}, u32[]{:S(2)}) collective-permute-start(f32[4,512]{1,0:T(4,128)S(1)} %add.14), channel_id=1, source_target_pairs={{0,4},{4,0},{8,12},{12,8},{16,20},{20,16},{24,28},{28,24},{1,5},{5... | collective-permute-start | bytes 24584 | tf_op jit(solution)/shard_map/ppermute | solution.py:481
  19.6 3.0 %advance.3.refs_1_ = f32[640,1024]{1,0:T(8,128)S(1)} custom-call(bf16[1024,1024]{1,0:T(8,128)(2,1)S(1)} %get-tuple-element.22.fd_hi, bf16[1024,1024]{1,0:T(8,128)(2,1)S(1)} %get-tuple-element.23.fd_lo, f32[1536,8]{1,0:T(8,128)S(1)} %get-tuple-element.24.par_ref), custom_call_target="tpu_custom_call" | custom-call | flops 2684354560 | bytes 5242880 | tf_op jit(solution)/shard_map/advance/pallas_call | solution.py:248
  22.7 0.0 collective-permute-done.1
  22.7 0.1 collective-permute-start.4
  22.8 0.1 collective-permute-done.5.refs_0_
  22.9 0.4 %collective-permute-start.6 = (f32[64,1024]{1,0:T(8,128)S(1)}, f32[64,1024]{1,0:T(8,128)S(1)}, u32[]{:S(2)}, u32[]{:S(2)}) collective-permute-start(f32[64,1024]{1,0:T(8,128)S(1)} %collective-permute-done.5.refs_0_), channel_id=1, source_target_pairs={{0,1},{1,0},{2,3},{3,2},{4,5},{5,4},{6,7},{7,6},{8,9},{9,8},{10,11... | collective-permute-start | bytes 786440 | tf_op jit(solution)/shard_map/ppermute | solution.py:508
  23.3 0.0 copy-done.3
  23.3 0.0 copy-done.4
  23.3 2.7 %collective-permute-start.2 = (f32[4,512]{1,0:T(4,128)S(1)}, f32[4,512]{1,0:T(4,128)S(1)}, u32[]{:S(2)}, u32[]{:S(2)}) collective-permute-start(f32[4,512]{1,0:T(4,128)S(1)} %add.15.g_ref), channel_id=1, source_target_pairs={{0,16},{4,20},{8,24},{12,28},{16,0},{20,4},{24,8},{28,12},{1,17},{... | collective-permute-start | bytes 24584 | tf_op jit(solution)/shard_map/ppermute | solution.py:481
  25.9 0.0 collective-permute-done.4.refs_1_
  26.0 0.7 %boundary_columns.2.near_ref = f32[128,1024]{1,0:T(8,128)S(1)} custom-call(bf16[1024,1024]{1,0:T(8,128)(2,1)S(1)} %get-tuple-element.20.pick, f32[64,1024]{1,0:T(8,128)S(1)} %collective-permute-done.3.refs_0_, f32[64,1024]{1,0:T(8,128)S(1)} %collective-permute-done.4.refs_1_), custom_call_target="tpu_custom_call" | custom-call | flops 536870912 | bytes 1 | tf_op jit(solution)/shard_map/boundary_columns/pallas_call | solution.py:277
  26.7 0.0 collective-permute-done.6.refs_1_
  26.7 0.7 %boundary_columns.3.far_edge_ref = f32[128,1024]{1,0:T(8,128)S(1)} custom-call(bf16[1024,1024]{1,0:T(8,128)(2,1)S(1)} %get-tuple-element.20.pick, f32[64,1024]{1,0:T(8,128)S(1)} %collective-permute-done.5.refs_0_, f32[64,1024]{1,0:T(8,128)S(1)} %collective-permute-done.6.refs_1_), custom_call_target="tpu_custom_call" | custom-call | flops 1 | bytes 1 | tf_op jit(solution)/shard_map/boundary_columns/pallas_call | solution.py:277
  27.5 0.4 %collective-permute-done.2.far_ref = f32[4,512]{1,0:T(4,128)S(1)} collective-permute-done((f32[4,512]{1,0:T(4,128)S(1)}, f32[4,512]{1,0:T(4,128)S(1)}, u32[]{:S(2)}, u32[]{:S(2)}) %collective-permute-start.2) | collective-permute-done | bytes 8224 | tf_op jit(solution)/shard_map/ppermute | solution.py:481
  27.9 3.3 %screen_branches.1 = (f32[1024,512]{1,0:T(8,128)}, f32[1536,512]{1,0:T(8,128)S(1)}, f32[12,128]{1,0:T(8,128)S(1)}) custom-call(f32[4,512]{1,0:T(4,128)S(1)} %add.15.g_ref, f32[4,512]{1,0:T(4,128)S(1)} %collective-permute-done.2.far_ref, f32[2,512]{1,0:T(2,128)S(1)} %case_rows.1.case_ref, f32[1536,8]{1,0:T(8,128)S(1)} %get-tuple-element.24.par_ref, ...), custom_call_target="tpu_custom_call" | custom-call | tf_op jit(solution)/shard_map/screen_branches/pallas_call | solution.py:383
  31.2 0.1 collective-permute-start.9
  31.3 1.5 %collective-permute-start.8 = (f32[12,128]{1,0:T(8,128)S(1)}, f32[12,128]{1,0:T(8,128)S(1)}, u32[]{:S(2)}, u32[]{:S(2)}) collective-permute-start(f32[12,128]{1,0:T(8,128)S(1)} %get-tuple-element.34), channel_id=1, source_target_pairs={{0,2},{1,3},{2,0},{3,1},{4,6},{5,7},{6,4},{7,5},{8,10},{9,11},{10,... | collective-permute-start | bytes 18440 | tf_op jit(solution)/shard_map/ppermute | solution.py:516
  32.7 0.4 %collective-permute-start.7 = (f32[12,128]{1,0:T(8,128)S(1)}, f32[12,128]{1,0:T(8,128)S(1)}, u32[]{:S(2)}, u32[]{:S(2)}) collective-permute-start(f32[12,128]{1,0:T(8,128)S(1)} %get-tuple-element.34), channel_id=1, source_target_pairs={{0,3},{1,2},{2,1},{3,0},{4,7},{5,6},{6,5},{7,4},{8,11},{9,10},{10,... | collective-permute-start | bytes 18440 | tf_op jit(solution)/shard_map/ppermute | solution.py:516
  33.1 0.0 copy-start.5
  33.1 0.0 copy-start.6
  33.1 2.4 %relay_rates.1 = f32[1536,512]{1,0:T(8,128)} custom-call(f32[1536,512]{1,0:T(8,128)S(1)} %get-tuple-element.33.square_ref, f32[1536,8]{1,0:T(8,128)S(1)} %get-tuple-element.24.par_ref), custom_call_target="tpu_custom_call" | custom-call | flops 6291456 | bytes 6291456 | tf_op jit(solution)/shard_map/relay_rates/pallas_call | solution.py:423
  35.5 0.0 collective-permute-done.9
  35.5 0.0 collective-permute-done.8
  35.6 0.3 collective-permute-done.7
  35.8 0.0 copy-done.5
  35.8 0.0 copy-done.6
  35.8 0.6 %fusion.4 = f32[1536]{0:T(1024)} fusion(f32[1536]{0:T(1024)S(1)} %copy-done.5, f32[12,128]{1,0:T(8,128)S(1)} %collective-permute-done.9, f32[12,128]{1,0:T(8,128)S(1)} %collective-permute-done.8, f32[12,128]{1,0:T(8,128)S(1)} %get-tuple-element.34, f32[12,128]{1,0:T(8,128)S(1)} %collective-permute-done.7, s32[1536]{0:T(1024)S(1)} %copy-done.6), kind=kLoop, calls=%fused_computation.5 | loop fusion | flops 27648 | bytes 43008 | tf_op jit(solution)/shard_map/mul | solution.py:290
  (3 shorter events, 0.0 us)
Async XLA Ops:
  0.6 6.5 %copy-start = (s32[512,2]{0,1:T(2,128)S(1)}, s32[512,2]{0,1:T(2,128)}, u32[]{:S(2)}) copy-start(s32[512,2]{0,1:T(2,128)} %param.15) | copy-start | bytes 12292
  0.6 6.5 %copy-start.1 = (s32[512]{0:T(512)S(1)}, s32[512]{0:T(512)}, u32[]{:S(2)}) copy-start(s32[512]{0:T(512)} %param.14) | copy-start | bytes 6148
  0.7 6.5 %copy-start.2 = (s32[1024]{0:T(1024)S(1)}, s32[1024]{0:T(1024)}, u32[]{:S(2)}) copy-start(s32[1024]{0:T(1024)} %param.13) | copy-start | bytes 12292
  2.3 13.1 %collective-permute-start.3 = (f32[64,1024]{1,0:T(8,128)S(1)}, f32[64,1024]{1,0:T(8,128)S(1)}, u32[]{:S(2)}, u32[]{:S(2)}) collective-permute-start(f32[64,1024]{1,0:T(8,128)S(1)} %get-tuple-element.28), channel_id=1, source_target_pairs={{0,4},{1,5},{4,8},{5,9},{6,2},{7,3},{8,12},{9,13},{10,6},{11,7},{1... | collective-permute-start | bytes 786440 | tf_op jit(solution)/shard_map/ppermute | solution.py:464
  13.8 4.9 %collective-permute-start = (f32[4,512]{1,0:T(4,128)S(1)}, f32[4,512]{1,0:T(4,128)S(1)}, u32[]{:S(2)}, u32[]{:S(2)}) collective-permute-start(f32[4,512]{1,0:T(4,128)S(1)} %get-tuple-element.21), channel_id=1, source_target_pairs={{0,8},{4,12},{8,0},{12,4},{16,24},{20,28},{24,16},{28,20},{1,9},{5... | collective-permute-start | bytes 24584 | tf_op jit(solution)/shard_map/ppermute | solution.py:481
  15.4 7.5 %collective-permute-start.5 = (f32[64,1024]{1,0:T(8,128)S(1)}, f32[64,1024]{1,0:T(8,128)S(1)}, u32[]{:S(2)}, u32[]{:S(2)}) collective-permute-start(f32[64,1024]{1,0:T(8,128)S(1)} %collective-permute-done.3.refs_0_), channel_id=1, source_target_pairs={{0,2},{1,3},{2,0},{3,1},{4,6},{5,7},{6,4},{7,5},{8,10},{9,11},{10,... | collective-permute-start | bytes 786440 | tf_op jit(solution)/shard_map/ppermute | solution.py:487
  18.7 4.5 %copy-start.3 = (f32[512]{0:T(512)S(1)}, f32[512]{0:T(512)}, u32[]{:S(2)}) copy-start(f32[512]{0:T(512)} %param.16) | copy-start | bytes 6148
  18.7 4.5 %copy-start.4 = (f32[512]{0:T(512)S(1)}, f32[512]{0:T(512)}, u32[]{:S(2)}) copy-start(f32[512]{0:T(512)} %param.17) | copy-start | bytes 6148
  18.8 3.9 %collective-permute-start.1 = (f32[4,512]{1,0:T(4,128)S(1)}, f32[4,512]{1,0:T(4,128)S(1)}, u32[]{:S(2)}, u32[]{:S(2)}) collective-permute-start(f32[4,512]{1,0:T(4,128)S(1)} %add.14), channel_id=1, source_target_pairs={{0,4},{4,0},{8,12},{12,8},{16,20},{20,16},{24,28},{28,24},{1,5},{5... | collective-permute-start | bytes 24584 | tf_op jit(solution)/shard_map/ppermute | solution.py:481
  22.7 3.3 %collective-permute-start.4 = (f32[64,1024]{1,0:T(8,128)S(1)}, f32[64,1024]{1,0:T(8,128)S(1)}, u32[]{:S(2)}, u32[]{:S(2)}) collective-permute-start(f32[64,1024]{1,0:T(8,128)S(1)} %collective-permute-done.3.refs_0_), channel_id=1, source_target_pairs={{0,1},{1,0},{2,3},{3,2},{4,5},{5,4},{6,7},{7,6},{8,9},{9,8},{10,11... | collective-permute-start | bytes 786440 | tf_op jit(solution)/shard_map/ppermute | solution.py:508
  22.9 3.8 %collective-permute-start.6 = (f32[64,1024]{1,0:T(8,128)S(1)}, f32[64,1024]{1,0:T(8,128)S(1)}, u32[]{:S(2)}, u32[]{:S(2)}) collective-permute-start(f32[64,1024]{1,0:T(8,128)S(1)} %collective-permute-done.5.refs_0_), channel_id=1, source_target_pairs={{0,1},{1,0},{2,3},{3,2},{4,5},{5,4},{6,7},{7,6},{8,9},{9,8},{10,11... | collective-permute-start | bytes 786440 | tf_op jit(solution)/shard_map/ppermute | solution.py:508
  23.3 4.6 %collective-permute-start.2 = (f32[4,512]{1,0:T(4,128)S(1)}, f32[4,512]{1,0:T(4,128)S(1)}, u32[]{:S(2)}, u32[]{:S(2)}) collective-permute-start(f32[4,512]{1,0:T(4,128)S(1)} %add.15.g_ref), channel_id=1, source_target_pairs={{0,16},{4,20},{8,24},{12,28},{16,0},{20,4},{24,8},{28,12},{1,17},{... | collective-permute-start | bytes 24584 | tf_op jit(solution)/shard_map/ppermute | solution.py:481
  31.2 4.3 %collective-permute-start.9 = (f32[12,128]{1,0:T(8,128)S(1)}, f32[12,128]{1,0:T(8,128)S(1)}, u32[]{:S(2)}, u32[]{:S(2)}) collective-permute-start(f32[12,128]{1,0:T(8,128)S(1)} %get-tuple-element.34), channel_id=1, source_target_pairs={{0,1},{1,0},{2,3},{3,2},{4,5},{5,4},{6,7},{7,6},{8,9},{9,8},{10,11... | collective-permute-start | bytes 18440 | tf_op jit(solution)/shard_map/ppermute | solution.py:516
  31.3 4.3 %collective-permute-start.8 = (f32[12,128]{1,0:T(8,128)S(1)}, f32[12,128]{1,0:T(8,128)S(1)}, u32[]{:S(2)}, u32[]{:S(2)}) collective-permute-start(f32[12,128]{1,0:T(8,128)S(1)} %get-tuple-element.34), channel_id=1, source_target_pairs={{0,2},{1,3},{2,0},{3,1},{4,6},{5,7},{6,4},{7,5},{8,10},{9,11},{10,... | collective-permute-start | bytes 18440 | tf_op jit(solution)/shard_map/ppermute | solution.py:516
  32.7 3.1 %collective-permute-start.7 = (f32[12,128]{1,0:T(8,128)S(1)}, f32[12,128]{1,0:T(8,128)S(1)}, u32[]{:S(2)}, u32[]{:S(2)}) collective-permute-start(f32[12,128]{1,0:T(8,128)S(1)} %get-tuple-element.34), channel_id=1, source_target_pairs={{0,3},{1,2},{2,1},{3,0},{4,7},{5,6},{6,5},{7,4},{8,11},{9,10},{10,... | collective-permute-start | bytes 18440 | tf_op jit(solution)/shard_map/ppermute | solution.py:516
  33.1 2.7 %copy-start.5 = (f32[1536]{0:T(1024)S(1)}, f32[1536]{0:T(1024)}, u32[]{:S(2)}) copy-start(f32[1536]{0:T(1024)} %param.22) | copy-start | bytes 18436
  33.1 2.7 %copy-start.6 = (s32[1536]{0:T(1024)S(1)}, s32[1536]{0:T(1024)}, u32[]{:S(2)}) copy-start(s32[1536]{0:T(1024)} %param.23) | copy-start | bytes 18436

commit v6 on v5

--- a/solution.py
+++ b/solution.py
@@ -63,7 +63,8 @@
     base = (my_case % half) * piece
     first = rim * TILE
     for i in range(piece):
-        send_ref[pl.ds(i, 1), :] = z_ref[pl.ds(lists[1 - down, base + i] - first, 1), :]
+        row = jnp.clip(lists[1 - down, base + i] - first, 0, TILE - 1)
+        send_ref[pl.ds(i, 1), :] = z_ref[pl.ds(row, 1), :]
     for load in loads[4:]:
         load.wait()
 
@@ -486,9 +487,8 @@
     (own,) = after(g, own)
     other = lax.ppermute(own, "case", [(i, i ^ half) for i in range(n_case)])
     ahead = []
-    sizes = [par.shape[0] // 12 * i for i in (3, 5)]
-    bits = [2**i for i in range(1, (n_bus - 1).bit_length())]
-    bits.insert(len(bits) - 1, 1)
+    sizes = [par.shape[0] // 12 * i for i in (3, 3)]
+    bits = [2**i for i in range((n_bus - 1).bit_length())]
     for n, bit in enumerate(bits[:-1]):
         far = swap_over_bus(g, bit)
         if n == 1:

time: 36.7 us -> 36.5 us (level)
  waiting for transfers between devices: 0.83 us -> 1.93 us
  Pallas kernels: 20.3 us -> 19.7 us
  starting transfers between devices: 13.8 us -> 13.2 us
    ppermute x1, waiting for transfers between devices: 0.12 us -> 1.3 us  [per_device(): other = lax.ppermute(own, 'case', [(i, i ^ half) for i in range(n_case)])]
    pallas_call x2, Pallas kernels: 4.93 us -> 3.79 us  [advance(): pl.pallas_call(functools.partial(advance_kernel, n_case // 2, start), in_...]
    ppermute x1, starting transfers between devices: 1.39 us -> 0.51 us  [per_device(): other = lax.ppermute(own, 'case', [(i, i ^ half) for i in range(n_case)])]
    ppermute x3, starting transfers between devices: 5.16 us -> 5.9 us  [swap_over_bus(): return lax.ppermute(g, 'bus', [(i, i ^ bit) for i in range(n_bus)])]
    pallas_call x1, Pallas kernels: 3.3 us -> 3.83 us  [screen_branches(): pl.pallas_call(functools.partial(branch_kernel, n_case // 2, len(ahead)),...]
    ppermute x2, starting transfers between devices: 0.45 us -> 0.01 us  [per_device(): pieces = pieces + [lax.ppermute(x, 'case', swap) for x in pieces]]
  transfers between devices with their start and end apart: 10 -> 10, of which waited for: 3 -> 3; matrix products, arithmetic and copies ran while one was open for 0% -> 0% of each run, Pallas kernels for 42% -> 39%
where the time goes in v6:
time: 36.5 us; the launch traced here: 36.4 us
  Pallas kernels  19.7 us (54%)
  starting transfers between devices  13.2 us (36%)
  waiting for transfers between devices  1.93 us (5%)
  between operations  0.86 us (2%)
  other arithmetic  0.64 us (2%)
    pallas_call x1, Pallas kernels, pick_columns(): pl.pallas_call(functools.partial(columns_kernel, n_case // 2), in_specs=[...  6.56 us
    ppermute x3, starting transfers between devices, swap_over_bus(): return lax.ppermute(g, 'bus', [(i, i ^ bit) for i in range(n_bus)])  5.9 us
    ppermute x1, starting transfers between devices, per_device(): own = lax.ppermute(send, ('bus', 'case'), pairs)  4.86 us
    pallas_call x1, Pallas kernels, screen_branches(): pl.pallas_call(functools.partial(branch_kernel, n_case // 2, len(ahead)),...  3.83 us
    pallas_call x2, Pallas kernels, advance(): pl.pallas_call(functools.partial(advance_kernel, n_case // 2, start), in_...  3.79 us
    pallas_call x1, Pallas kernels, relay_rates(): pl.pallas_call(relay_kernel, in_specs=[vmem, vmem], out_specs=pl.BlockSpe...  2.38 us
    ppermute x3, starting transfers between devices, per_device(): lax.ppermute(worst, 'case', [(i, i ^ m) for i in range(n_case)])  1.93 us
    pallas_call x1, Pallas kernels, stage(): pl.pallas_call(functools.partial(stage_kernel, half), in_specs=[pl.BlockS...  1.63 us
  transfers between devices with their start and end apart: 10, of which 3 were waited for; matrix products, arithmetic and copies ran while one was open for 0% of the time, Pallas kernels for 39%

profile of v6, /device:TPU:0, one launch (start us, length us, event | category | flops | bytes accessed | tf_op | source)
XLA Modules:
  0.0 36.4 jit_solution(10882577251636177116)
XLA Ops:
  0.6 0.0 copy-start
  0.6 0.0 copy-start.1
  0.7 0.0 copy-start.2
  0.7 1.6 %stage.1 = (f32[64,1024]{1,0:T(8,128)S(1)}, f32[512,1024]{1,0:T(8,128)S(1)}, bf16[1024,1024]{1,0:T(8,128)(2,1)S(1)}) custom-call(f32[1024,1024]{1,0:T(8,128)} %z_hbm.3, s32[8,2,128]{2,1,0:T(2,128)} %lists_hbm.1, s32[1,512]{1,0:T(1,128)} %bitcast.24, s32[2,512]{1,0:T(2,128)} %bitcast.22), custom_call_target="tpu_custom_call" | custom-call | tf_op jit(solution)/shard_map/stage/pallas_call | solution.py:76
  2.3 4.9 %collective-permute-start.3 = (f32[64,1024]{1,0:T(8,128)S(1)}, f32[64,1024]{1,0:T(8,128)S(1)}, u32[]{:S(2)}, u32[]{:S(2)}) collective-permute-start(f32[64,1024]{1,0:T(8,128)S(1)} %get-tuple-element.28), channel_id=1, source_target_pairs={{0,4},{1,5},{4,8},{5,9},{6,2},{7,3},{8,12},{9,13},{10,6},{11,7},{1... | collective-permute-start | bytes 786440 | tf_op jit(solution)/shard_map/ppermute | solution.py:465
  7.2 0.0 copy-done
  7.2 0.0 copy-done.1
  7.2 0.0 copy-done.2
  7.2 6.6 %pick_columns.1 = (f32[1024,1024]{1,0:T(8,128)S(1)}, f32[4,512]{1,0:T(4,128)S(1)}, f32[1536,8]{1,0:T(8,128)S(1)}, bf16[1024,1024]{1,0:T(8,128)(2,1)S(1)}, bf16[1024,1024]{1,0:T(8,128)(2,1)S(1)}) custom-call(f32[512,1024]{1,0:T(8,128)S(1)} %get-tuple-element.19.z_ref, bf16[1024,1024]{1,0:T(8,128)(2,1)S(1)} %get-tuple-element.20.pick, s32[1,512]{1,0:T(1,128)S(1)} %bitcast.25, ...), custom_call_target="tpu_custom_call" | custom-call | tf_op jit(solution)/shard_map/pick_columns/pallas_call | solution.py:201
  13.8 1.6 %collective-permute-start = (f32[4,512]{1,0:T(4,128)S(1)}, f32[4,512]{1,0:T(4,128)S(1)}, u32[]{:S(2)}, u32[]{:S(2)}) collective-permute-start(f32[4,512]{1,0:T(4,128)S(1)} %get-tuple-element.21), channel_id=1, source_target_pairs={{0,4},{4,0},{8,12},{12,8},{16,20},{20,16},{24,28},{28,24},{1,5},{5... | collective-permute-start | bytes 24584 | tf_op jit(solution)/shard_map/ppermute | solution.py:482
  15.4 0.0 collective-permute-done.3.refs_0_
  15.4 0.5 %collective-permute-start.5 = (f32[64,1024]{1,0:T(8,128)S(1)}, f32[64,1024]{1,0:T(8,128)S(1)}, u32[]{:S(2)}, u32[]{:S(2)}) collective-permute-start(f32[64,1024]{1,0:T(8,128)S(1)} %collective-permute-done.3.refs_0_), channel_id=1, source_target_pairs={{0,2},{1,3},{2,0},{3,1},{4,6},{5,7},{6,4},{7,5},{8,10},{9,11},{10,... | collective-permute-start | bytes 786440 | tf_op jit(solution)/shard_map/ppermute | solution.py:488
  15.9 1.9 %advance.2.refs_0_ = f32[384,1024]{1,0:T(8,128)S(1)} custom-call(bf16[1024,1024]{1,0:T(8,128)(2,1)S(1)} %get-tuple-element.22.fd_hi, bf16[1024,1024]{1,0:T(8,128)(2,1)S(1)} %get-tuple-element.23.fd_lo, f32[1536,8]{1,0:T(8,128)S(1)} %get-tuple-element.24.par_ref), custom_call_target="tpu_custom_call" | custom-call | flops 1610612736 | bytes 3145728 | tf_op jit(solution)/shard_map/advance/pallas_call | solution.py:249
  17.8 0.0 collective-permute-done
  17.8 0.0 copy-start.3
  17.8 0.0 copy-start.4
  17.8 1.6 %collective-permute-start.1 = (f32[4,512]{1,0:T(4,128)S(1)}, f32[4,512]{1,0:T(4,128)S(1)}, u32[]{:S(2)}, u32[]{:S(2)}) collective-permute-start(f32[4,512]{1,0:T(4,128)S(1)} %add.14), channel_id=1, source_target_pairs={{0,8},{4,12},{8,0},{12,4},{16,24},{20,28},{24,16},{28,20},{1,9},{5... | collective-permute-start | bytes 24584 | tf_op jit(solution)/shard_map/ppermute | solution.py:482
  19.5 1.9 %advance.3.refs_1_ = f32[384,1024]{1,0:T(8,128)S(1)} custom-call(bf16[1024,1024]{1,0:T(8,128)(2,1)S(1)} %get-tuple-element.22.fd_hi, bf16[1024,1024]{1,0:T(8,128)(2,1)S(1)} %get-tuple-element.23.fd_lo, f32[1536,8]{1,0:T(8,128)S(1)} %get-tuple-element.24.par_ref), custom_call_target="tpu_custom_call" | custom-call | flops 1610612736 | bytes 3145728 | tf_op jit(solution)/shard_map/advance/pallas_call | solution.py:249
  21.4 0.2 collective-permute-done.1
  21.6 0.0 collective-permute-start.4
  21.6 1.3 %collective-permute-done.5.refs_0_ = f32[64,1024]{1,0:T(8,128)S(1)} collective-permute-done((f32[64,1024]{1,0:T(8,128)S(1)}, f32[64,1024]{1,0:T(8,128)S(1)}, u32[]{:S(2)}, u32[]{:S(2)}) %collective-permute-start.5) | collective-permute-done | bytes 262176 | tf_op jit(solution)/shard_map/ppermute | solution.py:488
  22.9 0.0 collective-permute-start.6
  22.9 0.0 copy-done.3
  22.9 0.0 copy-done.4
  22.9 2.7 %collective-permute-start.2 = (f32[4,512]{1,0:T(4,128)S(1)}, f32[4,512]{1,0:T(4,128)S(1)}, u32[]{:S(2)}, u32[]{:S(2)}) collective-permute-start(f32[4,512]{1,0:T(4,128)S(1)} %add.15.g_ref), channel_id=1, source_target_pairs={{0,16},{4,20},{8,24},{12,28},{16,0},{20,4},{24,8},{28,12},{1,17},{... | collective-permute-start | bytes 24584 | tf_op jit(solution)/shard_map/ppermute | solution.py:482
  25.5 0.0 collective-permute-done.4.refs_1_
  25.5 0.7 %boundary_columns.2.near_ref = f32[128,1024]{1,0:T(8,128)S(1)} custom-call(bf16[1024,1024]{1,0:T(8,128)(2,1)S(1)} %get-tuple-element.20.pick, f32[64,1024]{1,0:T(8,128)S(1)} %collective-permute-done.3.refs_0_, f32[64,1024]{1,0:T(8,128)S(1)} %collective-permute-done.4.refs_1_), custom_call_target="tpu_custom_call" | custom-call | flops 536870912 | bytes 1 | tf_op jit(solution)/shard_map/boundary_columns/pallas_call | solution.py:278
  26.3 0.0 collective-permute-done.6.refs_1_
  26.3 0.8 %boundary_columns.3.far_edge_ref = f32[128,1024]{1,0:T(8,128)S(1)} custom-call(bf16[1024,1024]{1,0:T(8,128)(2,1)S(1)} %get-tuple-element.20.pick, f32[64,1024]{1,0:T(8,128)S(1)} %collective-permute-done.5.refs_0_, f32[64,1024]{1,0:T(8,128)S(1)} %collective-permute-done.6.refs_1_), custom_call_target="tpu_custom_call" | custom-call | flops 1 | bytes 1 | tf_op jit(solution)/shard_map/boundary_columns/pallas_call | solution.py:278
  27.1 0.4 %collective-permute-done.2.far_ref = f32[4,512]{1,0:T(4,128)S(1)} collective-permute-done((f32[4,512]{1,0:T(4,128)S(1)}, f32[4,512]{1,0:T(4,128)S(1)}, u32[]{:S(2)}, u32[]{:S(2)}) %collective-permute-start.2) | collective-permute-done | bytes 8224 | tf_op jit(solution)/shard_map/ppermute | solution.py:482
  27.5 3.8 %screen_branches.1 = (f32[1024,512]{1,0:T(8,128)}, f32[1536,512]{1,0:T(8,128)S(1)}, f32[12,128]{1,0:T(8,128)S(1)}) custom-call(f32[4,512]{1,0:T(4,128)S(1)} %add.15.g_ref, f32[4,512]{1,0:T(4,128)S(1)} %collective-permute-done.2.far_ref, f32[2,512]{1,0:T(2,128)S(1)} %case_rows.1.case_ref, f32[1536,8]{1,0:T(8,128)S(1)} %get-tuple-element.24.par_ref, ...), custom_call_target="tpu_custom_call" | custom-call | tf_op jit(solution)/shard_map/screen_branches/pallas_call | solution.py:384
  31.3 0.1 collective-permute-start.9
  31.4 0.8 %collective-permute-start.8 = (f32[12,128]{1,0:T(8,128)S(1)}, f32[12,128]{1,0:T(8,128)S(1)}, u32[]{:S(2)}, u32[]{:S(2)}) collective-permute-start(f32[12,128]{1,0:T(8,128)S(1)} %get-tuple-element.34), channel_id=1, source_target_pairs={{0,2},{1,3},{2,0},{3,1},{4,6},{5,7},{6,4},{7,5},{8,10},{9,11},{10,... | collective-permute-start | bytes 18440 | tf_op jit(solution)/shard_map/ppermute | solution.py:516
  32.2 1.1 %collective-permute-start.7 = (f32[12,128]{1,0:T(8,128)S(1)}, f32[12,128]{1,0:T(8,128)S(1)}, u32[]{:S(2)}, u32[]{:S(2)}) collective-permute-start(f32[12,128]{1,0:T(8,128)S(1)} %get-tuple-element.34), channel_id=1, source_target_pairs={{0,3},{1,2},{2,1},{3,0},{4,7},{5,6},{6,5},{7,4},{8,11},{9,10},{10,... | collective-permute-start | bytes 18440 | tf_op jit(solution)/shard_map/ppermute | solution.py:516
  33.3 0.0 copy-start.5
  33.3 0.0 copy-start.6
  33.3 2.4 %relay_rates.1 = f32[1536,512]{1,0:T(8,128)} custom-call(f32[1536,512]{1,0:T(8,128)S(1)} %get-tuple-element.33.square_ref, f32[1536,8]{1,0:T(8,128)S(1)} %get-tuple-element.24.par_ref), custom_call_target="tpu_custom_call" | custom-call | flops 6291456 | bytes 6291456 | tf_op jit(solution)/shard_map/relay_rates/pallas_call | solution.py:424
  35.7 0.0 collective-permute-done.9
  35.7 0.0 collective-permute-done.8
  35.7 0.0 collective-permute-done.7
  35.7 0.0 copy-done.5
  35.7 0.0 copy-done.6
  35.7 0.6 %fusion.4 = f32[1536]{0:T(1024)} fusion(f32[1536]{0:T(1024)S(1)} %copy-done.5, f32[12,128]{1,0:T(8,128)S(1)} %collective-permute-done.9, f32[12,128]{1,0:T(8,128)S(1)} %collective-permute-done.8, f32[12,128]{1,0:T(8,128)S(1)} %get-tuple-element.34, f32[12,128]{1,0:T(8,128)S(1)} %collective-permute-done.7, s32[1536]{0:T(1024)S(1)} %copy-done.6), kind=kLoop, calls=%fused_computation.5 | loop fusion | flops 27648 | bytes 43008 | tf_op jit(solution)/shard_map/mul | solution.py:291
  (3 shorter events, 0.0 us)
Async XLA Ops:
  0.6 6.5 %copy-start = (s32[512,2]{0,1:T(2,128)S(1)}, s32[512,2]{0,1:T(2,128)}, u32[]{:S(2)}) copy-start(s32[512,2]{0,1:T(2,128)} %param.15) | copy-start | bytes 12292
  0.6 6.5 %copy-start.1 = (s32[512]{0:T(512)S(1)}, s32[512]{0:T(512)}, u32[]{:S(2)}) copy-start(s32[512]{0:T(512)} %param.14) | copy-start | bytes 6148
  0.7 6.5 %copy-start.2 = (s32[1024]{0:T(1024)S(1)}, s32[1024]{0:T(1024)}, u32[]{:S(2)}) copy-start(s32[1024]{0:T(1024)} %param.13) | copy-start | bytes 12292
  2.3 13.1 %collective-permute-start.3 = (f32[64,1024]{1,0:T(8,128)S(1)}, f32[64,1024]{1,0:T(8,128)S(1)}, u32[]{:S(2)}, u32[]{:S(2)}) collective-permute-start(f32[64,1024]{1,0:T(8,128)S(1)} %get-tuple-element.28), channel_id=1, source_target_pairs={{0,4},{1,5},{4,8},{5,9},{6,2},{7,3},{8,12},{9,13},{10,6},{11,7},{1... | collective-permute-start | bytes 786440 | tf_op jit(solution)/shard_map/ppermute | solution.py:465
  13.8 4.0 %collective-permute-start = (f32[4,512]{1,0:T(4,128)S(1)}, f32[4,512]{1,0:T(4,128)S(1)}, u32[]{:S(2)}, u32[]{:S(2)}) collective-permute-start(f32[4,512]{1,0:T(4,128)S(1)} %get-tuple-element.21), channel_id=1, source_target_pairs={{0,4},{4,0},{8,12},{12,8},{16,20},{20,16},{24,28},{28,24},{1,5},{5... | collective-permute-start | bytes 24584 | tf_op jit(solution)/shard_map/ppermute | solution.py:482
  15.4 7.5 %collective-permute-start.5 = (f32[64,1024]{1,0:T(8,128)S(1)}, f32[64,1024]{1,0:T(8,128)S(1)}, u32[]{:S(2)}, u32[]{:S(2)}) collective-permute-start(f32[64,1024]{1,0:T(8,128)S(1)} %collective-permute-done.3.refs_0_), channel_id=1, source_target_pairs={{0,2},{1,3},{2,0},{3,1},{4,6},{5,7},{6,4},{7,5},{8,10},{9,11},{10,... | collective-permute-start | bytes 786440 | tf_op jit(solution)/shard_map/ppermute | solution.py:488
  17.8 5.1 %copy-start.3 = (f32[512]{0:T(512)S(1)}, f32[512]{0:T(512)}, u32[]{:S(2)}) copy-start(f32[512]{0:T(512)} %param.16) | copy-start | bytes 6148
  17.8 5.0 %copy-start.4 = (f32[512]{0:T(512)S(1)}, f32[512]{0:T(512)}, u32[]{:S(2)}) copy-start(f32[512]{0:T(512)} %param.17) | copy-start | bytes 6148
  17.8 3.7 %collective-permute-start.1 = (f32[4,512]{1,0:T(4,128)S(1)}, f32[4,512]{1,0:T(4,128)S(1)}, u32[]{:S(2)}, u32[]{:S(2)}) collective-permute-start(f32[4,512]{1,0:T(4,128)S(1)} %add.14), channel_id=1, source_target_pairs={{0,8},{4,12},{8,0},{12,4},{16,24},{20,28},{24,16},{28,20},{1,9},{5... | collective-permute-start | bytes 24584 | tf_op jit(solution)/shard_map/ppermute | solution.py:482
  21.6 4.0 %collective-permute-start.4 = (f32[64,1024]{1,0:T(8,128)S(1)}, f32[64,1024]{1,0:T(8,128)S(1)}, u32[]{:S(2)}, u32[]{:S(2)}) collective-permute-start(f32[64,1024]{1,0:T(8,128)S(1)} %collective-permute-done.3.refs_0_), channel_id=1, source_target_pairs={{0,1},{1,0},{2,3},{3,2},{4,5},{5,4},{6,7},{7,6},{8,9},{9,8},{10,11... | collective-permute-start | bytes 786440 | tf_op jit(solution)/shard_map/ppermute | solution.py:508
  22.9 3.4 %collective-permute-start.6 = (f32[64,1024]{1,0:T(8,128)S(1)}, f32[64,1024]{1,0:T(8,128)S(1)}, u32[]{:S(2)}, u32[]{:S(2)}) collective-permute-start(f32[64,1024]{1,0:T(8,128)S(1)} %collective-permute-done.5.refs_0_), channel_id=1, source_target_pairs={{0,1},{1,0},{2,3},{3,2},{4,5},{5,4},{6,7},{7,6},{8,9},{9,8},{10,11... | collective-permute-start | bytes 786440 | tf_op jit(solution)/shard_map/ppermute | solution.py:508
  22.9 4.6 %collective-permute-start.2 = (f32[4,512]{1,0:T(4,128)S(1)}, f32[4,512]{1,0:T(4,128)S(1)}, u32[]{:S(2)}, u32[]{:S(2)}) collective-permute-start(f32[4,512]{1,0:T(4,128)S(1)} %add.15.g_ref), channel_id=1, source_target_pairs={{0,16},{4,20},{8,24},{12,28},{16,0},{20,4},{24,8},{28,12},{1,17},{... | collective-permute-start | bytes 24584 | tf_op jit(solution)/shard_map/ppermute | solution.py:482
  31.3 4.3 %collective-permute-start.9 = (f32[12,128]{1,0:T(8,128)S(1)}, f32[12,128]{1,0:T(8,128)S(1)}, u32[]{:S(2)}, u32[]{:S(2)}) collective-permute-start(f32[12,128]{1,0:T(8,128)S(1)} %get-tuple-element.34), channel_id=1, source_target_pairs={{0,1},{1,0},{2,3},{3,2},{4,5},{5,4},{6,7},{7,6},{8,9},{9,8},{10,11... | collective-permute-start | bytes 18440 | tf_op jit(solution)/shard_map/ppermute | solution.py:516
  31.4 4.3 %collective-permute-start.8 = (f32[12,128]{1,0:T(8,128)S(1)}, f32[12,128]{1,0:T(8,128)S(1)}, u32[]{:S(2)}, u32[]{:S(2)}) collective-permute-start(f32[12,128]{1,0:T(8,128)S(1)} %get-tuple-element.34), channel_id=1, source_target_pairs={{0,2},{1,3},{2,0},{3,1},{4,6},{5,7},{6,4},{7,5},{8,10},{9,11},{10,... | collective-permute-start | bytes 18440 | tf_op jit(solution)/shard_map/ppermute | solution.py:516
  32.2 3.5 %collective-permute-start.7 = (f32[12,128]{1,0:T(8,128)S(1)}, f32[12,128]{1,0:T(8,128)S(1)}, u32[]{:S(2)}, u32[]{:S(2)}) collective-permute-start(f32[12,128]{1,0:T(8,128)S(1)} %get-tuple-element.34), channel_id=1, source_target_pairs={{0,3},{1,2},{2,1},{3,0},{4,7},{5,6},{6,5},{7,4},{8,11},{9,10},{10,... | collective-permute-start | bytes 18440 | tf_op jit(solution)/shard_map/ppermute | solution.py:516
  33.3 2.4 %copy-start.5 = (f32[1536]{0:T(1024)S(1)}, f32[1536]{0:T(1024)}, u32[]{:S(2)}) copy-start(f32[1536]{0:T(1024)} %param.22) | copy-start | bytes 18436
  33.3 2.4 %copy-start.6 = (s32[1536]{0:T(1024)S(1)}, s32[1536]{0:T(1024)}, u32[]{:S(2)}) copy-start(s32[1536]{0:T(1024)} %param.23) | copy-start | bytes 18436

commit v7 on v6

--- a/solution.py
+++ b/solution.py
@@ -311,7 +311,7 @@
 
 def branch_kernel(half, n_ahead, g_ref, far_ref, case_ref, par_ref, fd_ref, near_ref, far_edge_ref, *refs):
     ahead = refs[:n_ahead]
-    volt_hbm, square_ref, worst_ref, vbuf, uh, ul, vsem = refs[n_ahead:]
+    volt_hbm, square_ref, rate_ref, worst_ref, vbuf, uh, ul, vsem = refs[n_ahead:]
     rows, cases = vbuf.shape
     branches = par_ref.shape[0]
     ext = uh.shape[0]
@@ -359,8 +359,15 @@
             )
         return square
 
+    later = square_ref.shape[0]
+
     def finish(drop, par, start):
-        square_ref[pl.ds(start, par.shape[0]), :] = square_of(drop, par, start)
+        square = square_of(drop, par, start)
+        if start < later:
+            square_ref[pl.ds(start, par.shape[0]), :] = square
+        else:
+            rate = relay_of_square(square, par[:, 3:4], par[:, 4:5])
+            rate_ref[pl.ds(start - later, par.shape[0]), :] = rate
 
     starts = [sum(part.shape[0] for part in ahead[:i]) for i in range(n_ahead + 1)]
     whole = list(range(starts.pop(), branches, TILE))
@@ -379,15 +386,17 @@
     rows = fd.shape[0]
     branches = par.shape[0]
     ext = rows + sum(edge.shape[0] for edge in edges)
+    later = sum(part.shape[0] for part in ahead)
     vmem = pl.BlockSpec(memory_space=pltpu.VMEM)
     hbm = pl.BlockSpec(memory_space=pltpu.HBM)
     return pl.pallas_call(
         functools.partial(branch_kernel, n_case // 2, len(ahead)),
         in_specs=[vmem] * (7 + len(ahead)),
-        out_specs=[hbm, vmem, vmem],
+        out_specs=[hbm, vmem, vmem, vmem],
         out_shape=[
             jax.ShapeDtypeStruct((rows, count), F32),
-            pltpu.VMEM((branches, count), F32),
+            pltpu.VMEM((later, count), F32),
+            pltpu.VMEM((branches - later, count), F32),
             pltpu.VMEM((branches // 128, 128), F32),
         ],
         scratch_shapes=[
@@ -401,9 +410,11 @@
     )(g, g_far, case_par, par, fd, *edges, *ahead)
 
 
-def relay_kernel(square_ref, par_ref, relay_hbm, rbuf, sems):
+def relay_kernel(square_ref, rate_ref, par_ref, relay_hbm, rbuf, sems):
     rows = square_ref.shape[0]
-    copies = []
+    target = relay_hbm.at[pl.ds(rows, rate_ref.shape[0])]
+    copies = [pltpu.make_async_copy(rate_ref, target, sems.at[0])]
+    copies[0].start()
     first = 0
     while first < rows:
         count = TILE if first + 2 * TILE <= rows else TILE // 2
@@ -418,24 +429,24 @@
         copy.wait()
 
 
-def relay_rates(square, par):
-    rows = square.shape[0]
+def relay_rates(square, rate, par):
+    rows, count = square.shape
     vmem = pl.BlockSpec(memory_space=pltpu.VMEM)
     return pl.pallas_call(
         relay_kernel,
-        in_specs=[vmem, vmem],
+        in_specs=[vmem, vmem, vmem],
         out_specs=pl.BlockSpec(memory_space=pltpu.HBM),
-        out_shape=jax.ShapeDtypeStruct(square.shape, F32),
+        out_shape=jax.ShapeDtypeStruct((rows + rate.shape[0], count), F32),
         scratch_shapes=[
             pltpu.VMEM(square.shape, F32),
-            pltpu.SemaphoreType.DMA((rows // TILE + 1,)),
+            pltpu.SemaphoreType.DMA((rows // TILE + 2,)),
         ],
         compiler_params=pltpu.CompilerParams(vmem_limit_bytes=8 * 2**20),
         cost_estimate=pl.CostEstimate(
             flops=8 * square.size, bytes_accessed=8 * square.size, transcendentals=2 * square.size
         ),
         name="relay_rates",
-    )(square, par)
+    )(square, rate, par)
 
 
 def per_device(
@@ -509,14 +520,14 @@
             order = order + [m ^ bit for m in order]
             bit //= 2
         edges.append(boundary_columns(order, pick, pieces, flops))
-    voltage, square, worst = screen_branches(
+    voltage, square, rate, worst = screen_branches(
         g, g_far, case_rows(tie_x[None], fault_z[None]), par, fd, edges, ahead, n_case
     )
     others = [
         lax.ppermute(worst, "case", [(i, i ^ m) for i in range(n_case)])
         for m in range(n_case - 1, 0, -1)
     ]
-    relay_rate = relay_rates(square, par)
+    relay_rate = relay_rates(square, rate, par)
     half_power, factor = curve_constants(curve)
     worst = functools.reduce(jnp.maximum, others, worst).reshape(-1)
     worst_rate = relay_of_square(worst, half_power, 1.0 / (factor * tds))

time: 36.5 us -> 36.4 us (level)
  Pallas kernels: 19.7 us -> 19.3 us
    pallas_call x1, Pallas kernels: 2.38 us -> 1.69 us  [relay_rates(): pl.pallas_call(relay_kernel, in_specs=[vmem, vmem, vmem], out_specs=pl.Bl...]
  transfers between devices with their start and end apart: 10 -> 10, of which waited for: 3 -> 5; matrix products, arithmetic and copies ran while one was open for 0% -> 0% of each run, Pallas kernels for 39% -> 37%
where the time goes in v7:
time: 36.4 us; the launch traced here: 36.2 us
  Pallas kernels  19.3 us (53%)
  starting transfers between devices  13.2 us (36%)
  waiting for transfers between devices  2.2 us (6%)
  between operations  0.83 us (2%)
  other arithmetic  0.64 us (2%)
    pallas_call x1, Pallas kernels, pick_columns(): pl.pallas_call(functools.partial(columns_kernel, n_case // 2), in_specs=[...  6.56 us
    ppermute x3, starting transfers between devices, swap_over_bus(): return lax.ppermute(g, 'bus', [(i, i ^ bit) for i in range(n_bus)])  5.9 us
    ppermute x1, starting transfers between devices, per_device(): own = lax.ppermute(send, ('bus', 'case'), pairs)  4.86 us
    pallas_call x1, Pallas kernels, screen_branches(): pl.pallas_call(functools.partial(branch_kernel, n_case // 2, len(ahead)),...  4.15 us
    pallas_call x2, Pallas kernels, advance(): pl.pallas_call(functools.partial(advance_kernel, n_case // 2, start), in_...  3.79 us
    ppermute x3, starting transfers between devices, per_device(): lax.ppermute(worst, 'case', [(i, i ^ m) for i in range(n_case)])  1.93 us
    pallas_call x1, Pallas kernels, relay_rates(): pl.pallas_call(relay_kernel, in_specs=[vmem, vmem, vmem], out_specs=pl.Bl...  1.69 us
    pallas_call x1, Pallas kernels, stage(): pl.pallas_call(functools.partial(stage_kernel, half), in_specs=[pl.BlockS...  1.63 us
  transfers between devices with their start and end apart: 10, of which 5 were waited for; matrix products, arithmetic and copies ran while one was open for 0% of the time, Pallas kernels for 37%

profile of v7, /device:TPU:0, one launch (start us, length us, event | category | flops | bytes accessed | tf_op | source)
XLA Modules:
  0.0 36.2 jit_solution(3495568416738905575)
XLA Ops:
  0.6 0.0 copy-start
  0.6 0.0 copy-start.1
  0.7 0.0 copy-start.2
  0.7 1.6 %stage.1 = (f32[64,1024]{1,0:T(8,128)S(1)}, f32[512,1024]{1,0:T(8,128)S(1)}, bf16[1024,1024]{1,0:T(8,128)(2,1)S(1)}) custom-call(f32[1024,1024]{1,0:T(8,128)} %z_hbm.3, s32[8,2,128]{2,1,0:T(2,128)} %lists_hbm.1, s32[1,512]{1,0:T(1,128)} %bitcast.24, s32[2,512]{1,0:T(2,128)} %bitcast.22), custom_call_target="tpu_custom_call" | custom-call | tf_op jit(solution)/shard_map/stage/pallas_call | solution.py:76
  2.3 4.9 %collective-permute-start.3 = (f32[64,1024]{1,0:T(8,128)S(1)}, f32[64,1024]{1,0:T(8,128)S(1)}, u32[]{:S(2)}, u32[]{:S(2)}) collective-permute-start(f32[64,1024]{1,0:T(8,128)S(1)} %get-tuple-element.29), channel_id=1, source_target_pairs={{0,4},{1,5},{4,8},{5,9},{6,2},{7,3},{8,12},{9,13},{10,6},{11,7},{1... | collective-permute-start | bytes 786440 | tf_op jit(solution)/shard_map/ppermute | solution.py:476
  7.2 0.0 copy-done
  7.2 0.0 copy-done.1
  7.2 0.0 copy-done.2
  7.2 6.6 %pick_columns.1 = (f32[1024,1024]{1,0:T(8,128)S(1)}, f32[4,512]{1,0:T(4,128)S(1)}, f32[1536,8]{1,0:T(8,128)S(1)}, bf16[1024,1024]{1,0:T(8,128)(2,1)S(1)}, bf16[1024,1024]{1,0:T(8,128)(2,1)S(1)}) custom-call(f32[512,1024]{1,0:T(8,128)S(1)} %get-tuple-element.20.z_ref, bf16[1024,1024]{1,0:T(8,128)(2,1)S(1)} %get-tuple-element.21.pick, s32[1,512]{1,0:T(1,128)S(1)} %bitcast.25, ...), custom_call_target="tpu_custom_call" | custom-call | tf_op jit(solution)/shard_map/pick_columns/pallas_call | solution.py:201
  13.8 1.6 %collective-permute-start = (f32[4,512]{1,0:T(4,128)S(1)}, f32[4,512]{1,0:T(4,128)S(1)}, u32[]{:S(2)}, u32[]{:S(2)}) collective-permute-start(f32[4,512]{1,0:T(4,128)S(1)} %get-tuple-element.22), channel_id=1, source_target_pairs={{0,4},{4,0},{8,12},{12,8},{16,20},{20,16},{24,28},{28,24},{1,5},{5... | collective-permute-start | bytes 24584 | tf_op jit(solution)/shard_map/ppermute | solution.py:493
  15.4 0.0 collective-permute-done.3.refs_0_
  15.4 0.5 %collective-permute-start.5 = (f32[64,1024]{1,0:T(8,128)S(1)}, f32[64,1024]{1,0:T(8,128)S(1)}, u32[]{:S(2)}, u32[]{:S(2)}) collective-permute-start(f32[64,1024]{1,0:T(8,128)S(1)} %collective-permute-done.3.refs_0_), channel_id=1, source_target_pairs={{0,2},{1,3},{2,0},{3,1},{4,6},{5,7},{6,4},{7,5},{8,10},{9,11},{10,... | collective-permute-start | bytes 786440 | tf_op jit(solution)/shard_map/ppermute | solution.py:499
  15.9 1.9 %advance.2.refs_0_ = f32[384,1024]{1,0:T(8,128)S(1)} custom-call(bf16[1024,1024]{1,0:T(8,128)(2,1)S(1)} %get-tuple-element.23.fd_hi, bf16[1024,1024]{1,0:T(8,128)(2,1)S(1)} %get-tuple-element.24.fd_lo, f32[1536,8]{1,0:T(8,128)S(1)} %get-tuple-element.25.par_ref), custom_call_target="tpu_custom_call" | custom-call | flops 1610612736 | bytes 3145728 | tf_op jit(solution)/shard_map/advance/pallas_call | solution.py:249
  17.8 0.0 collective-permute-done
  17.8 0.0 copy-start.3
  17.8 0.0 copy-start.4
  17.8 1.6 %collective-permute-start.1 = (f32[4,512]{1,0:T(4,128)S(1)}, f32[4,512]{1,0:T(4,128)S(1)}, u32[]{:S(2)}, u32[]{:S(2)}) collective-permute-start(f32[4,512]{1,0:T(4,128)S(1)} %add.14), channel_id=1, source_target_pairs={{0,8},{4,12},{8,0},{12,4},{16,24},{20,28},{24,16},{28,20},{1,9},{5... | collective-permute-start | bytes 24584 | tf_op jit(solution)/shard_map/ppermute | solution.py:493
  19.5 1.9 %advance.3.refs_1_ = f32[384,1024]{1,0:T(8,128)S(1)} custom-call(bf16[1024,1024]{1,0:T(8,128)(2,1)S(1)} %get-tuple-element.23.fd_hi, bf16[1024,1024]{1,0:T(8,128)(2,1)S(1)} %get-tuple-element.24.fd_lo, f32[1536,8]{1,0:T(8,128)S(1)} %get-tuple-element.25.par_ref), custom_call_target="tpu_custom_call" | custom-call | flops 1610612736 | bytes 3145728 | tf_op jit(solution)/shard_map/advance/pallas_call | solution.py:249
  21.4 0.2 collective-permute-done.1
  21.6 0.0 collective-permute-start.4
  21.6 1.3 %collective-permute-done.5.refs_0_ = f32[64,1024]{1,0:T(8,128)S(1)} collective-permute-done((f32[64,1024]{1,0:T(8,128)S(1)}, f32[64,1024]{1,0:T(8,128)S(1)}, u32[]{:S(2)}, u32[]{:S(2)}) %collective-permute-start.5) | collective-permute-done | bytes 262176 | tf_op jit(solution)/shard_map/ppermute | solution.py:499
  22.9 0.0 collective-permute-start.6
  22.9 0.0 copy-done.3
  22.9 0.0 copy-done.4
  22.9 2.7 %collective-permute-start.2 = (f32[4,512]{1,0:T(4,128)S(1)}, f32[4,512]{1,0:T(4,128)S(1)}, u32[]{:S(2)}, u32[]{:S(2)}) collective-permute-start(f32[4,512]{1,0:T(4,128)S(1)} %add.15.g_ref), channel_id=1, source_target_pairs={{0,16},{4,20},{8,24},{12,28},{16,0},{20,4},{24,8},{28,12},{1,17},{... | collective-permute-start | bytes 24584 | tf_op jit(solution)/shard_map/ppermute | solution.py:493
  25.5 0.0 collective-permute-done.4.refs_1_
  25.5 0.7 %boundary_columns.2.near_ref = f32[128,1024]{1,0:T(8,128)S(1)} custom-call(bf16[1024,1024]{1,0:T(8,128)(2,1)S(1)} %get-tuple-element.21.pick, f32[64,1024]{1,0:T(8,128)S(1)} %collective-permute-done.3.refs_0_, f32[64,1024]{1,0:T(8,128)S(1)} %collective-permute-done.4.refs_1_), custom_call_target="tpu_custom_call" | custom-call | flops 536870912 | bytes 1 | tf_op jit(solution)/shard_map/boundary_columns/pallas_call | solution.py:278
  26.3 0.0 collective-permute-done.6.refs_1_
  26.3 0.8 %boundary_columns.3.far_edge_ref = f32[128,1024]{1,0:T(8,128)S(1)} custom-call(bf16[1024,1024]{1,0:T(8,128)(2,1)S(1)} %get-tuple-element.21.pick, f32[64,1024]{1,0:T(8,128)S(1)} %collective-permute-done.5.refs_0_, f32[64,1024]{1,0:T(8,128)S(1)} %collective-permute-done.6.refs_1_), custom_call_target="tpu_custom_call" | custom-call | flops 1 | bytes 1 | tf_op jit(solution)/shard_map/boundary_columns/pallas_call | solution.py:278
  27.1 0.4 %collective-permute-done.2.far_ref = f32[4,512]{1,0:T(4,128)S(1)} collective-permute-done((f32[4,512]{1,0:T(4,128)S(1)}, f32[4,512]{1,0:T(4,128)S(1)}, u32[]{:S(2)}, u32[]{:S(2)}) %collective-permute-start.2) | collective-permute-done | bytes 8224 | tf_op jit(solution)/shard_map/ppermute | solution.py:493
  27.5 4.1 %screen_branches.1 = (f32[1024,512]{1,0:T(8,128)}, f32[768,512]{1,0:T(8,128)S(1)}, f32[768,512]{1,0:T(8,128)S(1)}, f32[12,128]{1,0:T(8,128)S(1)}) custom-call(f32[4,512]{1,0:T(4,128)S(1)} %add.15.g_ref, f32[4,512]{1,0:T(4,128)S(1)} %collective-permute-done.2.far_ref, f32[2,512]{1,0:T(2,128)S(1)} %case_rows.1.case_ref, ...), custom_call_target="tpu_custom_call" | custom-call | tf_op jit(solution)/shard_map/screen_branches/pallas_call | solution.py:392
  31.7 0.1 collective-permute-start.9
  31.7 0.8 %collective-permute-start.8 = (f32[12,128]{1,0:T(8,128)S(1)}, f32[12,128]{1,0:T(8,128)S(1)}, u32[]{:S(2)}, u32[]{:S(2)}) collective-permute-start(f32[12,128]{1,0:T(8,128)S(1)} %get-tuple-element.36), channel_id=1, source_target_pairs={{0,2},{1,3},{2,0},{3,1},{4,6},{5,7},{6,4},{7,5},{8,10},{9,11},{10,... | collective-permute-start | bytes 18440 | tf_op jit(solution)/shard_map/ppermute | solution.py:527
  32.5 1.1 %collective-permute-start.7 = (f32[12,128]{1,0:T(8,128)S(1)}, f32[12,128]{1,0:T(8,128)S(1)}, u32[]{:S(2)}, u32[]{:S(2)}) collective-permute-start(f32[12,128]{1,0:T(8,128)S(1)} %get-tuple-element.36), channel_id=1, source_target_pairs={{0,3},{1,2},{2,1},{3,0},{4,7},{5,6},{6,5},{7,4},{8,11},{9,10},{10,... | collective-permute-start | bytes 18440 | tf_op jit(solution)/shard_map/ppermute | solution.py:527
  33.6 0.0 copy-start.5
  33.6 0.0 copy-start.6
  33.6 1.7 %relay_rates.1 = f32[1536,512]{1,0:T(8,128)} custom-call(f32[768,512]{1,0:T(8,128)S(1)} %get-tuple-element.34.square_ref, f32[768,512]{1,0:T(8,128)S(1)} %get-tuple-element.35.rate_ref, f32[1536,8]{1,0:T(8,128)S(1)} %get-tuple-element.25.par_ref), custom_call_target="tpu_custom_call" | custom-call | flops 3145728 | bytes 3145728 | tf_op jit(solution)/shard_map/relay_rates/pallas_call | solution.py:435
  35.3 0.0 collective-permute-done.9
  35.3 0.1 collective-permute-done.8
  35.5 0.1 collective-permute-done.7
  35.6 0.0 copy-done.5
  35.6 0.0 copy-done.6
  35.6 0.6 %fusion.4 = f32[1536]{0:T(1024)} fusion(f32[1536]{0:T(1024)S(1)} %copy-done.5, f32[12,128]{1,0:T(8,128)S(1)} %collective-permute-done.9, f32[12,128]{1,0:T(8,128)S(1)} %collective-permute-done.8, f32[12,128]{1,0:T(8,128)S(1)} %get-tuple-element.36, f32[12,128]{1,0:T(8,128)S(1)} %collective-permute-done.7, s32[1536]{0:T(1024)S(1)} %copy-done.6), kind=kLoop, calls=%fused_computation.5 | loop fusion | flops 27648 | bytes 43008 | tf_op jit(solution)/shard_map/mul | solution.py:291
  (3 shorter events, 0.0 us)
Async XLA Ops:
  0.6 6.5 %copy-start = (s32[512,2]{0,1:T(2,128)S(1)}, s32[512,2]{0,1:T(2,128)}, u32[]{:S(2)}) copy-start(s32[512,2]{0,1:T(2,128)} %param.15) | copy-start | bytes 12292
  0.6 6.5 %copy-start.1 = (s32[512]{0:T(512)S(1)}, s32[512]{0:T(512)}, u32[]{:S(2)}) copy-start(s32[512]{0:T(512)} %param.14) | copy-start | bytes 6148
  0.7 6.5 %copy-start.2 = (s32[1024]{0:T(1024)S(1)}, s32[1024]{0:T(1024)}, u32[]{:S(2)}) copy-start(s32[1024]{0:T(1024)} %param.13) | copy-start | bytes 12292
  2.3 13.1 %collective-permute-start.3 = (f32[64,1024]{1,0:T(8,128)S(1)}, f32[64,1024]{1,0:T(8,128)S(1)}, u32[]{:S(2)}, u32[]{:S(2)}) collective-permute-start(f32[64,1024]{1,0:T(8,128)S(1)} %get-tuple-element.29), channel_id=1, source_target_pairs={{0,4},{1,5},{4,8},{5,9},{6,2},{7,3},{8,12},{9,13},{10,6},{11,7},{1... | collective-permute-start | bytes 786440 | tf_op jit(solution)/shard_map/ppermute | solution.py:476
  13.8 4.0 %collective-permute-start = (f32[4,512]{1,0:T(4,128)S(1)}, f32[4,512]{1,0:T(4,128)S(1)}, u32[]{:S(2)}, u32[]{:S(2)}) collective-permute-start(f32[4,512]{1,0:T(4,128)S(1)} %get-tuple-element.22), channel_id=1, source_target_pairs={{0,4},{4,0},{8,12},{12,8},{16,20},{20,16},{24,28},{28,24},{1,5},{5... | collective-permute-start | bytes 24584 | tf_op jit(solution)/shard_map/ppermute | solution.py:493
  15.4 7.5 %collective-permute-start.5 = (f32[64,1024]{1,0:T(8,128)S(1)}, f32[64,1024]{1,0:T(8,128)S(1)}, u32[]{:S(2)}, u32[]{:S(2)}) collective-permute-start(f32[64,1024]{1,0:T(8,128)S(1)} %collective-permute-done.3.refs_0_), channel_id=1, source_target_pairs={{0,2},{1,3},{2,0},{3,1},{4,6},{5,7},{6,4},{7,5},{8,10},{9,11},{10,... | collective-permute-start | bytes 786440 | tf_op jit(solution)/shard_map/ppermute | solution.py:499
  17.8 5.1 %copy-start.3 = (f32[512]{0:T(512)S(1)}, f32[512]{0:T(512)}, u32[]{:S(2)}) copy-start(f32[512]{0:T(512)} %param.16) | copy-start | bytes 6148
  17.8 5.0 %copy-start.4 = (f32[512]{0:T(512)S(1)}, f32[512]{0:T(512)}, u32[]{:S(2)}) copy-start(f32[512]{0:T(512)} %param.17) | copy-start | bytes 6148
  17.8 3.7 %collective-permute-start.1 = (f32[4,512]{1,0:T(4,128)S(1)}, f32[4,512]{1,0:T(4,128)S(1)}, u32[]{:S(2)}, u32[]{:S(2)}) collective-permute-start(f32[4,512]{1,0:T(4,128)S(1)} %add.14), channel_id=1, source_target_pairs={{0,8},{4,12},{8,0},{12,4},{16,24},{20,28},{24,16},{28,20},{1,9},{5... | collective-permute-start | bytes 24584 | tf_op jit(solution)/shard_map/ppermute | solution.py:493
  21.6 4.0 %collective-permute-start.4 = (f32[64,1024]{1,0:T(8,128)S(1)}, f32[64,1024]{1,0:T(8,128)S(1)}, u32[]{:S(2)}, u32[]{:S(2)}) collective-permute-start(f32[64,1024]{1,0:T(8,128)S(1)} %collective-permute-done.3.refs_0_), channel_id=1, source_target_pairs={{0,1},{1,0},{2,3},{3,2},{4,5},{5,4},{6,7},{7,6},{8,9},{9,8},{10,11... | collective-permute-start | bytes 786440 | tf_op jit(solution)/shard_map/ppermute | solution.py:519
  22.9 3.4 %collective-permute-start.6 = (f32[64,1024]{1,0:T(8,128)S(1)}, f32[64,1024]{1,0:T(8,128)S(1)}, u32[]{:S(2)}, u32[]{:S(2)}) collective-permute-start(f32[64,1024]{1,0:T(8,128)S(1)} %collective-permute-done.5.refs_0_), channel_id=1, source_target_pairs={{0,1},{1,0},{2,3},{3,2},{4,5},{5,4},{6,7},{7,6},{8,9},{9,8},{10,11... | collective-permute-start | bytes 786440 | tf_op jit(solution)/shard_map/ppermute | solution.py:519
  22.9 4.6 %collective-permute-start.2 = (f32[4,512]{1,0:T(4,128)S(1)}, f32[4,512]{1,0:T(4,128)S(1)}, u32[]{:S(2)}, u32[]{:S(2)}) collective-permute-start(f32[4,512]{1,0:T(4,128)S(1)} %add.15.g_ref), channel_id=1, source_target_pairs={{0,16},{4,20},{8,24},{12,28},{16,0},{20,4},{24,8},{28,12},{1,17},{... | collective-permute-start | bytes 24584 | tf_op jit(solution)/shard_map/ppermute | solution.py:493
  31.7 3.6 %collective-permute-start.9 = (f32[12,128]{1,0:T(8,128)S(1)}, f32[12,128]{1,0:T(8,128)S(1)}, u32[]{:S(2)}, u32[]{:S(2)}) collective-permute-start(f32[12,128]{1,0:T(8,128)S(1)} %get-tuple-element.36), channel_id=1, source_target_pairs={{0,1},{1,0},{2,3},{3,2},{4,5},{5,4},{6,7},{7,6},{8,9},{9,8},{10,11... | collective-permute-start | bytes 18440 | tf_op jit(solution)/shard_map/ppermute | solution.py:527
  31.7 3.7 %collective-permute-start.8 = (f32[12,128]{1,0:T(8,128)S(1)}, f32[12,128]{1,0:T(8,128)S(1)}, u32[]{:S(2)}, u32[]{:S(2)}) collective-permute-start(f32[12,128]{1,0:T(8,128)S(1)} %get-tuple-element.36), channel_id=1, source_target_pairs={{0,2},{1,3},{2,0},{3,1},{4,6},{5,7},{6,4},{7,5},{8,10},{9,11},{10,... | collective-permute-start | bytes 18440 | tf_op jit(solution)/shard_map/ppermute | solution.py:527
  32.5 3.1 %collective-permute-start.7 = (f32[12,128]{1,0:T(8,128)S(1)}, f32[12,128]{1,0:T(8,128)S(1)}, u32[]{:S(2)}, u32[]{:S(2)}) collective-permute-start(f32[12,128]{1,0:T(8,128)S(1)} %get-tuple-element.36), channel_id=1, source_target_pairs={{0,3},{1,2},{2,1},{3,0},{4,7},{5,6},{6,5},{7,4},{8,11},{9,10},{10,... | collective-permute-start | bytes 18440 | tf_op jit(solution)/shard_map/ppermute | solution.py:527
  33.6 2.0 %copy-start.5 = (f32[1536]{0:T(1024)S(1)}, f32[1536]{0:T(1024)}, u32[]{:S(2)}) copy-start(f32[1536]{0:T(1024)} %param.22) | copy-start | bytes 18436
  33.6 2.0 %copy-start.6 = (s32[1536]{0:T(1024)S(1)}, s32[1536]{0:T(1024)}, u32[]{:S(2)}) copy-start(s32[1536]{0:T(1024)} %param.23) | copy-start | bytes 18436

commit v8 on v7

--- a/solution.py
+++ b/solution.py
@@ -498,7 +498,7 @@
     (own,) = after(g, own)
     other = lax.ppermute(own, "case", [(i, i ^ half) for i in range(n_case)])
     ahead = []
-    sizes = [par.shape[0] // 12 * i for i in (3, 3)]
+    sizes = [par.shape[0] // 12 * i for i in (2, 4)]
     bits = [2**i for i in range((n_bus - 1).bit_length())]
     for n, bit in enumerate(bits[:-1]):
         far = swap_over_bus(g, bit)

time: 36.4 us -> 36.5 us (level)
  no operation moved by 1% of the time
where the time goes in v8:
time: 36.5 us; the launch traced here: 36.3 us
  Pallas kernels  19.4 us (53%)
  starting transfers between devices  13.3 us (36%)
  waiting for transfers between devices  2.14 us (6%)
  between operations  0.82 us (2%)
  other arithmetic  0.64 us (2%)
    pallas_call x1, Pallas kernels, pick_columns(): pl.pallas_call(functools.partial(columns_kernel, n_case // 2), in_specs=[...  6.56 us
    ppermute x3, starting transfers between devices, swap_over_bus(): return lax.ppermute(g, 'bus', [(i, i ^ bit) for i in range(n_bus)])  5.91 us
    ppermute x1, starting transfers between devices, per_device(): own = lax.ppermute(send, ('bus', 'case'), pairs)  4.86 us
    pallas_call x1, Pallas kernels, screen_branches(): pl.pallas_call(functools.partial(branch_kernel, n_case // 2, len(ahead)),...  4.17 us
    pallas_call x2, Pallas kernels, advance(): pl.pallas_call(functools.partial(advance_kernel, n_case // 2, start), in_...  3.83 us
    ppermute x3, starting transfers between devices, per_device(): lax.ppermute(worst, 'case', [(i, i ^ m) for i in range(n_case)])  1.93 us
    pallas_call x1, Pallas kernels, relay_rates(): pl.pallas_call(relay_kernel, in_specs=[vmem, vmem, vmem], out_specs=pl.Bl...  1.69 us
    pallas_call x1, Pallas kernels, stage(): pl.pallas_call(functools.partial(stage_kernel, half), in_specs=[pl.BlockS...  1.63 us
  transfers between devices with their start and end apart: 10, of which 5 were waited for; matrix products, arithmetic and copies ran while one was open for 0% of the time, Pallas kernels for 37%

profile of v8, /device:TPU:0, one launch (start us, length us, event | category | flops | bytes accessed | tf_op | source)
XLA Modules:
  0.0 36.3 jit_solution(8360090157194154984)
XLA Ops:
  0.6 0.0 copy-start
  0.6 0.0 copy-start.1
  0.7 0.0 copy-start.2
  0.7 1.6 %stage.1 = (f32[64,1024]{1,0:T(8,128)S(1)}, f32[512,1024]{1,0:T(8,128)S(1)}, bf16[1024,1024]{1,0:T(8,128)(2,1)S(1)}) custom-call(f32[1024,1024]{1,0:T(8,128)} %z_hbm.3, s32[8,2,128]{2,1,0:T(2,128)} %lists_hbm.1, s32[1,512]{1,0:T(1,128)} %bitcast.24, s32[2,512]{1,0:T(2,128)} %bitcast.22), custom_call_target="tpu_custom_call" | custom-call | tf_op jit(solution)/shard_map/stage/pallas_call | solution.py:76
  2.3 4.9 %collective-permute-start.3 = (f32[64,1024]{1,0:T(8,128)S(1)}, f32[64,1024]{1,0:T(8,128)S(1)}, u32[]{:S(2)}, u32[]{:S(2)}) collective-permute-start(f32[64,1024]{1,0:T(8,128)S(1)} %get-tuple-element.29), channel_id=1, source_target_pairs={{0,4},{1,5},{4,8},{5,9},{6,2},{7,3},{8,12},{9,13},{10,6},{11,7},{1... | collective-permute-start | bytes 786440 | tf_op jit(solution)/shard_map/ppermute | solution.py:476
  7.2 0.0 copy-done
  7.2 0.0 copy-done.1
  7.2 0.0 copy-done.2
  7.2 6.6 %pick_columns.1 = (f32[1024,1024]{1,0:T(8,128)S(1)}, f32[4,512]{1,0:T(4,128)S(1)}, f32[1536,8]{1,0:T(8,128)S(1)}, bf16[1024,1024]{1,0:T(8,128)(2,1)S(1)}, bf16[1024,1024]{1,0:T(8,128)(2,1)S(1)}) custom-call(f32[512,1024]{1,0:T(8,128)S(1)} %get-tuple-element.20.z_ref, bf16[1024,1024]{1,0:T(8,128)(2,1)S(1)} %get-tuple-element.21.pick, s32[1,512]{1,0:T(1,128)S(1)} %bitcast.25, ...), custom_call_target="tpu_custom_call" | custom-call | tf_op jit(solution)/shard_map/pick_columns/pallas_call | solution.py:201
  13.8 1.6 %collective-permute-start = (f32[4,512]{1,0:T(4,128)S(1)}, f32[4,512]{1,0:T(4,128)S(1)}, u32[]{:S(2)}, u32[]{:S(2)}) collective-permute-start(f32[4,512]{1,0:T(4,128)S(1)} %get-tuple-element.22), channel_id=1, source_target_pairs={{0,4},{4,0},{8,12},{12,8},{16,20},{20,16},{24,28},{28,24},{1,5},{5... | collective-permute-start | bytes 24584 | tf_op jit(solution)/shard_map/ppermute | solution.py:493
  15.4 0.0 collective-permute-done.3.refs_0_
  15.4 0.5 %collective-permute-start.5 = (f32[64,1024]{1,0:T(8,128)S(1)}, f32[64,1024]{1,0:T(8,128)S(1)}, u32[]{:S(2)}, u32[]{:S(2)}) collective-permute-start(f32[64,1024]{1,0:T(8,128)S(1)} %collective-permute-done.3.refs_0_), channel_id=1, source_target_pairs={{0,2},{1,3},{2,0},{3,1},{4,6},{5,7},{6,4},{7,5},{8,10},{9,11},{10,... | collective-permute-start | bytes 786440 | tf_op jit(solution)/shard_map/ppermute | solution.py:499
  15.9 1.4 %advance.2.refs_0_ = f32[256,1024]{1,0:T(8,128)S(1)} custom-call(bf16[1024,1024]{1,0:T(8,128)(2,1)S(1)} %get-tuple-element.23.fd_hi, bf16[1024,1024]{1,0:T(8,128)(2,1)S(1)} %get-tuple-element.24.fd_lo, f32[1536,8]{1,0:T(8,128)S(1)} %get-tuple-element.25.par_ref), custom_call_target="tpu_custom_call" | custom-call | flops 1073741824 | bytes 2097152 | tf_op jit(solution)/shard_map/advance/pallas_call | solution.py:249
  17.3 0.2 collective-permute-done
  17.5 0.0 copy-start.3
  17.5 0.0 copy-start.4
  17.5 1.6 %collective-permute-start.1 = (f32[4,512]{1,0:T(4,128)S(1)}, f32[4,512]{1,0:T(4,128)S(1)}, u32[]{:S(2)}, u32[]{:S(2)}) collective-permute-start(f32[4,512]{1,0:T(4,128)S(1)} %add.14), channel_id=1, source_target_pairs={{0,8},{4,12},{8,0},{12,4},{16,24},{20,28},{24,16},{28,20},{1,9},{5... | collective-permute-start | bytes 24584 | tf_op jit(solution)/shard_map/ppermute | solution.py:493
  19.1 2.5 %advance.3.refs_1_ = f32[512,1024]{1,0:T(8,128)S(1)} custom-call(bf16[1024,1024]{1,0:T(8,128)(2,1)S(1)} %get-tuple-element.23.fd_hi, bf16[1024,1024]{1,0:T(8,128)(2,1)S(1)} %get-tuple-element.24.fd_lo, f32[1536,8]{1,0:T(8,128)S(1)} %get-tuple-element.25.par_ref), custom_call_target="tpu_custom_call" | custom-call | flops 2147483648 | bytes 4194304 | tf_op jit(solution)/shard_map/advance/pallas_call | solution.py:249
  21.6 0.0 collective-permute-done.1
  21.6 0.1 collective-permute-start.4
  21.7 1.1 %collective-permute-done.5.refs_0_ = f32[64,1024]{1,0:T(8,128)S(1)} collective-permute-done((f32[64,1024]{1,0:T(8,128)S(1)}, f32[64,1024]{1,0:T(8,128)S(1)}, u32[]{:S(2)}, u32[]{:S(2)}) %collective-permute-start.5) | collective-permute-done | bytes 262176 | tf_op jit(solution)/shard_map/ppermute | solution.py:499
  22.9 0.0 collective-permute-start.6
  22.9 0.0 copy-done.3
  22.9 0.0 copy-done.4
  22.9 2.7 %collective-permute-start.2 = (f32[4,512]{1,0:T(4,128)S(1)}, f32[4,512]{1,0:T(4,128)S(1)}, u32[]{:S(2)}, u32[]{:S(2)}) collective-permute-start(f32[4,512]{1,0:T(4,128)S(1)} %add.15.g_ref), channel_id=1, source_target_pairs={{0,16},{4,20},{8,24},{12,28},{16,0},{20,4},{24,8},{28,12},{1,17},{... | collective-permute-start | bytes 24584 | tf_op jit(solution)/shard_map/ppermute | solution.py:493
  25.5 0.0 collective-permute-done.4.refs_1_
  25.5 0.7 %boundary_columns.2.near_ref = f32[128,1024]{1,0:T(8,128)S(1)} custom-call(bf16[1024,1024]{1,0:T(8,128)(2,1)S(1)} %get-tuple-element.21.pick, f32[64,1024]{1,0:T(8,128)S(1)} %collective-permute-done.3.refs_0_, f32[64,1024]{1,0:T(8,128)S(1)} %collective-permute-done.4.refs_1_), custom_call_target="tpu_custom_call" | custom-call | flops 536870912 | bytes 1 | tf_op jit(solution)/shard_map/boundary_columns/pallas_call | solution.py:278
  26.3 0.0 collective-permute-done.6.refs_1_
  26.3 0.7 %boundary_columns.3.far_edge_ref = f32[128,1024]{1,0:T(8,128)S(1)} custom-call(bf16[1024,1024]{1,0:T(8,128)(2,1)S(1)} %get-tuple-element.21.pick, f32[64,1024]{1,0:T(8,128)S(1)} %collective-permute-done.5.refs_0_, f32[64,1024]{1,0:T(8,128)S(1)} %collective-permute-done.6.refs_1_), custom_call_target="tpu_custom_call" | custom-call | flops 1 | bytes 1 | tf_op jit(solution)/shard_map/boundary_columns/pallas_call | solution.py:278
  27.1 0.4 %collective-permute-done.2.far_ref = f32[4,512]{1,0:T(4,128)S(1)} collective-permute-done((f32[4,512]{1,0:T(4,128)S(1)}, f32[4,512]{1,0:T(4,128)S(1)}, u32[]{:S(2)}, u32[]{:S(2)}) %collective-permute-start.2) | collective-permute-done | bytes 8224 | tf_op jit(solution)/shard_map/ppermute | solution.py:493
  27.5 4.2 %screen_branches.1 = (f32[1024,512]{1,0:T(8,128)}, f32[768,512]{1,0:T(8,128)S(1)}, f32[768,512]{1,0:T(8,128)S(1)}, f32[12,128]{1,0:T(8,128)S(1)}) custom-call(f32[4,512]{1,0:T(4,128)S(1)} %add.15.g_ref, f32[4,512]{1,0:T(4,128)S(1)} %collective-permute-done.2.far_ref, f32[2,512]{1,0:T(2,128)S(1)} %case_rows.1.case_ref, ...), custom_call_target="tpu_custom_call" | custom-call | tf_op jit(solution)/shard_map/screen_branches/pallas_call | solution.py:392
  31.7 0.1 collective-permute-start.9
  31.8 0.8 %collective-permute-start.8 = (f32[12,128]{1,0:T(8,128)S(1)}, f32[12,128]{1,0:T(8,128)S(1)}, u32[]{:S(2)}, u32[]{:S(2)}) collective-permute-start(f32[12,128]{1,0:T(8,128)S(1)} %get-tuple-element.36), channel_id=1, source_target_pairs={{0,2},{1,3},{2,0},{3,1},{4,6},{5,7},{6,4},{7,5},{8,10},{9,11},{10,... | collective-permute-start | bytes 18440 | tf_op jit(solution)/shard_map/ppermute | solution.py:527
  32.6 1.0 %collective-permute-start.7 = (f32[12,128]{1,0:T(8,128)S(1)}, f32[12,128]{1,0:T(8,128)S(1)}, u32[]{:S(2)}, u32[]{:S(2)}) collective-permute-start(f32[12,128]{1,0:T(8,128)S(1)} %get-tuple-element.36), channel_id=1, source_target_pairs={{0,3},{1,2},{2,1},{3,0},{4,7},{5,6},{6,5},{7,4},{8,11},{9,10},{10,... | collective-permute-start | bytes 18440 | tf_op jit(solution)/shard_map/ppermute | solution.py:527
  33.6 0.0 copy-start.5
  33.6 0.0 copy-start.6
  33.6 1.7 %relay_rates.1 = f32[1536,512]{1,0:T(8,128)} custom-call(f32[768,512]{1,0:T(8,128)S(1)} %get-tuple-element.34.square_ref, f32[768,512]{1,0:T(8,128)S(1)} %get-tuple-element.35.rate_ref, f32[1536,8]{1,0:T(8,128)S(1)} %get-tuple-element.25.par_ref), custom_call_target="tpu_custom_call" | custom-call | flops 3145728 | bytes 3145728 | tf_op jit(solution)/shard_map/relay_rates/pallas_call | solution.py:435
  35.3 0.0 collective-permute-done.9
  35.3 0.1 collective-permute-done.8
  35.5 0.2 collective-permute-done.7
  35.7 0.0 copy-done.5
  35.7 0.0 copy-done.6
  35.7 0.6 %fusion.4 = f32[1536]{0:T(1024)} fusion(f32[1536]{0:T(1024)S(1)} %copy-done.5, f32[12,128]{1,0:T(8,128)S(1)} %collective-permute-done.9, f32[12,128]{1,0:T(8,128)S(1)} %collective-permute-done.8, f32[12,128]{1,0:T(8,128)S(1)} %get-tuple-element.36, f32[12,128]{1,0:T(8,128)S(1)} %collective-permute-done.7, s32[1536]{0:T(1024)S(1)} %copy-done.6), kind=kLoop, calls=%fused_computation.5 | loop fusion | flops 27648 | bytes 43008 | tf_op jit(solution)/shard_map/mul | solution.py:291
  (3 shorter events, 0.0 us)
Async XLA Ops:
  0.6 6.5 %copy-start = (s32[512,2]{0,1:T(2,128)S(1)}, s32[512,2]{0,1:T(2,128)}, u32[]{:S(2)}) copy-start(s32[512,2]{0,1:T(2,128)} %param.15) | copy-start | bytes 12292
  0.6 6.5 %copy-start.1 = (s32[512]{0:T(512)S(1)}, s32[512]{0:T(512)}, u32[]{:S(2)}) copy-start(s32[512]{0:T(512)} %param.14) | copy-start | bytes 6148
  0.7 6.5 %copy-start.2 = (s32[1024]{0:T(1024)S(1)}, s32[1024]{0:T(1024)}, u32[]{:S(2)}) copy-start(s32[1024]{0:T(1024)} %param.13) | copy-start | bytes 12292
  2.3 13.1 %collective-permute-start.3 = (f32[64,1024]{1,0:T(8,128)S(1)}, f32[64,1024]{1,0:T(8,128)S(1)}, u32[]{:S(2)}, u32[]{:S(2)}) collective-permute-start(f32[64,1024]{1,0:T(8,128)S(1)} %get-tuple-element.29), channel_id=1, source_target_pairs={{0,4},{1,5},{4,8},{5,9},{6,2},{7,3},{8,12},{9,13},{10,6},{11,7},{1... | collective-permute-start | bytes 786440 | tf_op jit(solution)/shard_map/ppermute | solution.py:476
  13.8 3.7 %collective-permute-start = (f32[4,512]{1,0:T(4,128)S(1)}, f32[4,512]{1,0:T(4,128)S(1)}, u32[]{:S(2)}, u32[]{:S(2)}) collective-permute-start(f32[4,512]{1,0:T(4,128)S(1)} %get-tuple-element.22), channel_id=1, source_target_pairs={{0,4},{4,0},{8,12},{12,8},{16,20},{20,16},{24,28},{28,24},{1,5},{5... | collective-permute-start | bytes 24584 | tf_op jit(solution)/shard_map/ppermute | solution.py:493
  15.4 7.5 %collective-permute-start.5 = (f32[64,1024]{1,0:T(8,128)S(1)}, f32[64,1024]{1,0:T(8,128)S(1)}, u32[]{:S(2)}, u32[]{:S(2)}) collective-permute-start(f32[64,1024]{1,0:T(8,128)S(1)} %collective-permute-done.3.refs_0_), channel_id=1, source_target_pairs={{0,2},{1,3},{2,0},{3,1},{4,6},{5,7},{6,4},{7,5},{8,10},{9,11},{10,... | collective-permute-start | bytes 786440 | tf_op jit(solution)/shard_map/ppermute | solution.py:499
  17.5 5.4 %copy-start.3 = (f32[512]{0:T(512)S(1)}, f32[512]{0:T(512)}, u32[]{:S(2)}) copy-start(f32[512]{0:T(512)} %param.16) | copy-start | bytes 6148
  17.5 5.4 %copy-start.4 = (f32[512]{0:T(512)S(1)}, f32[512]{0:T(512)}, u32[]{:S(2)}) copy-start(f32[512]{0:T(512)} %param.17) | copy-start | bytes 6148
  17.5 4.1 %collective-permute-start.1 = (f32[4,512]{1,0:T(4,128)S(1)}, f32[4,512]{1,0:T(4,128)S(1)}, u32[]{:S(2)}, u32[]{:S(2)}) collective-permute-start(f32[4,512]{1,0:T(4,128)S(1)} %add.14), channel_id=1, source_target_pairs={{0,8},{4,12},{8,0},{12,4},{16,24},{20,28},{24,16},{28,20},{1,9},{5... | collective-permute-start | bytes 24584 | tf_op jit(solution)/shard_map/ppermute | solution.py:493
  21.6 3.9 %collective-permute-start.4 = (f32[64,1024]{1,0:T(8,128)S(1)}, f32[64,1024]{1,0:T(8,128)S(1)}, u32[]{:S(2)}, u32[]{:S(2)}) collective-permute-start(f32[64,1024]{1,0:T(8,128)S(1)} %collective-permute-done.3.refs_0_), channel_id=1, source_target_pairs={{0,1},{1,0},{2,3},{3,2},{4,5},{5,4},{6,7},{7,6},{8,9},{9,8},{10,11... | collective-permute-start | bytes 786440 | tf_op jit(solution)/shard_map/ppermute | solution.py:519
  22.9 3.4 %collective-permute-start.6 = (f32[64,1024]{1,0:T(8,128)S(1)}, f32[64,1024]{1,0:T(8,128)S(1)}, u32[]{:S(2)}, u32[]{:S(2)}) collective-permute-start(f32[64,1024]{1,0:T(8,128)S(1)} %collective-permute-done.5.refs_0_), channel_id=1, source_target_pairs={{0,1},{1,0},{2,3},{3,2},{4,5},{5,4},{6,7},{7,6},{8,9},{9,8},{10,11... | collective-permute-start | bytes 786440 | tf_op jit(solution)/shard_map/ppermute | solution.py:519
  22.9 4.6 %collective-permute-start.2 = (f32[4,512]{1,0:T(4,128)S(1)}, f32[4,512]{1,0:T(4,128)S(1)}, u32[]{:S(2)}, u32[]{:S(2)}) collective-permute-start(f32[4,512]{1,0:T(4,128)S(1)} %add.15.g_ref), channel_id=1, source_target_pairs={{0,16},{4,20},{8,24},{12,28},{16,0},{20,4},{24,8},{28,12},{1,17},{... | collective-permute-start | bytes 24584 | tf_op jit(solution)/shard_map/ppermute | solution.py:493
  31.7 3.6 %collective-permute-start.9 = (f32[12,128]{1,0:T(8,128)S(1)}, f32[12,128]{1,0:T(8,128)S(1)}, u32[]{:S(2)}, u32[]{:S(2)}) collective-permute-start(f32[12,128]{1,0:T(8,128)S(1)} %get-tuple-element.36), channel_id=1, source_target_pairs={{0,1},{1,0},{2,3},{3,2},{4,5},{5,4},{6,7},{7,6},{8,9},{9,8},{10,11... | collective-permute-start | bytes 18440 | tf_op jit(solution)/shard_map/ppermute | solution.py:527
  31.8 3.7 %collective-permute-start.8 = (f32[12,128]{1,0:T(8,128)S(1)}, f32[12,128]{1,0:T(8,128)S(1)}, u32[]{:S(2)}, u32[]{:S(2)}) collective-permute-start(f32[12,128]{1,0:T(8,128)S(1)} %get-tuple-element.36), channel_id=1, source_target_pairs={{0,2},{1,3},{2,0},{3,1},{4,6},{5,7},{6,4},{7,5},{8,10},{9,11},{10,... | collective-permute-start | bytes 18440 | tf_op jit(solution)/shard_map/ppermute | solution.py:527
  32.6 3.1 %collective-permute-start.7 = (f32[12,128]{1,0:T(8,128)S(1)}, f32[12,128]{1,0:T(8,128)S(1)}, u32[]{:S(2)}, u32[]{:S(2)}) collective-permute-start(f32[12,128]{1,0:T(8,128)S(1)} %get-tuple-element.36), channel_id=1, source_target_pairs={{0,3},{1,2},{2,1},{3,0},{4,7},{5,6},{6,5},{7,4},{8,11},{9,10},{10,... | collective-permute-start | bytes 18440 | tf_op jit(solution)/shard_map/ppermute | solution.py:527
  33.6 2.0 %copy-start.5 = (f32[1536]{0:T(1024)S(1)}, f32[1536]{0:T(1024)}, u32[]{:S(2)}) copy-start(f32[1536]{0:T(1024)} %param.22) | copy-start | bytes 18436
  33.6 2.0 %copy-start.6 = (s32[1536]{0:T(1024)S(1)}, s32[1536]{0:T(1024)}, u32[]{:S(2)}) copy-start(s32[1536]{0:T(1024)} %param.23) | copy-start | bytes 18436
